TPU v7x, 32 devices: a whole 2x2x4 slice. The times are simulated.
32 devices in a mesh: slab: 8 (over z, x), tile: 4 (over y, core).
Axes of the slice: x: 2, y: 2, z: 4, core: 2. Of those that a mesh axis runs over, the one named last changes fastest.
Arguments:
- solution: float32 [128, 128, 256], P('tile', 'slab'), may hold values from -6 to 6
- source: float32 [128, 128, 256], P('tile', 'slab'), may hold values from 0 to 2
- phase_label: int32 [128, 128, 256], P('tile', 'slab'), may hold values from 0 to 2
- phase_diffusivity: float32 [3], replicated, may hold values from 0.1 to 2
- phase_uptake: float32 [3], replicated, may hold values from 0.2 to 1
- send_tiles: int32 [8, 4, 8, 8], P('slab', 'tile'), may hold values from 0 to 31
- support_slot: int32 [8, 4, 64], P('slab', 'tile'), may hold values from 0 to 63, each once within a row
- support_len: int32 [8, 4, 8], P('slab', 'tile'), may hold values from 1 to 8, 40 in all within a row
- coarse_ids: int32 [256], P(('slab', 'tile')), may hold values from 0 to 255, each once
- basis_values: bfloat16 [256, 8, 4096], P(('slab', 'tile')), may hold values from 0 to 0.25
- coarse_diag: float32 [256], P(('slab', 'tile')), may hold values from 320 to 480
- coarse_off: float32 [256, 26], P(('slab', 'tile')), may hold values from -12 to -4
- coarse_cols: int32 [256, 26], P(('slab', 'tile')), may hold values from 0 to 255
Outputs:
- new_solution: float32 [128, 128, 256], P('tile', 'slab')
- coarse_correction: float32 [256], P(('slab', 'tile'))
Inputs may be any that keep to these rules, and one draw needn't show every extreme that they name: `support_slot`: on each device the 64 entries are the numbers 0 to 63, each once. `support_len`: on each device the lengths sum to 40, and some cell has 8. `coarse_ids`: every coarse cell appears once.
All inputs are finite; a program needn't handle non-finite values.
Results may differ from a plain program's by a relative error of at most 0.00062.
Values may be sent and summed in bfloat16 or wider, within the bound.
No kernel may reach another device: no remote copies, remote signals or barrier semaphores. Data moves between devices by JAX's collectives and lax.ppermute only.
A program may use at most 64 MiB of HBM per device.

v0:
```python
import jax
import jax.numpy as jnp
from jax import lax
from jax.sharding import PartitionSpec as P

COARSE_SWEEPS = 4
SMOOTH_SWEEPS = 2


OMEGA = 0.8


def with_halo(block, sides, width):
    for axis, dim in sides:
        count = lax.axis_size(axis)
        forward = [(i, i + 1) for i in range(count - 1)]
        backward = [(target, source) for source, target in forward]
        low = lax.ppermute(
            lax.slice_in_dim(block, block.shape[dim] - width, None, axis=dim), axis, forward
        )
        high = lax.ppermute(lax.slice_in_dim(block, 0, width, axis=dim), axis, backward)
        block = jnp.concatenate([low, block, high], axis=dim)
    return block


def lookup(phase_label, table):
    result = jnp.zeros(phase_label.shape, jnp.float32)
    for category in range(table.shape[0]):
        result = result + jnp.where(phase_label == category, table[category], 0.0)
    return result


def widen(values):
    return jnp.pad(values, ((0, 0), (0, 0), (1, 1)))


def neighbours(padded):
    return (
        padded[2:, 1:-1, 1:-1],
        padded[:-2, 1:-1, 1:-1],
        padded[1:-1, 2:, 1:-1],
        padded[1:-1, :-2, 1:-1],
        padded[1:-1, 1:-1, 2:],
        padded[1:-1, 1:-1, :-2],
    )


def face_weights(center, padded):
    return tuple((0.5 * (center + other) for other in neighbours(padded)))


def operate(values, weights, diagonal):
    padded = widen(with_halo(values, (("slab", 1), ("tile", 0)), 1))
    beside_all = neighbours(padded)
    coupled = weights[0] * beside_all[0]
    for number in range(1, 6):
        coupled = coupled + weights[number] * beside_all[number]
    return diagonal * values - coupled


def shards(
    solution,
    source,
    phase_label,
    phase_diffusivity,
    phase_uptake,
    send_tiles,
    support_slot,
    support_len,
    coarse_ids,
    basis_values,
    coarse_diag,
    coarse_off,
    coarse_cols,
):
    conduct = lookup(phase_label, phase_diffusivity)
    uptake = lookup(phase_label, phase_uptake)
    padded = widen(with_halo(conduct, (("slab", 1), ("tile", 0)), 1))
    weights = face_weights(conduct, padded)
    diagonal = uptake + weights[0] + weights[1] + weights[2] + weights[3] + weights[4] + weights[5]
    residual = source - operate(solution, weights, diagonal)
    rows, depth, width = solution.shape
    voxels = depth * width
    tile_stack = residual.astype(jnp.bfloat16).reshape(rows, voxels)
    slab_count = lax.axis_size("slab")
    capacity = send_tiles.shape[3]
    slot_total = slab_count * capacity
    send_list = send_tiles.reshape(slot_total)
    cell_count = basis_values.shape[0]
    support_count = basis_values.shape[1]
    slot_list = support_slot.reshape(cell_count * support_count)
    live_mask = jnp.arange(support_count)[None, :] < support_len.reshape(cell_count)[:, None]
    selector = (send_list[None, :] == jnp.arange(rows)[:, None]).astype(jnp.bfloat16)
    outgoing = tile_stack[send_list].reshape(slab_count, capacity, voxels)
    incoming = lax.all_to_all(outgoing, "slab", split_axis=0, concat_axis=0, tiled=True).reshape(
        slot_total, voxels
    )
    pieces = incoming[slot_list].reshape(cell_count, support_count, voxels)
    products = jnp.einsum("csv,csv->cs", pieces, basis_values, preferred_element_type=jnp.float32)
    restricted = jnp.sum(jnp.where(live_mask, products, 0.0), axis=1)
    device_count = slab_count * lax.axis_size("tile")
    spread = jnp.zeros((cell_count * device_count,), jnp.float32).at[coarse_ids].set(restricted)
    coarse_rhs = lax.psum_scatter(spread, ("slab", "tile"), scatter_dimension=0, tiled=True)
    coarse_state = coarse_rhs / coarse_diag
    for repeat in range(COARSE_SWEEPS - 1):
        gathered = lax.all_gather(coarse_state, ("slab", "tile"), axis=0, tiled=True)
        coarse_state = (
            coarse_rhs - jnp.sum(coarse_off * gathered[coarse_cols], axis=1)
        ) / coarse_diag
    gathered = lax.all_gather(coarse_state, ("slab", "tile"), axis=0, tiled=True)
    coarse_correction = gathered[coarse_ids]
    contributions = jnp.where(
        live_mask[:, :, None], coarse_correction[:, None, None] * basis_values, 0.0
    ).astype(jnp.bfloat16)
    returning = (
        jnp.zeros((slot_total, voxels), jnp.bfloat16)
        .at[slot_list]
        .set(contributions.reshape(cell_count * support_count, voxels))
    )
    delivered = lax.all_to_all(
        returning.reshape(slab_count, capacity, voxels),
        "slab",
        split_axis=0,
        concat_axis=0,
        tiled=True,
    ).reshape(slot_total, voxels)
    prolonged = jnp.dot(selector, delivered, preferred_element_type=jnp.float32).reshape(
        rows, depth, width
    )
    corrected = solution + prolonged
    for repeat in range(SMOOTH_SWEEPS):
        corrected = corrected + OMEGA * (source - operate(corrected, weights, diagonal)) / diagonal
    return (corrected, coarse_correction)


def solution(mesh):
    placed = (
        P("tile", "slab", None),
        P("tile", "slab", None),
        P("tile", "slab", None),
        P(),
        P(),
        P("slab", "tile", None, None),
        P("slab", "tile", None),
        P("slab", "tile", None),
        P(("slab", "tile")),
        P(("slab", "tile"), None, None),
        P(("slab", "tile")),
        P(("slab", "tile"), None),
        P(("slab", "tile"), None),
    )
    return jax.shard_map(
        shards,
        mesh=mesh,
        in_specs=placed,
        out_specs=(P("tile", "slab", None), P(("slab", "tile"))),
        check_vma=False,
    )
```

profile of v0, /device:TPU:0, one launch (start us, length us, event | category | flops | bytes accessed | tf_op | source)
XLA Modules:
  0.0 337.2 jit_solution(1559686419506612282)
XLA Ops:
  0.6 1.4 fusion.77
  2.1 4.2 %select_add_fusion = (f32[32,16,256]{2,0,1:T(8,128)S(1)}, pred[32,16,256]{2,0,1:T(8,128)(4,1)S(1)}, pred[32,16,256]{2,0,1:T(8,128)(4,1)S(1)}, pred[32,16,256]{2,0,1:T(8,128)(4,1)}) fusion(f32[]{:T(128)} %bitcast.9, f32[]{:T(128)} %bitcast.8, f32[]{:T(128)} %bitcast.7, s32[32,16,256]{2,1,0:T(8,128)} %param.15), kind=kLoop, calls=%fused_computation.124 | loop fusion | flops 1048576 | bytes 1441804 | tf_op jit(solution)/shard_map/add | solution.py:29
  6.3 4.8 %collective-permute-start = (f32[32,1,256]{2,0,1:T(8,128)S(1)}, f32[32,1,256]{2,0,1:T(8,128)S(1)}, u32[]{:S(2)}, u32[]{:S(2)}) collective-permute-start(f32[32,1,256]{2,0,1:T(8,128)S(1)} %get-tuple-element.26), channel_id=1, source_target_pairs={{0,4},{4,8},{8,12},{12,16},{16,20},{20,24},{24,28},{1,5},{5,9},{9,... | collective-permute-start | bytes 98312 | tf_op jit(solution)/shard_map/ppermute | solution.py:18
  12.7 4.5 %collective-permute-start.4 = (f32[32,1,256]{2,0,1:T(8,128)S(1)}, f32[32,1,256]{2,0,1:T(8,128)S(1)}, u32[]{:S(2)}, u32[]{:S(2)}) collective-permute-start(f32[32,1,256]{2,0,1:T(8,128)S(1)} %get-tuple-element.29), channel_id=1, source_target_pairs={{0,4},{4,8},{8,12},{12,16},{16,20},{20,24},{24,28},{1,5},{5,9},{9,... | collective-permute-start | bytes 98312 | tf_op jit(solution)/shard_map/ppermute | solution.py:18
  21.9 3.0 collective-permute-start.3
  26.6 3.7 %collective-permute-start.7 = (f32[1,18,256]{2,0,1:T(1,128)S(1)}, f32[1,18,256]{2,0,1:T(1,128)S(1)}, u32[]{:S(2)}, u32[]{:S(2)}) collective-permute-start(f32[1,18,256]{2,0,1:T(1,128)S(1)} %get-tuple-element.20), channel_id=1, source_target_pairs={{0,1},{1,2},{2,3},{4,5},{5,6},{6,7},{8,9},{9,10},{10,11},{12,13},{... | collective-permute-start | bytes 55304 | tf_op jit(solution)/shard_map/ppermute | solution.py:18
  32.0 3.4 %fusion.63 = bf16[16,4,8,256]{3,2,1,0:T(8,128)(2,1)S(1)} fusion(f32[34,18,258]{2,0,1:T(8,128)S(1)} %select_maximum_fusion.8, f32[32,16,256]{2,0,1:T(8,128)S(1)} %copy.57, f32[32,1,256]{2,0,1:T(8,128)S(1)} %copy-done.8, f32[32,1,256]{2,0,1:T(8,128)S(1)} %copy-done.10, f32[32,18,256]{2,0,1:T(8,128)S(1)} %constant_dynamic-update-slice_fusion, ...), kind=kLoop, calls=%fused_computation.131 | loop fusion | flops 6553600 | bytes 5120012
  35.4 1.8 gather_fusion
  37.2 7.8 %all-to-all-start = ((bf16[8,8,4096]{2,1,0:T(8,128)(2,1)}), bf16[8,8,4096]{2,1,0:T(8,128)(2,1)S(1)}, u32[]{:S(2)}, u32[]{:S(2)}) async-start(bf16[8,8,4096]{2,1,0:T(8,128)(2,1)} %bitcast.40), calls=%async_computation | async-start | bytes 1048576 | tf_op jit(solution)/shard_map/all_to_all | solution.py:95
  50.1 10.5 %all-to-all-done = bf16[8,8,4096]{2,1,0:T(8,128)(2,1)S(1)} async-done(((bf16[8,8,4096]{2,1,0:T(8,128)(2,1)}), bf16[8,8,4096]{2,1,0:T(8,128)(2,1)S(1)}, u32[]{:S(2)}, u32[]{:S(2)}) %all-to-all-start) | async-done | bytes 524320 | tf_op jit(solution)/shard_map/all_to_all | solution.py:95
  60.5 1.8 gather_fusion.1
  62.3 1.4 fusion.1
  65.3 37.5 %all-reduce.8 = f32[256]{0:T(256)S(1)} all-reduce(f32[256]{0:T(256)S(1)} %scatter_custom_fusion), channel_id=2, replica_groups=mesh['slab'=8,'tile'=4] {'slab','tile'}, use_global_device_ids=true, to_apply=%region_2.3.clone | all-reduce | flops 256 | bytes 2048
  103.6 41.8 %all-reduce.4 = f32[256]{0:T(256)S(1)} all-reduce(f32[256]{0:T(256)S(1)} %get-tuple-element.8), channel_id=1, replica_groups=mesh['slab'=8,'tile'=4] {'slab','tile'}, use_global_device_ids=true, to_apply=%add.4 | all-reduce | flops 256 | bytes 2048
  145.4 1.9 gather_fusion.2
  147.6 38.7 %all-reduce.5 = f32[256]{0:T(256)S(1)} all-reduce(f32[256]{0:T(256)S(1)} %divide_dynamic-update-slice_fusion.2), channel_id=1, replica_groups=mesh['slab'=8,'tile'=4] {'slab','tile'}, use_global_device_ids=true, to_apply=%add.5 | all-reduce | flops 256 | bytes 2048
  186.3 1.9 gather_fusion.3
  188.6 41.2 %all-reduce.6 = f32[256]{0:T(256)S(1)} all-reduce(f32[256]{0:T(256)S(1)} %divide_dynamic-update-slice_fusion.1), channel_id=1, replica_groups=mesh['slab'=8,'tile'=4] {'slab','tile'}, use_global_device_ids=true, to_apply=%add.6 | all-reduce | flops 256 | bytes 2048
  229.8 2.8 gather_fusion.4
  236.1 39.1 %all-reduce.7 = f32[256]{0:T(256)S(1)} all-reduce(f32[256]{0:T(256)} %divide_dynamic-update-slice_fusion), channel_id=1, replica_groups=mesh['slab'=8,'tile'=4] {'slab','tile'}, use_global_device_ids=true, to_apply=%add.7 | all-reduce | flops 256 | bytes 2048
  276.5 2.5 scatter_custom_fusion.1
  279.0 5.2 %all-to-all-start.1 = ((bf16[8,8,4096]{2,1,0:T(8,128)(2,1)}), bf16[8,8,4096]{2,1,0:T(8,128)(2,1)S(1)}, u32[]{:S(2)}, u32[]{:S(2)}) async-start(bf16[8,8,4096]{2,1,0:T(8,128)(2,1)} %bitcast.42), calls=%async_computation.1 | async-start | bytes 1048576 | tf_op jit(solution)/shard_map/all_to_all | solution.py:120
  284.8 13.2 %all-to-all-done.1 = bf16[8,8,4096]{2,1,0:T(8,128)(2,1)S(1)} async-done(((bf16[8,8,4096]{2,1,0:T(8,128)(2,1)}), bf16[8,8,4096]{2,1,0:T(8,128)(2,1)S(1)}, u32[]{:S(2)}, u32[]{:S(2)}) %all-to-all-start.1) | async-done | bytes 524320 | tf_op jit(solution)/shard_map/all_to_all | solution.py:120
  299.1 3.3 collective-permute-start.8
  302.4 1.4 collective-permute-start.9
  304.0 4.4 %collective-permute-done.9 = f32[32,1,256]{2,0,1:T(8,128)S(1)} collective-permute-done((f32[32,1,256]{2,0,1:T(8,128)S(1)}, f32[32,1,256]{2,0,1:T(8,128)S(1)}, u32[]{:S(2)}, u32[]{:S(2)}) %collective-permute-start.9) | collective-permute-done | bytes 32800 | tf_op jit(solution)/shard_map/ppermute | solution.py:21
  309.7 3.0 collective-permute-start.11
  314.1 3.4 %fusion.28 = f32[32,16,256]{2,0,1:T(8,128)S(1)} fusion(f32[32,16,256]{2,0,1:T(8,128)S(1)} %convolution_add_fusion, f32[34,18,258]{2,0,1:T(8,128)S(1)} %select_maximum_fusion.4, f32[32,1,256]{2,0,1:T(8,128)S(1)} %collective-permute-done.8, f32[32,1,256]{2,0,1:T(8,128)S(1)} %collective-permute-done.9, f32[1,18,256]{2,0,1:T(1,128)S(1)} %collective-permute-done.11, ...), kind=kLoop, calls=%fused_computation.65 | loop fusion | flops 7340032 | bytes 4792332 | tf_op jit(solution)/shard_map/add | solution.py:132
  317.6 3.6 %collective-permute-start.12 = (f32[32,1,256]{2,0,1:T(8,128)S(1)}, f32[32,1,256]{2,0,1:T(8,128)S(1)}, u32[]{:S(2)}, u32[]{:S(2)}) collective-permute-start(f32[32,1,256]{2,0,1:T(8,128)S(1)} %get-tuple-element.22), channel_id=1, source_target_pairs={{0,4},{4,8},{8,12},{12,16},{16,20},{20,24},{24,28},{1,5},{5,9},{9,... | collective-permute-start | bytes 98312 | tf_op jit(solution)/shard_map/ppermute | solution.py:18
  322.7 4.2 %collective-permute-done.13 = f32[32,1,256]{2,0,1:T(8,128)S(1)} collective-permute-done((f32[32,1,256]{2,0,1:T(8,128)S(1)}, f32[32,1,256]{2,0,1:T(8,128)S(1)}, u32[]{:S(2)}, u32[]{:S(2)}) %collective-permute-start.13) | collective-permute-done | bytes 32800 | tf_op jit(solution)/shard_map/ppermute | solution.py:21
  328.3 3.0 collective-permute-start.15
  332.7 3.4 %fusion.14 = f32[32,16,256]{2,0,1:T(8,128)S(1)} fusion(f32[32,16,256]{2,0,1:T(8,128)S(1)} %fusion.28, f32[34,18,258]{2,0,1:T(8,128)S(1)} %select_maximum_fusion, f32[32,1,256]{2,0,1:T(8,128)S(1)} %collective-permute-done.12, f32[32,1,256]{2,0,1:T(8,128)S(1)} %collective-permute-done.13, f32[1,18,256]{2,0,1:T(1,128)S(1)} %collective-permute-done.15, ...), kind=kLoop, calls=%fused_computation.41 | loop fusion | flops 7340032 | bytes 4792332 | tf_op jit(solution)/shard_map/add | solution.py:132
  (112 shorter events, 31.9 us)
Async XLA Ops:
  0.6 11.8 %copy-start = (f32[32,16,256]{2,1,0:T(8,128)S(1)}, f32[32,16,256]{2,1,0:T(8,128)}, u32[]{:S(2)}) copy-start(f32[32,16,256]{2,1,0:T(8,128)} %param.13) | copy-start | bytes 1572868
  2.1 16.5 %copy-start.17 = (f32[3]{0:T(128)S(1)}, f32[3]{0:T(128)}, u32[]{:S(2)}) copy-start(f32[3]{0:T(128)} %param.17) | copy-start | bytes 40
  2.1 17.2 %copy-start.13 = (s32[1,1,8,8]{3,2,1,0:T(8,128)S(1)}, s32[1,1,8,8]{3,2,1,0:T(8,128)}, u32[]{:S(2)}) copy-start(s32[1,1,8,8]{3,2,1,0:T(8,128)} %param.18) | copy-start | bytes 772
  2.1 17.2 %copy-start.18 = (s32[8,26]{1,0:T(8,128)S(1)}, s32[8,26]{1,0:T(8,128)}, u32[]{:S(2)}) copy-start(s32[8,26]{1,0:T(8,128)} %param.25) | copy-start | bytes 2500
  6.3 14.3 %collective-permute-start = (f32[32,1,256]{2,0,1:T(8,128)S(1)}, f32[32,1,256]{2,0,1:T(8,128)S(1)}, u32[]{:S(2)}, u32[]{:S(2)}) collective-permute-start(f32[32,1,256]{2,0,1:T(8,128)S(1)} %get-tuple-element.26), channel_id=1, source_target_pairs={{0,4},{4,8},{8,12},{12,16},{16,20},{20,24},{24,28},{1,5},{5,9},{9,... | collective-permute-start | bytes 98312 | tf_op jit(solution)/shard_map/ppermute | solution.py:18
  11.1 9.5 %collective-permute-start.1 = (f32[32,1,256]{2,0,1:T(8,128)S(1)}, f32[32,1,256]{2,0,1:T(8,128)S(1)}, u32[]{:S(2)}, u32[]{:S(2)}) collective-permute-start(f32[32,1,256]{2,0,1:T(8,128)S(1)} %get-tuple-element.27), channel_id=1, source_target_pairs={{4,0},{8,4},{12,8},{16,12},{20,16},{24,20},{28,24},{5,1},{9,5},{13... | collective-permute-start | bytes 98312 | tf_op jit(solution)/shard_map/ppermute | solution.py:21
  12.7 12.2 %collective-permute-start.4 = (f32[32,1,256]{2,0,1:T(8,128)S(1)}, f32[32,1,256]{2,0,1:T(8,128)S(1)}, u32[]{:S(2)}, u32[]{:S(2)}) collective-permute-start(f32[32,1,256]{2,0,1:T(8,128)S(1)} %get-tuple-element.29), channel_id=1, source_target_pairs={{0,4},{4,8},{8,12},{12,16},{16,20},{20,24},{24,28},{1,5},{5,9},{9,... | collective-permute-start | bytes 98312 | tf_op jit(solution)/shard_map/ppermute | solution.py:18
  17.3 8.0 %collective-permute-start.5 = (f32[32,1,256]{2,0,1:T(8,128)S(1)}, f32[32,1,256]{2,0,1:T(8,128)S(1)}, u32[]{:S(2)}, u32[]{:S(2)}) collective-permute-start(f32[32,1,256]{2,0,1:T(8,128)S(1)} %get-tuple-element.28), channel_id=1, source_target_pairs={{4,0},{8,4},{12,8},{16,12},{20,16},{24,20},{28,24},{5,1},{9,5},{13... | collective-permute-start | bytes 98312 | tf_op jit(solution)/shard_map/ppermute | solution.py:21
  20.6 9.7 %collective-permute-start.2 = (f32[1,18,256]{2,0,1:T(1,128)S(1)}, f32[1,18,256]{2,0,1:T(1,128)S(1)}, u32[]{:S(2)}, u32[]{:S(2)}) collective-permute-start(f32[1,18,256]{2,0,1:T(1,128)S(1)} %get-tuple-element.19), channel_id=1, source_target_pairs={{1,0},{2,1},{3,2},{5,4},{6,5},{7,6},{9,8},{10,9},{11,10},{13,12},{... | collective-permute-start | bytes 55304 | tf_op jit(solution)/shard_map/ppermute | solution.py:21
  21.9 8.5 %collective-permute-start.3 = (f32[1,18,256]{2,0,1:T(1,128)S(1)}, f32[1,18,256]{2,0,1:T(1,128)S(1)}, u32[]{:S(2)}, u32[]{:S(2)}) collective-permute-start(f32[1,18,256]{2,0,1:T(1,128)S(1)} %get-tuple-element.18), channel_id=1, source_target_pairs={{0,1},{1,2},{2,3},{4,5},{5,6},{6,7},{8,9},{9,10},{10,11},{12,13},{... | collective-permute-start | bytes 55304 | tf_op jit(solution)/shard_map/ppermute | solution.py:18
  24.9 5.4 %copy-start.7 = (f32[32,1,256]{2,0,1:T(8,128)}, f32[32,1,256]{2,0,1:T(8,128)S(1)}, u32[]{:S(2)}) copy-start(f32[32,1,256]{2,0,1:T(8,128)S(1)} %collective-permute-done.4) | copy-start | bytes 98308
  25.3 5.1 %copy-start.9 = (f32[32,1,256]{2,0,1:T(8,128)}, f32[32,1,256]{2,0,1:T(8,128)S(1)}, u32[]{:S(2)}) copy-start(f32[32,1,256]{2,0,1:T(8,128)S(1)} %collective-permute-done.5) | copy-start | bytes 98308
  25.3 5.6 %collective-permute-start.6 = (f32[1,18,256]{2,0,1:T(1,128)S(1)}, f32[1,18,256]{2,0,1:T(1,128)S(1)}, u32[]{:S(2)}, u32[]{:S(2)}) collective-permute-start(f32[1,18,256]{2,0,1:T(1,128)S(1)} %get-tuple-element.21), channel_id=1, source_target_pairs={{1,0},{2,1},{3,2},{5,4},{6,5},{7,6},{9,8},{10,9},{11,10},{13,12},{... | collective-permute-start | bytes 55304 | tf_op jit(solution)/shard_map/ppermute | solution.py:21
  26.6 4.5 %collective-permute-start.7 = (f32[1,18,256]{2,0,1:T(1,128)S(1)}, f32[1,18,256]{2,0,1:T(1,128)S(1)}, u32[]{:S(2)}, u32[]{:S(2)}) collective-permute-start(f32[1,18,256]{2,0,1:T(1,128)S(1)} %get-tuple-element.20), channel_id=1, source_target_pairs={{0,1},{1,2},{2,3},{4,5},{5,6},{6,7},{8,9},{9,10},{10,11},{12,13},{... | collective-permute-start | bytes 55304 | tf_op jit(solution)/shard_map/ppermute | solution.py:18
  37.2 23.3 %all-to-all-start = ((bf16[8,8,4096]{2,1,0:T(8,128)(2,1)}), bf16[8,8,4096]{2,1,0:T(8,128)(2,1)S(1)}, u32[]{:S(2)}, u32[]{:S(2)}) async-start(bf16[8,8,4096]{2,1,0:T(8,128)(2,1)} %bitcast.40), calls=%async_computation | async-start | bytes 1048576 | tf_op jit(solution)/shard_map/all_to_all | solution.py:95
  47.5 138.8 %copy-start.11 = (s32[1024]{0:T(1024)}, s32[1024]{0:T(1024)S(1)}, u32[]{:S(2)}) copy-start(s32[1024]{0:T(1024)S(1)} %pad_clamp_fusion.1) | copy-start | bytes 12292
  103.6 84.9 %copy-start.16 = (f32[8]{0:T(128)}, f32[8]{0:T(128)S(1)}, u32[]{:S(2)}) copy-start(f32[8]{0:T(128)S(1)} %get-tuple-element.9) | copy-start | bytes 100
  145.4 2.0 copy-start.12
  145.4 2.2 copy-start.15
  229.8 46.6 %copy-start.4 = (bf16[8,8,4096]{2,1,0:T(8,128)(2,1)S(1)}, bf16[8,8,4096]{2,1,0:T(8,128)(2,1)}, u32[]{:S(2)}) copy-start(bf16[8,8,4096]{2,1,0:T(8,128)(2,1)} %param.22) | copy-start | bytes 1572868
  276.5 7.6 %copy-start.14 = (s32[1,1,8,8]{3,2,1,0:T(8,128)S(1)}, s32[1,1,8,8]{3,2,1,0:T(8,128)}, u32[]{:S(2)}) copy-start(s32[1,1,8,8]{3,2,1,0:T(8,128)} %param.18) | copy-start | bytes 772
  279.0 19.1 %all-to-all-start.1 = ((bf16[8,8,4096]{2,1,0:T(8,128)(2,1)}), bf16[8,8,4096]{2,1,0:T(8,128)(2,1)S(1)}, u32[]{:S(2)}, u32[]{:S(2)}) async-start(bf16[8,8,4096]{2,1,0:T(8,128)(2,1)} %bitcast.42), calls=%async_computation.1 | async-start | bytes 1048576 | tf_op jit(solution)/shard_map/all_to_all | solution.py:120
  299.1 4.9 %collective-permute-start.8 = (f32[32,1,256]{2,0,1:T(8,128)S(1)}, f32[32,1,256]{2,0,1:T(8,128)S(1)}, u32[]{:S(2)}, u32[]{:S(2)}) collective-permute-start(f32[32,1,256]{2,0,1:T(8,128)S(1)} %get-tuple-element.24), channel_id=1, source_target_pairs={{0,4},{4,8},{8,12},{12,16},{16,20},{20,24},{24,28},{1,5},{5,9},{9,... | collective-permute-start | bytes 98312 | tf_op jit(solution)/shard_map/ppermute | solution.py:18
  302.4 11.7 %copy-start.3 = (pred[32,16,256]{2,0,1:T(8,128)(4,1)S(1)}, pred[32,16,256]{2,0,1:T(8,128)(4,1)}, u32[]{:S(2)}) copy-start(pred[32,16,256]{2,0,1:T(8,128)(4,1)} %get-tuple-element.13) | copy-start | bytes 393220
  302.4 11.7 %copy-start.6 = (f32[1,18,256]{2,0,1:T(1,128)S(1)}, f32[1,18,256]{2,0,1:T(1,128)}, u32[]{:S(2)}) copy-start(f32[1,18,256]{2,0,1:T(1,128)} %copy-done.5) | copy-start | bytes 55300
  302.4 5.9 %collective-permute-start.9 = (f32[32,1,256]{2,0,1:T(8,128)S(1)}, f32[32,1,256]{2,0,1:T(8,128)S(1)}, u32[]{:S(2)}, u32[]{:S(2)}) collective-permute-start(f32[32,1,256]{2,0,1:T(8,128)S(1)} %get-tuple-element.25), channel_id=1, source_target_pairs={{4,0},{8,4},{12,8},{16,12},{20,16},{24,20},{28,24},{5,1},{9,5},{13... | collective-permute-start | bytes 98312 | tf_op jit(solution)/shard_map/ppermute | solution.py:21
  308.4 4.3 %collective-permute-start.10 = (f32[1,18,256]{2,0,1:T(1,128)S(1)}, f32[1,18,256]{2,0,1:T(1,128)S(1)}, u32[]{:S(2)}, u32[]{:S(2)}) collective-permute-start(f32[1,18,256]{2,0,1:T(1,128)S(1)} %get-tuple-element.17), channel_id=1, source_target_pairs={{1,0},{2,1},{3,2},{5,4},{6,5},{7,6},{9,8},{10,9},{11,10},{13,12},{... | collective-permute-start | bytes 55304 | tf_op jit(solution)/shard_map/ppermute | solution.py:21
  309.7 3.9 %collective-permute-start.11 = (f32[1,18,256]{2,0,1:T(1,128)S(1)}, f32[1,18,256]{2,0,1:T(1,128)S(1)}, u32[]{:S(2)}, u32[]{:S(2)}) collective-permute-start(f32[1,18,256]{2,0,1:T(1,128)S(1)} %get-tuple-element.16), channel_id=1, source_target_pairs={{0,1},{1,2},{2,3},{4,5},{5,6},{6,7},{8,9},{9,10},{10,11},{12,13},{... | collective-permute-start | bytes 55304 | tf_op jit(solution)/shard_map/ppermute | solution.py:18
  317.6 5.2 %collective-permute-start.12 = (f32[32,1,256]{2,0,1:T(8,128)S(1)}, f32[32,1,256]{2,0,1:T(8,128)S(1)}, u32[]{:S(2)}, u32[]{:S(2)}) collective-permute-start(f32[32,1,256]{2,0,1:T(8,128)S(1)} %get-tuple-element.22), channel_id=1, source_target_pairs={{0,4},{4,8},{8,12},{12,16},{16,20},{20,24},{24,28},{1,5},{5,9},{9,... | collective-permute-start | bytes 98312 | tf_op jit(solution)/shard_map/ppermute | solution.py:18
  321.1 5.8 %collective-permute-start.13 = (f32[32,1,256]{2,0,1:T(8,128)S(1)}, f32[32,1,256]{2,0,1:T(8,128)S(1)}, u32[]{:S(2)}, u32[]{:S(2)}) collective-permute-start(f32[32,1,256]{2,0,1:T(8,128)S(1)} %get-tuple-element.23), channel_id=1, source_target_pairs={{4,0},{8,4},{12,8},{16,12},{20,16},{24,20},{28,24},{5,1},{9,5},{13... | collective-permute-start | bytes 98312 | tf_op jit(solution)/shard_map/ppermute | solution.py:21
  327.0 4.3 %collective-permute-start.14 = (f32[1,18,256]{2,0,1:T(1,128)S(1)}, f32[1,18,256]{2,0,1:T(1,128)S(1)}, u32[]{:S(2)}, u32[]{:S(2)}) collective-permute-start(f32[1,18,256]{2,0,1:T(1,128)S(1)} %get-tuple-element.15), channel_id=1, source_target_pairs={{1,0},{2,1},{3,2},{5,4},{6,5},{7,6},{9,8},{10,9},{11,10},{13,12},{... | collective-permute-start | bytes 55304 | tf_op jit(solution)/shard_map/ppermute | solution.py:21
  328.3 3.9 %collective-permute-start.15 = (f32[1,18,256]{2,0,1:T(1,128)S(1)}, f32[1,18,256]{2,0,1:T(1,128)S(1)}, u32[]{:S(2)}, u32[]{:S(2)}) collective-permute-start(f32[1,18,256]{2,0,1:T(1,128)S(1)} %get-tuple-element.14), channel_id=1, source_target_pairs={{0,1},{1,2},{2,3},{4,5},{5,6},{6,7},{8,9},{9,10},{10,11},{12,13},{... | collective-permute-start | bytes 55304 | tf_op jit(solution)/shard_map/ppermute | solution.py:18
  (7 other events, 6.7 us)
where the time goes:
time: 341 us; the launch traced here: 337 us
  blocking collectives  198 us (58%)
  starting transfers between devices  52.5 us (15%)
  waiting for transfers between devices  34.6 us (10%)
  other arithmetic  29.7 us (9%)
  local copies, waits for them, and re-layouts  19.8 us (6%)
    unnamed x5, blocking collectives  198 us
    ppermute x8, starting transfers between devices, with_halo(): lax.ppermute(lax.slice_in_dim(block, block.shape[dim] - width, None, axis...  29 us
    all_to_all x1, waiting for transfers between devices, shards(): lax.all_to_all(returning.reshape(slab_count, capacity, voxels), 'slab', s...  13.2 us
    all_to_all x1, waiting for transfers between devices, shards(): lax.all_to_all(outgoing, 'slab', split_axis=0, concat_axis=0, tiled=True)  10.5 us
    ppermute x8, starting transfers between devices, with_halo(): lax.ppermute(lax.slice_in_dim(block, 0, width, axis=dim), axis, backward)  10.5 us
    ppermute x8, waiting for transfers between devices, with_halo(): lax.ppermute(lax.slice_in_dim(block, 0, width, axis=dim), axis, backward)  8.63 us
    all_to_all x1, starting transfers between devices, shards(): lax.all_to_all(outgoing, 'slab', split_axis=0, concat_axis=0, tiled=True)  7.83 us
    gather x6, local copies, waits for them, and re-layouts, shards(): gathered[coarse_cols]  7.56 us
  transfers between devices with their start and end apart: 18, of which 9 were waited for; matrix products, arithmetic and copies ran while one was open for 2% of the time, Pallas kernels for 0%

commit v1 on v0

v1 whole, which is shorter than its diff:
```python
import functools

import jax
import jax.numpy as jnp
from jax import lax
from jax.experimental import pallas as pl
from jax.experimental.pallas import tpu as pltpu
from jax.sharding import PartitionSpec as P

COARSE_SWEEPS = 4
SMOOTH_SWEEPS = 2
OMEGA = 0.8

VMEM = pl.BlockSpec(memory_space=pltpu.VMEM)
SMEM = pl.BlockSpec(memory_space=pltpu.SMEM)
PARAMS = pltpu.CompilerParams(vmem_limit_bytes=48 * 1024 * 1024)
HALF = 64
DIAG_LANE = 60


def wheel(count, step):
    return [(i, (i + step) % count) for i in range(count)]


def extend(stack, fills):
    fill = jnp.asarray(fills, jnp.float32).reshape(-1, 1, 1, 1)
    slabs, tiles = lax.axis_size("slab"), lax.axis_size("tile")
    slab, tile = lax.axis_index("slab"), lax.axis_index("tile")
    low = lax.ppermute(stack[:, -2:], "slab", wheel(slabs, 1))
    high = lax.ppermute(stack[:, :2], "slab", wheel(slabs, -1))
    low = jnp.where(slab == 0, fill, low)
    high = jnp.where(slab == slabs - 1, fill, high)
    stack = jnp.concatenate([stack, high, low], axis=1)
    low = lax.ppermute(stack[:, :, -2:], "tile", wheel(tiles, 1))
    high = lax.ppermute(stack[:, :, :2], "tile", wheel(tiles, -1))
    low = jnp.where(tile == 0, fill, low)
    high = jnp.where(tile == tiles - 1, fill, high)
    unused = jnp.zeros(high.shape[:2] + (4,) + high.shape[3:], jnp.float32)
    return jnp.concatenate([stack, high, unused, low], axis=2)


def in_plane(plane):
    rows, width = plane.shape
    lane = lax.broadcasted_iota(jnp.int32, plane.shape, 1)
    left = jnp.where(lane == 0, 0.0, pltpu.roll(plane, 1, 1))
    right = jnp.where(lane == width - 1, 0.0, pltpu.roll(plane, width - 1, 1))
    return left + right + pltpu.roll(plane, 1, 0) + pltpu.roll(plane, rows - 1, 0)


def around(z, planes):
    above = jnp.where(z == planes - 1, 0, z + 1)
    below = jnp.where(z == 0, planes - 1, z - 1)
    return above, below


def sort_kernel(slot_ref, len_ref, ids_ref, basis_ref, out_ref):
    entries, voxels = basis_ref.shape
    cells = len_ref.shape[0]
    support = entries // cells
    lane = lax.broadcasted_iota(jnp.int32, (1, entries), 1)
    length = jnp.zeros((1, entries), jnp.int32)
    ident = jnp.zeros((1, entries), jnp.int32)
    for cell in range(cells):
        here = lane // support == cell
        length = jnp.where(here, len_ref[cell], length)
        ident = jnp.where(here, ids_ref[cell], ident)
    live = lane % support < length
    slot = jnp.where(live, slot_ref[...], -1)
    hit = slot == lax.broadcasted_iota(jnp.int32, (entries, entries), 0)
    pick = jnp.where(hit, 1.0, 0.0).astype(jnp.bfloat16)
    step = 512
    for start in range(0, voxels, step):
        out_ref[:, start : start + step] = jnp.dot(
            pick, basis_ref[:, start : start + step], preferred_element_type=jnp.float32
        ).astype(jnp.bfloat16)
    low = jnp.sum(jnp.where(hit, ident % 256, 0).astype(jnp.float32), axis=1, keepdims=True)
    high = jnp.sum(jnp.where(hit, ident // 256, 0).astype(jnp.float32), axis=1, keepdims=True)
    extra = lax.broadcasted_iota(jnp.int32, (entries, out_ref.shape[1] - voxels), 1)
    out_ref[:, voxels:] = jnp.where(extra == 0, low, jnp.where(extra == 1, high, 0.0)).astype(
        jnp.bfloat16
    )


def residual_kernel(diff_ref, upt_ref, ext_ref, res_ref, conduct_ref, scale_ref):
    unused, planes, rows, width = ext_ref.shape
    depth, own, unused = res_ref.shape
    phases = diff_ref.shape[0]

    def fill(z, carry):
        label = ext_ref[1, z]
        conduct = jnp.zeros(label.shape, jnp.float32)
        for phase in range(phases):
            conduct = jnp.where(label == float(phase), diff_ref[phase], conduct)
        conduct_ref[z] = conduct
        return carry

    lax.fori_loop(0, planes, fill, 0)

    def step(z, carry):
        above, below = around(z, planes)
        label, conduct = ext_ref[1, z], conduct_ref[z]
        uptake = jnp.zeros(label.shape, jnp.float32)
        for phase in range(phases):
            uptake = jnp.where(label == float(phase), upt_ref[phase], uptake)
        c_up, c_down = conduct_ref[above], conduct_ref[below]
        diagonal = uptake + 0.5 * (6.0 * conduct + (in_plane(conduct) + c_up + c_down))
        inside = conduct > 0.0
        scale_ref[z] = jnp.where(inside, OMEGA / jnp.where(inside, diagonal, 1.0), 0.0)

        @pl.when(z < depth)
        def _():
            v, v_up, v_down = ext_ref[0, z], ext_ref[0, above], ext_ref[0, below]
            near = in_plane(v) + v_up + v_down
            flow = in_plane(conduct * v) + c_up * v_up + c_down * v_down
            residual = ext_ref[2, z] - (diagonal * v - 0.5 * (conduct * near + flow))
            res_ref[z] = residual[:own].astype(jnp.bfloat16)

        return carry

    lax.fori_loop(0, planes, step, 0)


def owner_of(basis_ref, voxels):
    tail = basis_ref[:, voxels:].astype(jnp.float32)
    return (tail[:, 0:1] + 256.0 * tail[:, 1:2]).astype(jnp.int32)


def restrict_kernel(row_ref, record_ref, res_ref, basis_ref, out_ref):
    depth, own, width = res_ref.shape
    entries = basis_ref.shape[0]
    pick = jnp.where(
        row_ref[...] == lax.broadcasted_iota(jnp.int32, (entries, own), 1), 1.0, 0.0
    ).astype(jnp.bfloat16)
    total = jnp.zeros((entries, width), jnp.float32)
    for z in range(depth):
        piece = jnp.dot(pick, res_ref[z], preferred_element_type=jnp.float32)
        total = total + piece * basis_ref[:, z * width : (z + 1) * width].astype(jnp.float32)
    product = jnp.sum(total, axis=1, keepdims=True)
    ident = owner_of(basis_ref, depth * width)
    copies, lines, lanes = out_ref.shape
    lane = lax.broadcasted_iota(jnp.int32, (entries, lanes), 1)
    line = lax.broadcasted_iota(jnp.int32, (8, lanes), 0)
    for base in range(0, lines, 8):
        block = record_ref[...] if base == 0 else jnp.zeros((8, lanes), jnp.float32)
        for row in range(8):
            share = jnp.where(ident == (base + row) * HALF + lane - HALF, product, 0.0)
            share = jnp.sum(jnp.where(lane >= HALF, share, 0.0), axis=0, keepdims=True)
            block = jnp.where((line == row) & (lane[:8] >= HALF), share, block)

        def put(copy, carry):
            out_ref[copy, base : base + 8, :] = block
            return carry

        lax.fori_loop(0, copies, put, 0, unroll=8)


def solve(got_ref, matrix_ref, count, nnz):
    devices, lines, lanes = got_ref.shape
    column_id = lax.broadcasted_iota(jnp.int32, (8, count), 1)

    def build(device, carry):
        record = got_ref[device, 0:8, :]
        where_to = record.astype(jnp.int32)
        row = jnp.zeros((8, count), jnp.float32)
        for entry in range(nnz):
            hit = where_to[:, 32 + entry : 33 + entry] == column_id
            row = row + jnp.where(hit, record[:, entry : entry + 1], 0.0)
        matrix_ref[pl.ds(device * 8, 8), :] = row
        return carry

    lax.fori_loop(0, devices, build, 0, unroll=2)
    summed = lax.fori_loop(
        1, devices, lambda device, total: total + got_ref[device], got_ref[0], unroll=4
    )
    rhs = jnp.concatenate([summed[line : line + 1, HALF:] for line in range(count // HALF)], axis=1)
    rhs_column, diag_column = [], []
    for device in range(devices):
        eye = column_id == device * 8 + lax.broadcasted_iota(jnp.int32, (8, count), 0)
        rhs_column.append(jnp.sum(jnp.where(eye, rhs, 0.0), axis=1, keepdims=True))
        diag_column.append(got_ref[device, 0:8, DIAG_LANE : DIAG_LANE + 1])

    def to_row(columns):
        total = jnp.zeros((8, count), jnp.float32)
        for device in range(devices):
            eye = column_id == device * 8 + lax.broadcasted_iota(jnp.int32, (8, count), 0)
            total = total + jnp.where(eye, columns[device], 0.0)
        return jnp.sum(total, axis=0, keepdims=True)

    state = to_row([rhs_column[d] / diag_column[d] for d in range(devices)])
    for repeat in range(COARSE_SWEEPS - 1):
        columns = []
        for d in range(devices):
            product = jnp.sum(matrix_ref[d * 8 : d * 8 + 8, :] * state, axis=1, keepdims=True)
            columns.append((rhs_column[d] - product) / diag_column[d])
        state = to_row(columns)
    return state


def prolong_kernel(nnz, ids_ref, row_ref, got_ref, basis_ref, sol_ref, cor_ref, out_ref, matrix_ref):
    depth, own, width = cor_ref.shape
    entries = basis_ref.shape[0]
    count = matrix_ref.shape[0]
    state = solve(got_ref, matrix_ref, count, nnz)
    cells = ids_ref.shape[0]
    line = lax.broadcasted_iota(jnp.int32, (cells, count), 0)
    mine = jnp.zeros((cells, count), jnp.int32)
    for cell in range(cells):
        mine = jnp.where(line == cell, ids_ref[cell], mine)
    hit = mine == lax.broadcasted_iota(jnp.int32, (cells, count), 1)
    out_ref[...] = jnp.sum(jnp.where(hit, state, 0.0), axis=1, keepdims=True)
    ident = owner_of(basis_ref, depth * width)
    hit = ident == lax.broadcasted_iota(jnp.int32, (entries, count), 1)
    factor = jnp.sum(jnp.where(hit, state, 0.0), axis=1, keepdims=True)
    pick = jnp.where(
        row_ref[...] == lax.broadcasted_iota(jnp.int32, (own, entries), 0), 1.0, 0.0
    ).astype(jnp.bfloat16)
    for z in range(depth):
        part = basis_ref[:, z * width : (z + 1) * width].astype(jnp.float32) * factor
        added = jnp.dot(pick, part.astype(jnp.bfloat16), preferred_element_type=jnp.float32)
        cor_ref[z] = sol_ref[z] + added


def smooth_kernel(ext_ref, conduct_ref, scale_ref, src_ref, out_ref, mid_ref):
    planes, rows, width = ext_ref.shape
    depth, own, unused = out_ref.shape

    def sweep(v_ref, z):
        above, below = around(z, planes)
        conduct = conduct_ref[z]
        v, v_up, v_down = v_ref[z], v_ref[above], v_ref[below]
        near = in_plane(v) + v_up + v_down
        flow = in_plane(conduct * v) + conduct_ref[above] * v_up + conduct_ref[below] * v_down
        return (1.0 - OMEGA) * v + scale_ref[z] * (src_ref[0, z] + 0.5 * (conduct * near + flow))

    def first(step, carry):
        z = jnp.where(step == depth + 1, planes - 1, step)
        mid_ref[z] = sweep(ext_ref, z)
        return carry

    def second(z, carry):
        out_ref[z] = sweep(mid_ref, z)[:own]
        return carry

    lax.fori_loop(0, depth + 2, first, 0)
    lax.fori_loop(0, depth, second, 0)


def shards(
    solution,
    source,
    phase_label,
    phase_diffusivity,
    phase_uptake,
    send_tiles,
    support_slot,
    support_len,
    coarse_ids,
    basis_values,
    coarse_diag,
    coarse_off,
    coarse_cols,
):
    f32, bf16 = jnp.float32, jnp.bfloat16
    rows, depth, width = solution.shape
    voxels = depth * width
    slabs, tiles = lax.axis_size("slab"), lax.axis_size("tile")
    devices = slabs * tiles
    capacity = send_tiles.shape[3]
    cells, support, unused = basis_values.shape
    entries = cells * support
    count = cells * devices
    nnz = coarse_off.shape[1]
    shape = jax.ShapeDtypeStruct

    wide = voxels + 128
    outgoing = pl.pallas_call(
        sort_kernel,
        out_shape=shape((entries, wide), bf16),
        in_specs=[VMEM, SMEM, SMEM, VMEM],
        out_specs=VMEM,
        compiler_params=PARAMS,
        name="sort_basis",
    )(
        support_slot.reshape(1, entries),
        support_len.reshape(cells),
        coarse_ids,
        basis_values.reshape(entries, voxels),
    )
    basis = lax.all_to_all(
        outgoing.reshape(slabs, capacity, wide), "slab", split_axis=0, concat_axis=0, tiled=True
    ).reshape(entries, wide)

    stack = jnp.stack([solution, phase_label.astype(f32), source]).transpose(0, 2, 1, 3)
    ext = extend(stack, (0.0, -1.0, 0.0))
    planes, tall = ext.shape[1:3]
    residual, conduct, scale = pl.pallas_call(
        residual_kernel,
        out_shape=(
            shape((depth, rows, width), bf16),
            shape((planes, tall, width), f32),
            shape((planes, tall, width), f32),
        ),
        in_specs=[SMEM, SMEM, VMEM],
        out_specs=(VMEM, VMEM, VMEM),
        compiler_params=PARAMS,
        name="residual",
    )(phase_diffusivity, phase_uptake, ext)

    record = jnp.concatenate(
        [
            coarse_off,
            jnp.zeros((cells, 32 - nnz), f32),
            coarse_cols.astype(f32),
            jnp.zeros((cells, DIAG_LANE - 32 - nnz), f32),
            coarse_diag[:, None],
            jnp.zeros((cells, 128 - DIAG_LANE - 1), f32),
        ],
        axis=1,
    )
    lines = max(8, count // HALF)
    row_of = send_tiles.reshape(entries)
    payload = pl.pallas_call(
        restrict_kernel,
        out_shape=shape((devices, lines, 128), f32),
        in_specs=[VMEM, VMEM, VMEM, VMEM],
        out_specs=VMEM,
        compiler_params=PARAMS,
        name="restrict",
    )(row_of[:, None], record, residual, basis)
    got = lax.all_to_all(payload, ("slab", "tile"), split_axis=0, concat_axis=0, tiled=True)

    corrected, coarse_correction = pl.pallas_call(
        functools.partial(prolong_kernel, nnz),
        out_shape=(shape((depth, rows, width), f32), shape((cells, 1), f32)),
        in_specs=[SMEM, VMEM, VMEM, VMEM, VMEM],
        out_specs=(VMEM, VMEM),
        scratch_shapes=[pltpu.VMEM((count, count), f32)],
        compiler_params=PARAMS,
        name="solve_prolong",
    )(coarse_ids, row_of[None, :], got, basis, stack[0])

    cor_ext = extend(corrected[None], (0.0,))[0]
    smooth = pl.pallas_call(
        smooth_kernel,
        out_shape=shape((depth, rows, width), f32),
        in_specs=[VMEM, VMEM, VMEM, VMEM],
        out_specs=VMEM,
        scratch_shapes=[pltpu.VMEM((planes, tall, width), f32)],
        compiler_params=PARAMS,
        name="smooth",
    )(cor_ext, conduct, scale, ext[2:3])
    return smooth.transpose(1, 0, 2), coarse_correction.reshape(cells)


def solution(mesh):
    placed = (
        P("tile", "slab", None),
        P("tile", "slab", None),
        P("tile", "slab", None),
        P(),
        P(),
        P("slab", "tile", None, None),
        P("slab", "tile", None),
        P("slab", "tile", None),
        P(("slab", "tile")),
        P(("slab", "tile"), None, None),
        P(("slab", "tile")),
        P(("slab", "tile"), None),
        P(("slab", "tile"), None),
    )
    return jax.shard_map(
        shards,
        mesh=mesh,
        in_specs=placed,
        out_specs=(P("tile", "slab", None), P(("slab", "tile"))),
        check_vma=False,
    )
```

time: 341 us -> 75.3 us (0.22)
  blocking collectives: 198 us -> 0 us
  starting transfers between devices: 52.5 us -> 19.1 us
  other arithmetic: 29.7 us -> 6.28 us
  Pallas kernels: 0 us -> 18.1 us
  waiting for transfers between devices: 34.6 us -> 21.7 us
  local copies, waits for them, and re-layouts: 19.8 us -> 8.63 us
    unnamed x5 -> x0, blocking collectives: 198 us -> none
    ppermute x16 -> x8, starting transfers between devices: 39.5 us -> 9.22 us  [the longest x2 7.51 us: extend(): high = lax.ppermute(stack[:, :2], 'slab', wheel(slabs, -1))]
    pallas_call x0 -> x5, Pallas kernels: none -> 18.1 us  [the longest x1 6.11 us: shards(): pl.pallas_call(functools.partial(prolong_kernel, nnz), out_shape=(shape((...]
    all_to_all x2, waiting for transfers between devices: 23.7 us -> 7.04 us  [the longest x1 7.03 us: shards(): lax.all_to_all(payload, ('slab', 'tile'), split_axis=0, concat_axis=0, ti...]
    gather x9 -> x0, local copies, waits for them, and re-layouts: 12.4 us -> none  [the longest x6 7.56 us: shards(): gathered[coarse_cols]]
    add x3 -> x0, other arithmetic: 11.1 us -> none  [the longest x2 6.87 us: shards(): corrected + OMEGA * (source - operate(corrected, weights, diagonal)) / di...]
    unnamed x5 -> x0, other arithmetic: 5.8 us -> none
    ppermute x16 -> x8, waiting for transfers between devices: 10.9 us -> 14.7 us  [the longest x2 5.48 us: extend(): low = lax.ppermute(stack[:, -2:], 'slab', wheel(slabs, 1))]
  transfers between devices with their start and end apart: 18 -> 10, of which waited for: 9 -> 8; matrix products, arithmetic and copies ran while one was open for 2% -> 7% of each run, Pallas kernels for 0% -> 9%
where the time goes in v1:
time: 75.3 us; the launch traced here: 74.7 us
  waiting for transfers between devices  21.7 us (29%)
  starting transfers between devices  19.1 us (25%)
  Pallas kernels  18.1 us (24%)
  local copies, waits for them, and re-layouts  8.63 us (11%)
  other arithmetic  6.28 us (8%)
  between operations  0.97 us (1%)
    ppermute x2, starting transfers between devices, extend(): high = lax.ppermute(stack[:, :2], 'slab', wheel(slabs, -1))  7.51 us
    all_to_all x1, waiting for transfers between devices, shards(): lax.all_to_all(payload, ('slab', 'tile'), split_axis=0, concat_axis=0, ti...  7.03 us
    pallas_call x1, Pallas kernels, shards(): pl.pallas_call(functools.partial(prolong_kernel, nnz), out_shape=(shape((...  6.11 us
    all_to_all x1, starting transfers between devices, shards(): lax.all_to_all(outgoing.reshape(slabs, capacity, wide), 'slab', split_axi...  6 us
    ppermute x2, waiting for transfers between devices, extend(): low = lax.ppermute(stack[:, -2:], 'slab', wheel(slabs, 1))  5.48 us
    unnamed x35, local copies, waits for them, and re-layouts  5.25 us
    pallas_call x1, Pallas kernels, shards(): pl.pallas_call(residual_kernel, out_shape=(shape((depth, rows, width), bf...  4.94 us
    ppermute x2, waiting for transfers between devices, extend(): low = lax.ppermute(stack[:, :, -2:], 'tile', wheel(tiles, 1))  4.62 us
  transfers between devices with their start and end apart: 10, of which 8 were waited for; matrix products, arithmetic and copies ran while one was open for 7% of the time, Pallas kernels for 9%

profile of v1, /device:TPU:0, one launch (start us, length us, event | category | flops | bytes accessed | tf_op | source)
XLA Modules:
  0.0 74.7 jit_solution(6018083066485041289)
XLA Ops:
  0.6 1.4 %fusion = f32[1,32,16,256]{3,1,2,0:T(8,128)S(1)} fusion(s32[32,16,256]{2,1,0:T(8,128)} %param.17), kind=kLoop, calls=%fused_computation.6 | loop fusion | flops 131072 | bytes 1048576 | tf_op jit(solution)/shard_map/stack | solution.py:293
  2.0 1.8 %copy_bitcast_fusion = (f32[1,32,16,256]{3,1,2,0:T(8,128)S(1)}, f32[1,32,16,256]{3,1,2,0:T(8,128)S(1)}) fusion(f32[32,16,256]{2,1,0:T(8,128)} %param.16, f32[32,16,256]{2,1,0:T(8,128)} %param.15), kind=kLoop, calls=%fused_computation.4 | loop fusion | bytes 2097152 | tf_op jit(solution)/shard_map/stack | solution.py:293
  4.1 6.0 %collective-permute-start = (f32[3,2,32,256]{3,2,1,0:T(8,128)S(1)}, f32[3,2,32,256]{3,2,1,0:T(8,128)S(1)}, u32[]{:S(2)}, u32[]{:S(2)}) collective-permute-start(f32[3,2,32,256]{3,2,1,0:T(8,128)S(1)} %get-tuple-element.18), channel_id=1, source_target_pairs={{0,28},{4,0},{8,4},{12,8},{16,12},{20,16},{24,20},{28,24},{1,29},{... | collective-permute-start | bytes 589832 | tf_op jit(solution)/shard_map/ppermute | solution.py:30
  10.2 1.6 %sort_basis.1 = bf16[64,4224]{1,0:T(8,128)(2,1)} custom-call(s32[1,64]{1,0:T(1,128)S(1)} %bitcast.31, s32[8]{0:T(128)S(1)} %bitcast.32, s32[8]{0:T(128)S(1)} %copy-done.6, bf16[64,4096]{1,0:T(8,128)(2,1)S(1)} %bitcast.30), custom_call_target="tpu_custom_call" | custom-call | tf_op jit(solution)/shard_map/sort_basis/pallas_call | solution.py:276
  11.8 6.0 %all-to-all-start = ((bf16[8,8,4224]{2,1,0:T(8,128)(2,1)}), bf16[8,8,4224]{2,1,0:T(8,128)(2,1)S(1)}, u32[]{:S(2)}, u32[]{:S(2)}) async-start(bf16[8,8,4224]{2,1,0:T(8,128)(2,1)} %bitcast.8), calls=%async_computation | async-start | bytes 1081344 | tf_op jit(solution)/shard_map/all_to_all | solution.py:289
  17.8 1.4 %collective-permute-done.1 = f32[3,2,32,256]{3,2,1,0:T(8,128)S(1)} collective-permute-done((f32[3,2,32,256]{3,2,1,0:T(8,128)S(1)}, f32[3,2,32,256]{3,2,1,0:T(8,128)S(1)}, u32[]{:S(2)}, u32[]{:S(2)}) %collective-permute-start.1) | collective-permute-done | bytes 196640 | tf_op jit(solution)/shard_map/ppermute | solution.py:29
  19.4 0.5 collective-permute-start.3
  20.3 1.9 %collective-permute-done.2 = f32[3,20,2,256]{3,2,1,0:T(2,128)S(1)} collective-permute-done((f32[3,20,2,256]{3,2,1,0:T(2,128)S(1)}, f32[3,20,2,256]{3,2,1,0:T(2,128)S(1)}, u32[]{:S(2)}, u32[]{:S(2)}) %collective-permute-start.2) | collective-permute-done | bytes 122912 | tf_op jit(solution)/shard_map/ppermute | solution.py:35
  22.1 3.0 %collective-permute-done.3 = f32[3,20,2,256]{3,2,1,0:T(2,128)S(1)} collective-permute-done((f32[3,20,2,256]{3,2,1,0:T(2,128)S(1)}, f32[3,20,2,256]{3,2,1,0:T(2,128)S(1)}, u32[]{:S(2)}, u32[]{:S(2)}) %collective-permute-start.3) | collective-permute-done | bytes 122912 | tf_op jit(solution)/shard_map/ppermute | solution.py:34
  25.3 1.8 %pad_maximum_fusion.ext_ref = f32[3,20,40,256]{3,2,1,0:T(8,128)S(1)} fusion(f32[3,20,2,256]{3,2,1,0:T(2,128)S(1)} %get-tuple-element.25, f32[3,20,2,256]{3,2,1,0:T(2,128)S(1)} %get-tuple-element.24, f32[3,2,32,256]{3,2,1,0:T(8,128)S(1)} %get-tuple-element.27, f32[3,2,32,256]{3,2,1,0:T(8,128)S(1)} %get-tuple-element.26, f32[3,16,32,256]{3,2,1,0:T(8,128)} %copy-done.11, ...), kind=kLoop, calls=%fused_computation | loop fusion | flops 3072000 | bytes 4669600 | tf_op jit(solution)/shard_map/concatenate | solution.py:39
  27.1 4.9 %residual.1 = (bf16[16,32,256]{2,1,0:T(8,128)(2,1)S(1)}, f32[20,40,256]{2,1,0:T(8,128)S(1)}, f32[20,40,256]{2,1,0:T(8,128)S(1)}) custom-call(f32[3]{0:T(128)S(1)} %copy-done.9, f32[3]{0:T(128)S(1)} %copy-done.10, f32[3,20,40,256]{3,2,1,0:T(8,128)S(1)} %pad_maximum_fusion.ext_ref), custom_call_target="tpu_custom_call" | custom-call | tf_op jit(solution)/shard_map/residual/pallas_call | solution.py:296
  32.0 0.9 %copy-done.1 = f32[20,40,256]{2,1,0:T(8,128)} copy-done((f32[20,40,256]{2,1,0:T(8,128)}, f32[20,40,256]{2,1,0:T(8,128)S(1)}, u32[]{:S(2)}) %copy-start.1) | copy-done | bytes 819224
  32.9 0.9 %copy-done.3 = f32[20,40,256]{2,1,0:T(8,128)} copy-done((f32[20,40,256]{2,1,0:T(8,128)}, f32[20,40,256]{2,1,0:T(8,128)S(1)}, u32[]{:S(2)}) %copy-start.3) | copy-done | bytes 819224
  33.8 1.1 %restrict.1 = f32[32,8,128]{2,1,0:T(8,128)} custom-call(s32[64,1]{1,0:T(8,128)S(1)} %broadcast_in_dim_reshape.8.row_ref, f32[8,128]{1,0:T(8,128)S(1)} %concatenate.15.record_ref, bf16[16,32,256]{2,1,0:T(8,128)(2,1)S(1)} %get-tuple-element.7.res_ref, bf16[64,4224]{1,0:T(8,128)(2,1)S(1)} %bitcast.24), custom_call_target="tpu_custom_call" | custom-call | tf_op jit(solution)/shard_map/restrict/pallas_call | solution.py:322
  34.9 3.9 %all-to-all-start.1 = ((f32[32,8,128]{2,1,0:T(8,128)}), f32[32,8,128]{2,1,0:T(8,128)}, u32[]{:S(2)}, u32[]{:S(2)}) async-start(f32[32,8,128]{2,1,0:T(8,128)} %restrict.1), calls=%async_computation.1 | async-start | bytes 262144 | tf_op jit(solution)/shard_map/all_to_all | solution.py:330
  38.9 1.1 %slice_bitcast_fusion.sol_ref = f32[16,32,256]{2,1,0:T(8,128)S(1)} fusion(f32[3,16,32,256]{3,2,1,0:T(8,128)} %copy-done.11), kind=kLoop, calls=%fused_computation.3 | loop fusion | bytes 1048576 | tf_op jit(solution)/shard_map/squeeze | solution.py:340
  40.0 7.0 %all-to-all-done.1.got_ref = f32[32,8,128]{2,1,0:T(8,128)} async-done(((f32[32,8,128]{2,1,0:T(8,128)}), f32[32,8,128]{2,1,0:T(8,128)}, u32[]{:S(2)}, u32[]{:S(2)}) %all-to-all-start.1) | async-done | bytes 131104 | tf_op jit(solution)/shard_map/all_to_all | solution.py:330
  47.0 6.1 %solve_prolong.1 = (f32[16,32,256]{2,1,0:T(8,128)S(1)}, f32[8,1]{1,0:T(8,128)S(1)}) custom-call(s32[8]{0:T(128)S(1)} %copy-done.6, s32[1,64]{1,0:T(1,128)S(1)} %broadcast_in_dim_reshape.6.row_ref, f32[32,8,128]{2,1,0:T(8,128)} %all-to-all-done.1.got_ref, bf16[64,4224]{1,0:T(8,128)(2,1)S(1)} %bitcast.25, f32[16,32,256]{2,1,0:T(8,128)S(1)} %slice_bitcast_fusion.sol_ref), custom_call_target="tpu_custom_call" | custom-call | tf_op jit(solution)/shard_map/solve_prolong/pallas_call | solution.py:332
  53.2 1.5 %collective-permute-start.4 = (f32[1,2,32,256]{3,2,1,0:T(8,128)S(1)}, f32[1,2,32,256]{3,2,1,0:T(8,128)S(1)}, u32[]{:S(2)}, u32[]{:S(2)}) collective-permute-start(f32[1,2,32,256]{3,2,1,0:T(8,128)S(1)} %get-tuple-element.22), channel_id=1, source_target_pairs={{0,28},{4,0},{8,4},{12,8},{16,12},{20,16},{24,20},{28,24},{1,29},{... | collective-permute-start | bytes 196616 | tf_op jit(solution)/shard_map/ppermute | solution.py:30
  54.6 0.6 collective-permute-start.5
  55.2 2.2 %collective-permute-done.4 = f32[1,2,32,256]{3,2,1,0:T(8,128)S(1)} collective-permute-done((f32[1,2,32,256]{3,2,1,0:T(8,128)S(1)}, f32[1,2,32,256]{3,2,1,0:T(8,128)S(1)}, u32[]{:S(2)}, u32[]{:S(2)}) %collective-permute-start.4) | collective-permute-done | bytes 65568 | tf_op jit(solution)/shard_map/ppermute | solution.py:30
  57.5 4.1 %collective-permute-done.5 = f32[1,2,32,256]{3,2,1,0:T(8,128)S(1)} collective-permute-done((f32[1,2,32,256]{3,2,1,0:T(8,128)S(1)}, f32[1,2,32,256]{3,2,1,0:T(8,128)S(1)}, u32[]{:S(2)}, u32[]{:S(2)}) %collective-permute-start.5) | collective-permute-done | bytes 65568 | tf_op jit(solution)/shard_map/ppermute | solution.py:29
  61.8 0.6 reduce
  62.4 0.5 collective-permute-start.7
  62.9 0.5 collective-permute-done.6
  63.4 0.8 %broadcast_select_fusion.5 = f32[1,20,2,256]{3,2,1,0:T(2,128)S(1)} fusion(f32[1,20,2,256]{3,2,1,0:T(2,128)} %collective-permute-done.6, pred[]{:T(512)S(6)} %eq.18), kind=kLoop, calls=%fused_computation.19 | loop fusion | flops 10240 | bytes 81921 | tf_op jit(solution)/shard_map/jit(_where)/select_n | solution.py:37
  64.2 1.7 %collective-permute-done.7 = f32[1,20,2,256]{3,2,1,0:T(2,128)S(1)} collective-permute-done((f32[1,20,2,256]{3,2,1,0:T(2,128)S(1)}, f32[1,20,2,256]{3,2,1,0:T(2,128)S(1)}, u32[]{:S(2)}, u32[]{:S(2)}) %collective-permute-start.7) | collective-permute-done | bytes 40992 | tf_op jit(solution)/shard_map/ppermute | solution.py:34
  65.9 1.2 %maximum_bitcast_fusion.1.ext_ref = f32[20,40,256]{2,1,0:T(8,128)S(1)} fusion(f32[1,20,2,256]{3,2,1,0:T(2,128)S(1)} %broadcast_select_fusion.4, f32[1,20,2,256]{3,2,1,0:T(2,128)S(1)} %broadcast_select_fusion.5, f32[1,2,32,256]{3,2,1,0:T(8,128)S(1)} %broadcast_select_fusion.6, f32[1,2,32,256]{3,2,1,0:T(8,128)S(1)} %broadcast_select_fusion.7, ...), kind=kLoop, calls=%fused_computation.2 | loop fusion | flops 1024000 | bytes 1556640 | tf_op jit(solution)/shard_map/squeeze | solution.py:342
  67.1 1.1 %copy-done.2 = f32[20,40,256]{2,1,0:T(8,128)S(1)} copy-done((f32[20,40,256]{2,1,0:T(8,128)S(1)}, f32[20,40,256]{2,1,0:T(8,128)}, u32[]{:S(2)}) %copy-start.2) | copy-done | bytes 819224
  68.2 1.1 %copy-done.4 = f32[20,40,256]{2,1,0:T(8,128)S(1)} copy-done((f32[20,40,256]{2,1,0:T(8,128)S(1)}, f32[20,40,256]{2,1,0:T(8,128)}, u32[]{:S(2)}) %copy-start.4) | copy-done | bytes 819224
  69.3 4.3 %smooth.1 = f32[16,32,256]{2,1,0:T(8,128)S(1)} custom-call(f32[20,40,256]{2,1,0:T(8,128)S(1)} %maximum_bitcast_fusion.1.ext_ref, f32[20,40,256]{2,1,0:T(8,128)S(1)} %copy-done.2, f32[20,40,256]{2,1,0:T(8,128)S(1)} %copy-done.4, f32[1,20,40,256]{3,2,1,0:T(8,128)S(1)} %slice.45.src_ref), custom_call_target="tpu_custom_call" | custom-call | tf_op jit(solution)/shard_map/smooth/pallas_call | solution.py:343
  73.6 1.1 %copy.28 = f32[32,16,256]{2,1,0:T(8,128)} copy(f32[32,16,256]{2,0,1:T(8,128)S(1)} %bitcast.29) | data formatting | bytes 1048576
  (56 shorter events, 1.3 us)
Async XLA Ops:
  3.8 6.3 %copy-start.5 = (bf16[8,8,4096]{2,1,0:T(8,128)(2,1)S(1)}, bf16[8,8,4096]{2,1,0:T(8,128)(2,1)}, u32[]{:S(2)}) copy-start(bf16[8,8,4096]{2,1,0:T(8,128)(2,1)} %param.24) | copy-start | bytes 1572868
  3.8 6.3 %copy-start.6 = (s32[8]{0:T(128)S(1)}, s32[8]{0:T(128)}, u32[]{:S(2)}) copy-start(s32[8]{0:T(128)} %ids_ref.3) | copy-start | bytes 100
  3.8 6.3 %copy-start.7 = (s32[1,1,64]{2,1,0:T(1,128)S(1)}, s32[1,1,64]{2,1,0:T(1,128)}, u32[]{:S(2)}) copy-start(s32[1,1,64]{2,1,0:T(1,128)} %param.21) | copy-start | bytes 772
  3.8 6.3 %copy-start.8 = (s32[1,1,8]{2,1,0:T(1,128)S(1)}, s32[1,1,8]{2,1,0:T(1,128)}, u32[]{:S(2)}) copy-start(s32[1,1,8]{2,1,0:T(1,128)} %param.22) | copy-start | bytes 100
  3.8 15.3 %copy-start.15 = (f32[3]{0:T(128)S(1)}, f32[3]{0:T(128)}, u32[]{:S(2)}) copy-start(f32[3]{0:T(128)} %constant.8.clone) | copy-start | bytes 40
  4.0 21.2 %copy-start.11 = (f32[3,16,32,256]{3,2,1,0:T(8,128)}, f32[3,16,32,256]{3,2,1,0:T(8,128)S(1)}, u32[]{:S(2)}) copy-start(f32[3,16,32,256]{3,2,1,0:T(8,128)S(1)} %maximum_bitcast_fusion) | copy-start | bytes 4718596
  4.1 13.7 %collective-permute-start = (f32[3,2,32,256]{3,2,1,0:T(8,128)S(1)}, f32[3,2,32,256]{3,2,1,0:T(8,128)S(1)}, u32[]{:S(2)}, u32[]{:S(2)}) collective-permute-start(f32[3,2,32,256]{3,2,1,0:T(8,128)S(1)} %get-tuple-element.18), channel_id=1, source_target_pairs={{0,28},{4,0},{8,4},{12,8},{16,12},{20,16},{24,20},{28,24},{1,29},{... | collective-permute-start | bytes 589832 | tf_op jit(solution)/shard_map/ppermute | solution.py:30
  10.1 9.1 %collective-permute-start.1 = (f32[3,2,32,256]{3,2,1,0:T(8,128)S(1)}, f32[3,2,32,256]{3,2,1,0:T(8,128)S(1)}, u32[]{:S(2)}, u32[]{:S(2)}) collective-permute-start(f32[3,2,32,256]{3,2,1,0:T(8,128)S(1)} %get-tuple-element.19), channel_id=1, source_target_pairs={{0,4},{4,8},{8,12},{12,16},{16,20},{20,24},{24,28},{28,0},{1,5},{5... | collective-permute-start | bytes 589832 | tf_op jit(solution)/shard_map/ppermute | solution.py:29
  10.1 9.8 %copy-start.16 = (f32[8]{0:T(128)S(1)}, f32[8]{0:T(128)}, u32[]{:S(2)}) copy-start(f32[8]{0:T(128)} %param.25) | copy-start | bytes 100
  10.1 9.9 %copy-start.14 = (s32[8,26]{1,0:T(8,128)S(1)}, s32[8,26]{1,0:T(8,128)}, u32[]{:S(2)}) copy-start(s32[8,26]{1,0:T(8,128)} %param.27) | copy-start | bytes 2500
  10.2 9.9 %copy-start.12 = (s32[1,1,8,8]{3,2,1,0:T(8,128)S(1)}, s32[1,1,8,8]{3,2,1,0:T(8,128)}, u32[]{:S(2)}) copy-start(s32[1,1,8,8]{3,2,1,0:T(8,128)} %param.20) | copy-start | bytes 772
  10.2 10.0 %copy-start.13 = (f32[8,26]{1,0:T(8,128)S(1)}, f32[8,26]{1,0:T(8,128)}, u32[]{:S(2)}) copy-start(f32[8,26]{1,0:T(8,128)} %param.26) | copy-start | bytes 2500
  11.8 22.0 %all-to-all-start = ((bf16[8,8,4224]{2,1,0:T(8,128)(2,1)}), bf16[8,8,4224]{2,1,0:T(8,128)(2,1)S(1)}, u32[]{:S(2)}, u32[]{:S(2)}) async-start(bf16[8,8,4224]{2,1,0:T(8,128)(2,1)} %bitcast.8), calls=%async_computation | async-start | bytes 1081344 | tf_op jit(solution)/shard_map/all_to_all | solution.py:289
  19.4 2.8 %collective-permute-start.2 = (f32[3,20,2,256]{3,2,1,0:T(2,128)S(1)}, f32[3,20,2,256]{3,2,1,0:T(2,128)S(1)}, u32[]{:S(2)}, u32[]{:S(2)}) collective-permute-start(f32[3,20,2,256]{3,2,1,0:T(2,128)S(1)} %get-tuple-element.16), channel_id=1, source_target_pairs={{0,3},{1,0},{2,1},{3,2},{4,7},{5,4},{6,5},{7,6},{8,11},{9,8},{10,9... | collective-permute-start | bytes 368648 | tf_op jit(solution)/shard_map/ppermute | solution.py:35
  19.4 5.7 %collective-permute-start.3 = (f32[3,20,2,256]{3,2,1,0:T(2,128)S(1)}, f32[3,20,2,256]{3,2,1,0:T(2,128)S(1)}, u32[]{:S(2)}, u32[]{:S(2)}) collective-permute-start(f32[3,20,2,256]{3,2,1,0:T(2,128)S(1)} %get-tuple-element.17), channel_id=1, source_target_pairs={{0,1},{1,2},{2,3},{3,0},{4,5},{5,6},{6,7},{7,4},{8,9},{9,10},{10,1... | collective-permute-start | bytes 368648 | tf_op jit(solution)/shard_map/ppermute | solution.py:34
  25.2 1.8 %copy-start.9 = (f32[3]{0:T(128)S(1)}, f32[3]{0:T(128)}, u32[]{:S(2)}) copy-start(f32[3]{0:T(128)} %diff_ref.1) | copy-start | bytes 40
  25.3 1.8 %copy-start.10 = (f32[3]{0:T(128)S(1)}, f32[3]{0:T(128)}, u32[]{:S(2)}) copy-start(f32[3]{0:T(128)} %upt_ref.1) | copy-start | bytes 40
  32.0 0.9 %copy-start.1 = (f32[20,40,256]{2,1,0:T(8,128)}, f32[20,40,256]{2,1,0:T(8,128)S(1)}, u32[]{:S(2)}) copy-start(f32[20,40,256]{2,1,0:T(8,128)S(1)} %get-tuple-element.9.conduct_ref) | copy-start | bytes 2457604
  32.9 0.9 %copy-start.3 = (f32[20,40,256]{2,1,0:T(8,128)}, f32[20,40,256]{2,1,0:T(8,128)S(1)}, u32[]{:S(2)}) copy-start(f32[20,40,256]{2,1,0:T(8,128)S(1)} %get-tuple-element.10.scale_ref) | copy-start | bytes 2457604
  34.9 12.1 %all-to-all-start.1 = ((f32[32,8,128]{2,1,0:T(8,128)}), f32[32,8,128]{2,1,0:T(8,128)}, u32[]{:S(2)}, u32[]{:S(2)}) async-start(f32[32,8,128]{2,1,0:T(8,128)} %restrict.1), calls=%async_computation.1 | async-start | bytes 262144 | tf_op jit(solution)/shard_map/all_to_all | solution.py:330
  53.1 8.7 %copy-start = (f32[16,32,256]{2,1,0:T(8,128)}, f32[16,32,256]{2,1,0:T(8,128)S(1)}, u32[]{:S(2)}) copy-start(f32[16,32,256]{2,1,0:T(8,128)S(1)} %get-tuple-element.8) | copy-start | bytes 1572868
  53.2 4.3 %collective-permute-start.4 = (f32[1,2,32,256]{3,2,1,0:T(8,128)S(1)}, f32[1,2,32,256]{3,2,1,0:T(8,128)S(1)}, u32[]{:S(2)}, u32[]{:S(2)}) collective-permute-start(f32[1,2,32,256]{3,2,1,0:T(8,128)S(1)} %get-tuple-element.22), channel_id=1, source_target_pairs={{0,28},{4,0},{8,4},{12,8},{16,12},{20,16},{24,20},{28,24},{1,29},{... | collective-permute-start | bytes 196616 | tf_op jit(solution)/shard_map/ppermute | solution.py:30
  54.6 7.0 %collective-permute-start.5 = (f32[1,2,32,256]{3,2,1,0:T(8,128)S(1)}, f32[1,2,32,256]{3,2,1,0:T(8,128)S(1)}, u32[]{:S(2)}, u32[]{:S(2)}) collective-permute-start(f32[1,2,32,256]{3,2,1,0:T(8,128)S(1)} %get-tuple-element.23), channel_id=1, source_target_pairs={{0,4},{4,8},{8,12},{12,16},{16,20},{20,24},{24,28},{28,0},{1,5},{5... | collective-permute-start | bytes 196616 | tf_op jit(solution)/shard_map/ppermute | solution.py:29
  61.6 1.7 %collective-permute-start.6 = (f32[1,20,2,256]{3,2,1,0:T(2,128)S(1)}, f32[1,20,2,256]{3,2,1,0:T(2,128)}, u32[]{:S(2)}, u32[]{:S(2)}) collective-permute-start(f32[1,20,2,256]{3,2,1,0:T(2,128)S(1)} %get-tuple-element.20), channel_id=1, source_target_pairs={{0,3},{1,0},{2,1},{3,2},{4,7},{5,4},{6,5},{7,6},{8,11},{9,8},{10,9... | collective-permute-start | bytes 122888 | tf_op jit(solution)/shard_map/ppermute | solution.py:35
  62.4 3.4 %collective-permute-start.7 = (f32[1,20,2,256]{3,2,1,0:T(2,128)S(1)}, f32[1,20,2,256]{3,2,1,0:T(2,128)S(1)}, u32[]{:S(2)}, u32[]{:S(2)}) collective-permute-start(f32[1,20,2,256]{3,2,1,0:T(2,128)S(1)} %get-tuple-element.21), channel_id=1, source_target_pairs={{0,1},{1,2},{2,3},{3,0},{4,5},{5,6},{6,7},{7,4},{8,9},{9,10},{10,1... | collective-permute-start | bytes 122888 | tf_op jit(solution)/shard_map/ppermute | solution.py:34
  67.1 1.1 %copy-start.2 = (f32[20,40,256]{2,1,0:T(8,128)S(1)}, f32[20,40,256]{2,1,0:T(8,128)}, u32[]{:S(2)}) copy-start(f32[20,40,256]{2,1,0:T(8,128)} %copy-done.1) | copy-start | bytes 2457604
  68.2 1.1 %copy-start.4 = (f32[20,40,256]{2,1,0:T(8,128)S(1)}, f32[20,40,256]{2,1,0:T(8,128)}, u32[]{:S(2)}) copy-start(f32[20,40,256]{2,1,0:T(8,128)} %copy-done.3) | copy-start | bytes 2457604

commit v2 on v0

v2 whole, which is shorter than its diff:
```python
import functools

import jax
import jax.numpy as jnp
from jax import lax
from jax.experimental import pallas as pl
from jax.experimental.pallas import tpu as pltpu
from jax.sharding import PartitionSpec as P

COARSE_SWEEPS = 4
SMOOTH_SWEEPS = 2
OMEGA = 0.8

VMEM = pl.BlockSpec(memory_space=pltpu.VMEM)
SMEM = pl.BlockSpec(memory_space=pltpu.SMEM)
HBM = pl.BlockSpec(memory_space=pltpu.HBM)
MIB = 1024 * 1024
COLS_LANE = 32
HALF = 64
DIAG_LANE = 60


def params(mib=16):
    return pltpu.CompilerParams(vmem_limit_bytes=mib * MIB)


def wheel(count, step):
    return [(i, (i + step) % count) for i in range(count)]


def pairs(count, odd):
    start = 1 if odd else 0
    table = list(range(count))
    for i in range(start, count - 1, 2):
        table[i], table[i + 1] = i + 1, i
    return list(enumerate(table))


def fetch(pairs_of_refs, sems):
    copies = [
        pltpu.make_async_copy(source, target, sems.at[k])
        for k, (source, target) in enumerate(pairs_of_refs)
    ]
    for copy in copies:
        copy.start()
    return copies


def prepare_kernel(
    slot_hbm, len_hbm, ids_hbm, basis_hbm, sol_hbm, label_hbm, src_hbm, table_hbm,
    out_hbm, even_ref, odd_ref, late_even_ref, late_odd_ref, top_ref, bottom_ref,
    slot_ref, len_ref, ids_ref, basis_ref, sol_ref, label_ref, src_ref, table_ref, out_ref, sems, *, capacity
):
    entries, voxels = basis_ref.shape
    rows, depth, width = sol_ref.shape
    cells = len_ref.shape[0]
    support = entries // cells
    border = (out_ref.shape[1] - 128 - voxels) // 2
    chunk, half = voxels // 4, depth // 2
    pieces = [
        (basis_hbm.at[:, pl.ds(k * chunk, chunk)], basis_ref.at[:, pl.ds(k * chunk, chunk)]) for k in range(4)
    ]
    blocks = [
        (hbm.at[:, pl.ds(start, half)], ref.at[:, pl.ds(start, half)])
        for hbm, ref in ((sol_hbm, sol_ref), (label_hbm, label_ref), (src_hbm, src_ref))
        for start in (0, half)
    ]
    small = [(slot_hbm, slot_ref), (len_hbm, len_ref), (ids_hbm, ids_ref), (table_hbm, table_ref)]
    copies = fetch(small + pieces + blocks, sems)
    for copy in copies[:4]:
        copy.wait()
    lane = lax.broadcasted_iota(jnp.int32, (1, entries), 1)
    length = jnp.zeros((1, entries), jnp.int32)
    ident = jnp.zeros((1, entries), jnp.int32)
    for cell in range(cells):
        here = lane // support == cell
        length = jnp.where(here, len_ref[cell], length)
        ident = jnp.where(here, ids_ref[cell], ident)
    live = lane % support < length
    slot = jnp.where(live, slot_ref[...], -1)
    row = lax.broadcasted_iota(jnp.int32, (entries, entries), 0)
    above = jnp.where(row >= entries - capacity, row + capacity - entries, row + capacity)
    below = jnp.where(row < capacity, row - capacity + entries, row - capacity)
    hits = [slot == row, slot == above, slot == below]
    picks = [jnp.where(hit, 1.0, 0.0).astype(jnp.bfloat16) for hit in hits]
    sent = []

    def move(pick, start, size, target):
        out_ref[:, target : target + size] = jnp.dot(
            pick, basis_ref[:, start : start + size], preferred_element_type=jnp.float32
        ).astype(jnp.bfloat16)

    def send(start, size):
        part = pl.ds(start, size)
        copy = pltpu.make_async_copy(out_ref.at[:, part], out_hbm.at[:, part], sems.at[len(copies) + len(sent)])
        copy.start()
        sent.append(copy)

    extra = lax.broadcasted_iota(jnp.int32, (entries, 128), 1)
    tail = jnp.zeros((entries, 128), jnp.float32)
    for k, hit in enumerate(hits):
        low = jnp.sum(jnp.where(hit, ident % 256, 0).astype(jnp.float32), axis=1, keepdims=True)
        high = jnp.sum(jnp.where(hit, ident // 256, 0).astype(jnp.float32), axis=1, keepdims=True)
        tail = jnp.where(extra == 2 * k, low, jnp.where(extra == 2 * k + 1, high, tail))
    out_ref[:, voxels + 2 * border :] = tail.astype(jnp.bfloat16)
    for k in range(4):
        copies[4 + k].wait()
        for start in range(k * chunk, (k + 1) * chunk, 512):
            move(picks[0], start, 512, start)
        send(k * chunk, chunk)
        if k == 0:
            move(picks[1], 0, border, voxels)
    move(picks[2], voxels - border, border, voxels + border)
    send(voxels, 2 * border + 128)

    slots = table_ref.shape[0]
    odd = lax.axis_index("slab") % 2 == 1
    for ref in (even_ref, odd_ref):
        ref[rows + 8 :] = jnp.zeros((ref.shape[0] - rows - 8, width), jnp.float32)
        ref[rows + 8 : rows + 8 + slots, :capacity] = table_ref[...].astype(jnp.float32)
    for copy in copies[8:]:
        copy.wait()

    def planes(start):
        parts = [ref[:, start : start + 2, :].astype(jnp.float32) for ref in (sol_ref, label_ref, src_ref, src_ref)]
        block = jnp.transpose(jnp.concatenate(parts, axis=1), (1, 0, 2))
        return [block[k] for k in range(6)]

    near, far, label, label_far, origin, unused = planes(0)
    down = near, pack_labels(label, label_far), far, origin
    far, near, label_far, label, unused, origin = planes(depth - 2)
    up = near, pack_labels(label, label_far), far, origin
    for first, second, early, late in ((up, down, even_ref, late_even_ref), (down, up, odd_ref, late_odd_ref)):
        mine = [jnp.where(odd, b, a) for a, b in zip(first, second)]
        early[:rows] = mine[0]
        early[rows : rows + 8] = mine[1]
        late[:rows] = mine[2]
        late[rows:] = mine[3]
    for ref, near, far in ((top_ref, 0, 1), (bottom_ref, rows - 1, rows - 2)):
        ref[0, :depth] = sol_ref[near]
        ref[1, :depth] = (label_ref[near] + 3 * label_ref[far]).astype(jnp.float32)
        ref[2, :depth] = src_ref[near]
        for k in range(3):
            ref[k, depth:] = jnp.zeros((ref.shape[1] - depth, width), jnp.float32)
    for copy in sent:
        copy.wait()


def pack_labels(near, far):
    pair = near + 3.0 * far
    packed = pair[0:8]
    for k in range(1, pair.shape[0] // 8):
        packed = packed + float(9**k) * pair[8 * k : 8 * k + 8]
    return packed


def unpack_labels(packed, rows):
    found = []
    for k in range(rows // 8):
        rest = jnp.floor((packed + 0.5) * (1.0 / 9.0))
        found.append(packed - 9.0 * rest)
        packed = rest
    return part_pair(jnp.concatenate(found, axis=0))


def part_pair(pair):
    far = jnp.floor((pair + 0.5) * (1.0 / 3.0))
    return pair - 3.0 * far, far


def halo_labels(even_ref, odd_ref, own):
    swap = lax.axis_index("slab") % 2 == 1
    even, odd = even_ref[own : own + 8], odd_ref[own : own + 8]
    near_high, far_high = unpack_labels(jnp.where(swap, odd, even), own)
    near_low, far_low = unpack_labels(jnp.where(swap, even, odd), own)
    return near_high, far_high, far_low, near_low


def edge_kernel(top_in, bottom_in, even_in, odd_in, top_ref, bottom_ref, even_ref, odd_ref, sems, *, own, depth):
    moves = [(top_in, top_ref), (bottom_in, bottom_ref), (even_in, even_ref), (odd_in, odd_ref)]
    for copy in fetch(moves, sems):
        copy.wait()
    for k, label in enumerate(halo_labels(even_ref, odd_ref, own)):
        z = depth + k
        top_ref[1, z : z + 1] = label[0:1] + 3.0 * label[1:2]
        bottom_ref[1, z : z + 1] = label[own - 1 :] + 3.0 * label[own - 2 : own - 1]


def collect(diag_ref, off_ref, cols_ref, table_ref, even_ref, odd_ref, tables_ref, column_ref, record_ref, own):
    slots, capacity = table_ref.shape
    cells, nnz = off_ref.shape
    line = lax.broadcasted_iota(jnp.int32, record_ref.shape, 0)
    record = jnp.zeros(record_ref.shape, jnp.float32)
    for cell in range(cells):
        record = jnp.where(line == cell, diag_ref[cell], record)
    record_ref[...] = record
    record_ref[:, :nnz] = off_ref[...]
    record_ref[:, COLS_LANE : COLS_LANE + nnz] = cols_ref[...].astype(jnp.float32)
    swap = lax.axis_index("slab") % 2 == 1
    even = even_ref[own + 8 : own + 8 + slots, :capacity]
    odd = odd_ref[own + 8 : own + 8 + slots, :capacity]

    def flat(table):
        return jnp.concatenate([table[at : at + 1] for at in range(slots)], axis=1)

    tables_ref[...] = jnp.zeros(tables_ref.shape, jnp.int32)
    tables_ref[0:1] = flat(table_ref[...])
    tables_ref[1:2] = flat(jnp.where(swap, odd, even).astype(jnp.int32))
    tables_ref[2:3] = flat(jnp.where(swap, even, odd).astype(jnp.int32))
    column_ref[...] = jnp.transpose(tables_ref[...].astype(jnp.float32)).astype(jnp.int32)


def beside(plane, lane):
    rows, width = plane.shape
    left = jnp.where(lane == 0, 0.0, pltpu.roll(plane, 1, 1))
    right = jnp.where(lane == width - 1, 0.0, pltpu.roll(plane, width - 1, 1))
    return left + right + pltpu.roll(plane, 1, 0) + pltpu.roll(plane, rows - 1, 0)


class Grid:
    def __init__(self, diff_ref, upt_ref, labels, even_ref, odd_ref, top_ref, bottom_ref, conduct_ref, uptake_ref):
        self.conduct_ref, self.uptake_ref = conduct_ref, uptake_ref
        depth = len(labels)
        own, width = labels[0].shape
        planes, rows = conduct_ref.shape[0:2]
        phases = diff_ref.shape[0]
        row = lax.broadcasted_iota(jnp.int32, (rows, width), 0)
        self.lane = lax.broadcasted_iota(jnp.int32, (rows, width), 1)
        slab, tile = lax.axis_index("slab"), lax.axis_index("tile")
        tile_first, tile_last = tile == 0, tile == lax.axis_size("tile") - 1
        slab_first, slab_last = slab == 0, slab == lax.axis_size("slab") - 1
        beyond = (row >= own + 2) & (row < rows - 2)
        beyond = beyond | ((row >= own) & (row < own + 4) & tile_last)
        beyond = beyond | ((row >= own + 4) & tile_first)
        blank = jnp.zeros((8, width), jnp.float32)

        def look(z, label, outside):
            conduct_ref[z, :own] = label
            conduct_ref[z, own:] = blank
            near, far = part_pair(top_ref[1, z : z + 1])
            conduct_ref[z, own : own + 1] = near
            conduct_ref[z, own + 1 : own + 2] = far
            near, far = part_pair(bottom_ref[1, z : z + 1])
            conduct_ref[z, rows - 1 :] = near
            conduct_ref[z, rows - 2 : rows - 1] = far
            label = jnp.where(outside, -1.0, conduct_ref[z])
            conduct = jnp.zeros(label.shape, jnp.float32)
            uptake = jnp.zeros(label.shape, jnp.float32)
            for phase in range(phases):
                conduct = jnp.where(label == float(phase), diff_ref[phase], conduct)
                uptake = jnp.where(label == float(phase), upt_ref[phase], uptake)
            conduct_ref[z] = conduct
            uptake_ref[z] = uptake

        for z, label in enumerate(labels):
            look(z, label, beyond)
        for k, label in enumerate(halo_labels(even_ref, odd_ref, own)):
            look(depth + k, label, beyond | (slab_last if k < 2 else slab_first))

    def around(self, z):
        rows, width = self.conduct_ref.shape[1:]
        planes = self.conduct_ref.shape[0]
        plane = self.conduct_ref[z]
        return (
            jnp.where(self.lane == 0, 0.0, pltpu.roll(plane, 1, 1)),
            jnp.where(self.lane == width - 1, 0.0, pltpu.roll(plane, width - 1, 1)),
            pltpu.roll(plane, 1, 0),
            pltpu.roll(plane, rows - 1, 0),
            self.conduct_ref[(z - 1) % planes],
            self.conduct_ref[(z + 1) % planes],
        )

    def diagonal(self, z, near):
        return self.uptake_ref[z] + 3.0 * self.conduct_ref[z] + 0.5 * sum(near[1:], near[0])


def residual_kernel(*refs):
    operands, outputs, scratch = refs[:13], refs[13:19], refs[19:]
    conduct_ref, uptake_ref, sol_ref = scratch[:3]
    local, sems = scratch[3:16], scratch[16]
    diff_ref, upt_ref, diag_ref, off_ref, cols_ref, table_ref, sol_in, label_in, src_in = local[:9]
    even_ref, odd_ref, top_ref, bottom_ref = local[9:]
    res_ref, plain_ref, packed_ref, tables_ref, column_ref, record_ref = outputs
    for copy in fetch(list(zip(operands, local)), sems):
        copy.wait()
    own, depth, width = sol_in.shape
    planes, rows = conduct_ref.shape[0:2]
    collect(diag_ref, off_ref, cols_ref, table_ref, even_ref, odd_ref, tables_ref, column_ref, record_ref, own)
    labels = []
    for start in range(0, depth, 8):
        block = jnp.transpose(label_in[:, start : start + 8, :].astype(jnp.float32), (1, 0, 2))
        labels = labels + [block[at] for at in range(8)]
    for k in range(depth // 2):
        packed_ref[k] = pack_labels(labels[2 * k], labels[2 * k + 1])
    grid = Grid(diff_ref, upt_ref, labels, even_ref, odd_ref, top_ref, bottom_ref, conduct_ref, uptake_ref)
    lane = grid.lane
    blank = jnp.zeros((8, width), jnp.float32)
    swap = lax.axis_index("slab") % 2 == 1
    even, odd = even_ref[:own], odd_ref[:own]
    sources = []

    def settle(z, value):
        sol_ref[z, :own] = value
        sol_ref[z, own:] = blank
        if z < depth:
            sol_ref[z, own : own + 1] = top_ref[0, z : z + 1]
            sol_ref[z, rows - 1 :] = bottom_ref[0, z : z + 1]
        sol_ref[z] = jnp.where(conduct_ref[z] > 0.0, sol_ref[z], 0.0)

    for start in range(0, depth, 8):
        block = jnp.transpose(sol_in[:, start : start + 8, :], (1, 0, 2))
        for at in range(8):
            plain_ref[start + at] = block[at]
            settle(start + at, block[at])
    settle(depth, jnp.where(swap, odd, even))
    settle(planes - 1, jnp.where(swap, even, odd))
    for start in range(0, depth, 8):
        block = jnp.transpose(src_in[:, start : start + 8, :], (1, 0, 2))
        for at in range(8):
            z = start + at
            above, below = z + 1, (z - 1) % planes
            conduct, value, up, down = conduct_ref[z], sol_ref[z], sol_ref[above], sol_ref[below]
            diagonal = grid.diagonal(z, grid.around(z))
            near = beside(value, lane) + up + down
            flow = beside(conduct * value, lane) + conduct_ref[above] * up + conduct_ref[below] * down
            applied = diagonal * value - 0.5 * (conduct * near + flow)
            res_ref[z] = (block[at] - applied[:own]).astype(jnp.bfloat16)


def weigh_kernel(
    diff_ref, upt_ref, packed_ref, src_in, even_ref, odd_ref, top_ref, bottom_ref, late_even_ref, late_odd_ref,
    weight_ref, conduct_ref, uptake_ref,
):
    own, depth, width = src_in.shape
    planes, rows = conduct_ref.shape[0:2]
    labels = []
    for k in range(depth // 2):
        labels = labels + list(unpack_labels(packed_ref[k], own))
    grid = Grid(diff_ref, upt_ref, labels, even_ref, odd_ref, top_ref, bottom_ref, conduct_ref, uptake_ref)
    blank = jnp.zeros((8, width), jnp.float32)
    swap = lax.axis_index("slab") % 2 == 1
    late = late_even_ref[own:], late_odd_ref[own:]
    outer = {depth: jnp.where(swap, late[1], late[0]), planes - 1: jnp.where(swap, late[0], late[1])}
    for start in (0, 8, planes - 1, depth):
        if start < depth:
            block = jnp.transpose(src_in[:, start : start + 8, :], (1, 0, 2))
            sources = {start + at: block[at] for at in range(8)}
        else:
            sources = {start: outer[start]}
        for z, source in sources.items():
            conduct = conduct_ref[z]
            near = grid.around(z)
            inside = conduct > 0.0
            scale = jnp.where(inside, OMEGA / jnp.where(inside, grid.diagonal(z, near), 1.0), 0.0)
            for k, other in enumerate(near):
                weight_ref[k, z] = jnp.where(other > 0.0, 0.5 * scale * (conduct + other), 0.0)
            weight_ref[6, z, :own] = scale[:own] * source
            weight_ref[6, z, own:] = blank
            if z < depth:
                weight_ref[6, z, own : own + 1] = scale[own : own + 1] * top_ref[2, z : z + 1]
                weight_ref[6, z, rows - 1 :] = scale[rows - 1 :] * bottom_ref[2, z : z + 1]


def owners_of(basis_ref, base):
    tail = basis_ref[:, base:].astype(jnp.float32)
    return [
        (tail[:, 2 * k : 2 * k + 1] + 256.0 * tail[:, 2 * k + 1 : 2 * k + 2]).astype(jnp.int32)
        for k in range(3)
    ]


def restrict_kernel(column_ref, record_ref, res_ref, basis_ref, out_ref):
    depth, own, width = res_ref.shape
    entries = basis_ref.shape[0]
    pick = column_ref[:, 0:1] == lax.broadcasted_iota(jnp.int32, (entries, own), 1)
    pick = jnp.where(pick, 1.0, 0.0).astype(jnp.bfloat16)
    total = jnp.zeros((entries, width), jnp.float32)
    for z in range(depth):
        piece = jnp.dot(pick, res_ref[z], preferred_element_type=jnp.float32)
        total = total + piece * basis_ref[:, z * width : (z + 1) * width].astype(jnp.float32)
    product = jnp.sum(total, axis=1, keepdims=True)
    ident = owners_of(basis_ref, basis_ref.shape[1] - 128)[0]
    copies, lines, lanes = out_ref.shape
    lane = lax.broadcasted_iota(jnp.int32, (entries, lanes), 1)
    line = lax.broadcasted_iota(jnp.int32, (8, lanes), 0)
    for base in range(0, lines, 8):
        block = record_ref[...] if base == 0 else jnp.zeros((8, lanes), jnp.float32)
        for row in range(8):
            share = jnp.where(ident == (base + row) * HALF + lane - HALF, product, 0.0)
            share = jnp.sum(jnp.where(lane >= HALF, share, 0.0), axis=0, keepdims=True)
            block = jnp.where((line == row) & (lane[:8] >= HALF), share, block)

        def put(copy, carry):
            out_ref[copy, base : base + 8, :] = block
            return carry

        lax.fori_loop(0, copies, put, 0, unroll=8)


def solve(got_ref, count, nnz):
    devices, lines, lanes = got_ref.shape
    summed = got_ref[0]
    if devices <= 64:
        for device in range(1, devices):
            summed = summed + got_ref[device]
    else:
        summed = lax.fori_loop(1, devices, lambda d, total: total + got_ref[d], summed)
    rhs = jnp.concatenate([summed[at : at + 1, HALF:] for at in range(count // HALF)], axis=1)
    record = jnp.transpose(got_ref[:, 0:8, :].reshape(count, lanes))
    line = lax.broadcasted_iota(jnp.int32, (COLS_LANE, lanes), 0)
    inverse = 1.0 / record[DIAG_LANE : DIAG_LANE + 1]
    chunks = range(0, count, lanes)
    values = [jnp.where(line < nnz, record[:COLS_LANE, at : at + lanes], 0.0) for at in chunks]
    places = [
        jnp.where(line < nnz, record[COLS_LANE : 2 * COLS_LANE, at : at + lanes], 0.0).astype(jnp.int32)
        for at in chunks
    ]
    state = rhs * inverse
    for repeat in range(COARSE_SWEEPS - 1):
        sources = [jnp.broadcast_to(state[:, at : at + lanes], (COLS_LANE, lanes)) for at in chunks]
        pulled = []
        for value, place in zip(values, places):
            found = jnp.zeros((COLS_LANE, lanes), jnp.float32)
            for k, source in enumerate(sources):
                taken = jnp.take_along_axis(source, place % lanes, axis=1, mode="promise_in_bounds")
                found = jnp.where(place // lanes == k, taken, found)
            pulled.append(jnp.sum(value * found, axis=0, keepdims=True))
        state = (rhs - jnp.concatenate(pulled, axis=1)) * inverse
    return state


def prolong_kernel(
    ids_ref, tables_ref, even_ref, odd_ref, late_even_ref, late_odd_ref, got_ref, basis_ref, plain_ref, cor_ref, top_ref, bottom_ref,
    correction_ref, *, nnz, depth,
):
    planes, own, width = cor_ref.shape
    entries = tables_ref.shape[1]
    cells = ids_ref.shape[0]
    count = cells * got_ref.shape[0]
    state = solve(got_ref, count, nnz)

    line = lax.broadcasted_iota(jnp.int32, (cells, 1), 0)
    mine = jnp.zeros((cells, 1), jnp.int32)
    for cell in range(cells):
        mine = jnp.where(line == cell, ids_ref[cell], mine)

    def look_up(ident):
        hit = ident == lax.broadcasted_iota(jnp.int32, (ident.shape[0], count), 1)
        return jnp.sum(jnp.where(hit, state, 0.0), axis=1, keepdims=True)

    diagonal = line == lax.broadcasted_iota(jnp.int32, (cells, cells), 1)
    correction_ref[...] = jnp.sum(jnp.where(diagonal, look_up(mine), 0.0), axis=0, keepdims=True)
    swap = lax.axis_index("slab") % 2 == 1
    early = even_ref[:own], odd_ref[:own]
    late = late_even_ref[:own], late_odd_ref[:own]
    wide = {
        depth: jnp.where(swap, early[1], early[0]),
        depth + 1: jnp.where(swap, late[1], late[0]),
        depth + 2: jnp.where(swap, late[0], late[1]),
        depth + 3: jnp.where(swap, early[0], early[1]),
    }
    base = depth * width
    owners = owners_of(basis_ref, basis_ref.shape[1] - 128)
    for group, owner in enumerate(owners):
        pick = tables_ref[group : group + 1] == lax.broadcasted_iota(jnp.int32, (own, entries), 0)
        pick = jnp.where(pick, 1.0, 0.0).astype(jnp.bfloat16)
        factor = look_up(owner)
        if group == 0:
            places = [(z, z * width) for z in range(depth)]
        else:
            at = depth + 2 * (group - 1)
            places = [(at + k, base + (at + k - depth) * width) for k in range(2)]
        for z, start in places:
            part = (basis_ref[:, start : start + width].astype(jnp.float32) * factor).astype(jnp.bfloat16)
            added = jnp.dot(pick, part, preferred_element_type=jnp.float32)
            value = (plain_ref[z] if z < depth else wide[z]) + added
            cor_ref[z] = value
            top_ref[z] = value[:2]
            bottom_ref[z] = value[own - 2 :]


def smooth_kernel(cor_ref, top_ref, bottom_ref, weight_ref, out_ref, ext_ref, mid_ref):
    planes, rows, width = ext_ref.shape
    own, depth, unused = out_ref.shape
    blank = jnp.zeros((8, width), jnp.float32)
    for z in range(planes):
        ext_ref[z, :own] = cor_ref[z]
        ext_ref[z, own:] = blank
        ext_ref[z, own : own + 2] = top_ref[z]
        ext_ref[z, rows - 2 :] = bottom_ref[z]

    def sweep(ref, z, upto):
        value = ref[z]
        near = (
            pltpu.roll(value, 1, 1)[:upto],
            pltpu.roll(value, width - 1, 1)[:upto],
            pltpu.roll(value, 1, 0)[:upto],
            pltpu.roll(value, rows - 1, 0)[:upto],
            ref[(z - 1) % planes, :upto],
            ref[(z + 1) % planes, :upto],
        )
        total = (1.0 - OMEGA) * value[:upto] + weight_ref[6, z, :upto]
        for k in range(6):
            total = total + weight_ref[k, z, :upto] * near[k]
        return total

    for z in [planes - 1] + list(range(depth + 1)):
        mid_ref[z] = sweep(ext_ref, z, rows)
    for start in range(0, depth, 8):
        for z in range(start, start + 8):
            ext_ref[z, :own] = sweep(mid_ref, z, own)
        out_ref[:, start : start + 8, :] = jnp.transpose(ext_ref[start : start + 8, :own], (1, 0, 2))


def shards(
    solution,
    source,
    phase_label,
    phase_diffusivity,
    phase_uptake,
    send_tiles,
    support_slot,
    support_len,
    coarse_ids,
    basis_values,
    coarse_diag,
    coarse_off,
    coarse_cols,
):
    f32, i32, bf16 = jnp.float32, jnp.int32, jnp.bfloat16
    rows, depth, width = solution.shape
    voxels = depth * width
    slabs, tiles = lax.axis_size("slab"), lax.axis_size("tile")
    devices = slabs * tiles
    capacity = send_tiles.shape[3]
    cells, support, unused = basis_values.shape
    entries = cells * support
    count = cells * devices
    nnz = coarse_off.shape[1]
    shape = jax.ShapeDtypeStruct
    planes, tall = depth + 4, rows + 8
    block = (rows, depth, width)
    table = send_tiles.reshape(slabs, capacity)
    wide = voxels + 4 * width + 128
    early = shape((rows + 8 + max(8, slabs), width), f32)
    late = shape((2 * rows, width), f32)
    edge = shape((3, -(-planes // 8) * 8, width), f32)
    outgoing, even, odd, late_even, late_odd, top, bottom = pl.pallas_call(
        functools.partial(prepare_kernel, capacity=capacity),
        out_shape=(shape((entries, wide), bf16), early, early, late, late, edge, edge),
        in_specs=[HBM] * 8,
        out_specs=(HBM,) + (VMEM,) * 6,
        scratch_shapes=[
            pltpu.VMEM((1, entries), i32),
            pltpu.SMEM((cells,), i32),
            pltpu.SMEM((cells,), i32),
            pltpu.VMEM((entries, voxels), bf16),
            pltpu.VMEM(block, f32),
            pltpu.VMEM(block, i32),
            pltpu.VMEM(block, f32),
            pltpu.VMEM((slabs, capacity), i32),
            pltpu.VMEM((entries, wide), bf16),
            pltpu.SemaphoreType.DMA((19,)),
        ],
        compiler_params=params(60),
        name="prepare",
    )(
        support_slot.reshape(1, entries),
        support_len.reshape(cells),
        coarse_ids,
        basis_values.reshape(entries, voxels),
        solution,
        phase_label,
        source,
        table,
    )
    even = lax.ppermute(even, "slab", pairs(slabs, False))
    odd = lax.ppermute(odd, "slab", pairs(slabs, True))
    outgoing, even, odd = lax.optimization_barrier((outgoing, even, odd))
    basis = lax.all_to_all(
        outgoing.reshape(slabs, capacity, wide), "slab", split_axis=0, concat_axis=0, tiled=True
    ).reshape(entries, wide)

    late_even, late_odd, outgoing = lax.optimization_barrier((late_even, late_odd, outgoing))
    top, bottom = pl.pallas_call(
        functools.partial(edge_kernel, own=rows, depth=depth),
        out_shape=(edge, edge),
        in_specs=[HBM] * 4,
        out_specs=(VMEM,) * 2,
        scratch_shapes=[
            pltpu.VMEM(early.shape, f32),
            pltpu.VMEM(early.shape, f32),
            pltpu.SemaphoreType.DMA((4,)),
        ],
        compiler_params=params(8),
        name="edge",
    )(*[pltpu.with_memory_space_constraint(array, pltpu.HBM) for array in (top, bottom)], even, odd)
    top = lax.ppermute(top, "tile", wheel(tiles, -1))
    bottom = lax.ppermute(bottom, "tile", wheel(tiles, 1))
    row_top, row_bottom = top, bottom
    late_even = lax.ppermute(late_even, "slab", pairs(slabs, False))
    late_odd = lax.ppermute(late_odd, "slab", pairs(slabs, True))

    wide_block = pltpu.VMEM((planes, tall, width), f32)
    operands = [
        phase_diffusivity, phase_uptake, coarse_diag, coarse_off, coarse_cols, table,
        solution, phase_label, source, even, odd, top, bottom,
    ]
    residual, plain, packed, tables, column, record = pl.pallas_call(
        residual_kernel,
        out_shape=(
            shape((depth, rows, width), bf16),
            shape((depth, rows, width), f32),
            shape((depth // 2, 8, width), f32),
            shape((8, entries), i32),
            shape((entries, 8), i32),
            shape((cells, 128), f32),
        ),
        in_specs=[HBM] * 13,
        out_specs=(VMEM,) * 6,
        scratch_shapes=[wide_block] * 3
        + [pltpu.SMEM(array.shape, array.dtype) for array in operands[:3]]
        + [pltpu.VMEM(array.shape, array.dtype) for array in operands[3:]]
        + [pltpu.SemaphoreType.DMA((13,))],
        compiler_params=params(12),
        name="residual",
    )(*[pltpu.with_memory_space_constraint(array, pltpu.HBM) for array in operands[:9]], *operands[9:])

    basis, late_even, late_odd = lax.optimization_barrier((basis, late_even, late_odd))
    lines = max(8, count // HALF)
    payload = pl.pallas_call(
        restrict_kernel,
        out_shape=shape((devices, lines, 128), f32),
        in_specs=[VMEM, VMEM, VMEM, VMEM],
        out_specs=VMEM,
        compiler_params=params(8),
        name="restrict",
    )(column, record, residual, basis)
    got = lax.all_to_all(payload, ("slab", "tile"), split_axis=0, concat_axis=0, tiled=True)

    edge = shape((planes, 2, width), f32)
    corrected, top, bottom, coarse_correction = pl.pallas_call(
        functools.partial(prolong_kernel, nnz=nnz, depth=depth),
        out_shape=(shape((planes, rows, width), f32), edge, edge, shape((1, cells), f32)),
        in_specs=[SMEM] + [VMEM] * 8,
        out_specs=(VMEM, VMEM, VMEM, VMEM),
        compiler_params=params(12 + count * count // (8 * MIB)),
        name="prolong",
    )(coarse_ids, tables, even, odd, late_even, late_odd, got, basis, plain)
    corrected, packed = lax.optimization_barrier((corrected, packed))
    weights = pl.pallas_call(
        weigh_kernel,
        out_shape=shape((7, planes, tall, width), f32),
        in_specs=[SMEM, SMEM] + [VMEM] * 8,
        out_specs=VMEM,
        scratch_shapes=[wide_block] * 2,
        compiler_params=params(12),
        name="weigh",
    )(phase_diffusivity, phase_uptake, packed, source, even, odd, row_top, row_bottom, late_even, late_odd)
    top = lax.ppermute(top, "tile", wheel(tiles, -1))
    bottom = lax.ppermute(bottom, "tile", wheel(tiles, 1))
    smooth = pl.pallas_call(
        smooth_kernel,
        out_shape=shape((rows, depth, width), f32),
        in_specs=[VMEM] * 4,
        out_specs=VMEM,
        scratch_shapes=[wide_block] * 2,
        compiler_params=params(16),
        name="smooth",
    )(corrected, top, bottom, weights)
    return smooth, coarse_correction.reshape(cells)


def solution(mesh):
    placed = (
        P("tile", "slab", None),
        P("tile", "slab", None),
        P("tile", "slab", None),
        P(),
        P(),
        P("slab", "tile", None, None),
        P("slab", "tile", None),
        P("slab", "tile", None),
        P(("slab", "tile")),
        P(("slab", "tile"), None, None),
        P(("slab", "tile")),
        P(("slab", "tile"), None),
        P(("slab", "tile"), None),
    )
    return jax.shard_map(
        shards,
        mesh=mesh,
        in_specs=placed,
        out_specs=(P("tile", "slab", None), P(("slab", "tile"))),
        check_vma=False,
    )
```

time: 341 us -> 56.5 us (0.17)
  blocking collectives: 198 us -> 11.7 us
  starting transfers between devices: 52.5 us -> 18.7 us
  other arithmetic: 29.7 us -> 0 us
  waiting for transfers between devices: 34.6 us -> 10.2 us
  local copies, waits for them, and re-layouts: 19.8 us -> 0.02 us
  Pallas kernels: 0 us -> 14.4 us
    unnamed x5 -> x0, blocking collectives: 198 us -> none
    ppermute x16 -> x8, starting transfers between devices: 39.5 us -> 9.02 us  [the longest x1 3 us: shards(): even = lax.ppermute(even, 'slab', pairs(slabs, False))]
    all_to_all x2 -> x1, waiting for transfers between devices: 23.7 us -> 7.94 us  [shards(): lax.all_to_all(outgoing.reshape(slabs, capacity, wide), 'slab', split_axi...]
    pallas_call x0 -> x7, Pallas kernels: none -> 14.4 us  [the longest x1 3.32 us: shards(): pl.pallas_call(functools.partial(prepare_kernel, capacity=capacity), out_...]
    gather x9 -> x0, local copies, waits for them, and re-layouts: 12.4 us -> none  [the longest x6 7.56 us: shards(): gathered[coarse_cols]]
    all_to_all x0 -> x1, blocking collectives: none -> 11.7 us  [shards(): lax.all_to_all(payload, ('slab', 'tile'), split_axis=0, concat_axis=0, ti...]
    add x3 -> x0, other arithmetic: 11.1 us -> none  [the longest x2 6.87 us: shards(): corrected + OMEGA * (source - operate(corrected, weights, diagonal)) / di...]
    ppermute x16 -> x8, waiting for transfers between devices: 10.9 us -> 2.24 us  [the longest x2 1.4 us: shards(): bottom = lax.ppermute(bottom, 'tile', wheel(tiles, 1))]
  transfers between devices with their start and end apart: 18 -> 9, of which waited for: 9 -> 4; matrix products, arithmetic and copies ran while one was open for 2% -> 0% of each run, Pallas kernels for 0% -> 12%
where the time goes in v2:
time: 56.5 us; the launch traced here: 55.8 us
  starting transfers between devices  18.7 us (33%)
  Pallas kernels  14.4 us (25%)
  blocking collectives  11.7 us (21%)
  waiting for transfers between devices  10.2 us (18%)
  between operations  0.74 us (1%)
    all_to_all x1, blocking collectives, shards(): lax.all_to_all(payload, ('slab', 'tile'), split_axis=0, concat_axis=0, ti...  11.7 us
    all_to_all x1, starting transfers between devices, shards(): lax.all_to_all(outgoing.reshape(slabs, capacity, wide), 'slab', split_axi...  9.67 us
    all_to_all x1, waiting for transfers between devices, shards(): lax.all_to_all(outgoing.reshape(slabs, capacity, wide), 'slab', split_axi...  7.94 us
    pallas_call x1, Pallas kernels, shards(): pl.pallas_call(functools.partial(prepare_kernel, capacity=capacity), out_...  3.32 us
    pallas_call x1, Pallas kernels, shards(): pl.pallas_call(residual_kernel, out_shape=(shape((depth, rows, width), bf...  3.28 us
    ppermute x1, starting transfers between devices, shards(): even = lax.ppermute(even, 'slab', pairs(slabs, False))  3 us
    pallas_call x1, Pallas kernels, shards(): pl.pallas_call(weigh_kernel, out_shape=shape((7, planes, tall, width), f3...  2.47 us
    pallas_call x1, Pallas kernels, shards(): pl.pallas_call(smooth_kernel, out_shape=shape((rows, depth, width), f32),...  2.12 us
  transfers between devices with their start and end apart: 9, of which 4 were waited for; matrix products, arithmetic and copies ran while one was open for 0% of the time, Pallas kernels for 12%

profile of v2, /device:TPU:0, one launch (start us, length us, event | category | flops | bytes accessed | tf_op | source)
XLA Modules:
  0.0 55.8 jit_solution(11513203009519372826)
XLA Ops:
  0.6 0.0 copy-start
  0.6 0.0 copy-start.1
  0.7 0.0 copy-start.3
  0.7 0.0 copy-start.2
  0.7 3.3 %prepare.1 = (bf16[64,5248]{1,0:T(8,128)(2,1)}, f32[48,256]{1,0:T(8,128)}, f32[48,256]{1,0:T(8,128)}, f32[64,256]{1,0:T(8,128)}, f32[64,256]{1,0:T(8,128)}, /*in...) custom-call(s32[1,64]{1,0:T(1,128)} %bitcast.13, s32[8]{0:T(128)} %bitcast.14, s32[8]{0:T(128)} %ids_ref.1, ...), custom_call_target="tpu_custom_call" | custom-call | tf_op jit(solution)/shard_map/prepare/pallas_call | solution.py:548
  4.0 3.0 %collective-permute-start = (f32[48,256]{1,0:T(8,128)}, f32[48,256]{1,0:T(8,128)S(1)}, u32[]{:S(2)}, u32[]{:S(2)}) collective-permute-start(f32[48,256]{1,0:T(8,128)} %get-tuple-element.32), channel_id=1, source_target_pairs={{0,4},{4,0},{8,12},{12,8},{16,20},{20,16},{24,28},{28,24},{1,5},{5... | collective-permute-start | bytes 147464 | tf_op jit(solution)/shard_map/ppermute | solution.py:577
  7.0 1.4 %collective-permute-start.1 = (f32[48,256]{1,0:T(8,128)}, f32[48,256]{1,0:T(8,128)S(1)}, u32[]{:S(2)}, u32[]{:S(2)}) collective-permute-start(f32[48,256]{1,0:T(8,128)} %get-tuple-element.33), channel_id=1, source_target_pairs={{0,0},{4,8},{8,4},{12,16},{16,12},{20,24},{24,20},{28,28},{1,1},{5... | collective-permute-start | bytes 147464 | tf_op jit(solution)/shard_map/ppermute | solution.py:578
  8.5 0.8 %collective-permute-done.even_in.refs_9_.even_ref = f32[48,256]{1,0:T(8,128)S(1)} collective-permute-done((f32[48,256]{1,0:T(8,128)}, f32[48,256]{1,0:T(8,128)S(1)}, u32[]{:S(2)}, u32[]{:S(2)}) %collective-permute-start) | collective-permute-done | bytes 49184 | tf_op jit(solution)/shard_map/ppermute | solution.py:577
  9.3 0.0 collective-permute-done.1.odd_in.refs_10_.odd_ref
  9.3 9.7 %all-to-all-start = ((bf16[8,8,5248]{2,1,0:T(8,128)(2,1)}), bf16[8,8,5248]{2,1,0:T(8,128)(2,1)S(1)}, u32[]{:S(2)}, u32[]{:S(2)}) async-start(bf16[8,8,5248]{2,1,0:T(8,128)(2,1)} %bitcast.9), calls=%async_computation | async-start | bytes 1343488 | tf_op jit(solution)/shard_map/all_to_all | solution.py:580
  19.0 1.0 %edge.1 = (f32[3,24,256]{2,1,0:T(8,128)S(1)}, f32[3,24,256]{2,1,0:T(8,128)S(1)}) custom-call(f32[3,24,256]{2,1,0:T(8,128)} %get-tuple-element.36.top_in, f32[3,24,256]{2,1,0:T(8,128)} %get-tuple-element.37.bottom_in, f32[48,256]{1,0:T(8,128)S(1)} %collective-permute-done.even_in.refs_9_.even_ref, f32[48,256]{1,0:T(8,128)S(1)} %collective-permute-done.1.odd_in.refs_10_.odd_ref), custom_call_target="tpu_custom_call" | custom-call | tf_op jit(solution)/shard_map/edge/pallas_call | solution.py:585
  20.0 0.1 collective-permute-start.2
  20.0 0.5 collective-permute-start.3
  20.5 2.0 %collective-permute-start.4 = (f32[64,256]{1,0:T(8,128)}, f32[64,256]{1,0:T(8,128)S(1)}, u32[]{:S(2)}, u32[]{:S(2)}) collective-permute-start(f32[64,256]{1,0:T(8,128)} %get-tuple-element.44), channel_id=1, source_target_pairs={{0,4},{4,0},{8,12},{12,8},{16,20},{20,16},{24,28},{28,24},{1,5},{5... | collective-permute-start | bytes 196616 | tf_op jit(solution)/shard_map/ppermute | solution.py:601
  22.6 1.5 %collective-permute-start.5 = (f32[64,256]{1,0:T(8,128)}, f32[64,256]{1,0:T(8,128)S(1)}, u32[]{:S(2)}, u32[]{:S(2)}) collective-permute-start(f32[64,256]{1,0:T(8,128)} %get-tuple-element.45), channel_id=1, source_target_pairs={{0,0},{4,8},{8,4},{12,16},{16,12},{20,24},{24,20},{28,28},{1,1},{5... | collective-permute-start | bytes 196616 | tf_op jit(solution)/shard_map/ppermute | solution.py:602
  24.0 0.0 collective-permute-done.2.refs_11_.top_ref
  24.0 0.6 %collective-permute-done.3.refs_12_.bottom_ref = f32[3,24,256]{2,1,0:T(8,128)S(1)} collective-permute-done((f32[3,24,256]{2,1,0:T(8,128)S(1)}, f32[3,24,256]{2,1,0:T(8,128)S(1)}, u32[]{:S(2)}, u32[]{:S(2)}) %collective-permute-start.3) | collective-permute-done | bytes 73760 | tf_op jit(solution)/shard_map/ppermute | solution.py:599
  24.6 3.3 %residual.1 = (bf16[16,32,256]{2,1,0:T(8,128)(2,1)S(1)}, f32[16,32,256]{2,1,0:T(8,128)S(1)}, f32[8,8,256]{2,1,0:T(8,128)S(1)}, s32[8,64]{1,0:T(8,128)S(1)}, s32[64,8]{1,0:T(8,128)S(1)}, /*index=5*/f32[8,128]{1,0:T(8,128)S(1)}) custom-call(f32[3]{0:T(128)} %diff_ref.1, f32[3]{0:T(128)} %upt_ref.1, f32[8]{0:T(128)} %refs_2_.1, f32[8,26]{1,0:T(8,128)} %refs_3_.1, ...), custom_call_target="tpu_custom_call" | custom-call | tf_op jit(solution)/shard_map/residual/pallas_call | solution.py:609
  27.9 0.0 collective-permute-done.4.late_even_ref
  27.9 0.0 collective-permute-done.5.late_odd_ref
  28.0 7.9 %all-to-all-done = bf16[8,8,5248]{2,1,0:T(8,128)(2,1)S(1)} async-done(((bf16[8,8,5248]{2,1,0:T(8,128)(2,1)}), bf16[8,8,5248]{2,1,0:T(8,128)(2,1)S(1)}, u32[]{:S(2)}, u32[]{:S(2)}) %all-to-all-start) | async-done | bytes 671776 | tf_op jit(solution)/shard_map/all_to_all | solution.py:580
  35.9 0.5 restrict.1
  36.4 11.7 %all_to_all.10.got_ref = f32[32,8,128]{2,1,0:T(8,128)S(1)} all-to-all(f32[32,8,128]{2,1,0:T(8,128)S(1)} %restrict.1), channel_id=1, replica_groups=mesh['slab'=8,'tile'=4] {'slab','tile'}, dimensions={0} | all-to-all | bytes 262144 | tf_op jit(solution)/shard_map/all_to_all | solution.py:639
  48.1 0.0 copy-done.1
  48.1 1.8 %prolong.1 = (f32[20,32,256]{2,1,0:T(8,128)S(1)}, f32[20,2,256]{2,1,0:T(2,128)S(1)}, f32[20,2,256]{2,1,0:T(2,128)S(1)}, f32[1,8]{1,0:T(1,128)}) custom-call(s32[8]{0:T(128)S(1)} %copy-done.1, s32[8,64]{1,0:T(8,128)S(1)} %get-tuple-element.40.tables_ref, f32[48,256]{1,0:T(8,128)S(1)} %collective-permute-done.even_in.refs_9_.even_ref, ...), custom_call_target="tpu_custom_call" | custom-call | tf_op jit(solution)/shard_map/prolong/pallas_call | solution.py:642
  49.9 0.2 collective-permute-start.6
  50.0 0.3 collective-permute-start.7
  50.4 0.0 copy-done
  50.4 2.5 %weigh.1.weight_ref = f32[7,20,40,256]{3,2,1,0:T(8,128)S(1)} custom-call(f32[3]{0:T(128)S(1)} %copy-done.2, f32[3]{0:T(128)S(1)} %copy-done.3, f32[8,8,256]{2,1,0:T(8,128)S(1)} %get-tuple-element.58.packed_ref, f32[32,16,256]{2,1,0:T(8,128)S(1)} %copy-done, f32[48,256]{1,0:T(8,128)S(1)} %collective-permute-done.even_in.refs_9_.even_ref, ...), custom_call_target="tpu_custom_call" | custom-call | tf_op jit(solution)/shard_map/weigh/pallas_call | solution.py:651
  52.9 0.0 collective-permute-done.6.top_ref
  52.9 0.8 %collective-permute-done.7.bottom_ref = f32[20,2,256]{2,1,0:T(2,128)S(1)} collective-permute-done((f32[20,2,256]{2,1,0:T(2,128)S(1)}, f32[20,2,256]{2,1,0:T(2,128)S(1)}, u32[]{:S(2)}, u32[]{:S(2)}) %collective-permute-start.7) | collective-permute-done | bytes 40992 | tf_op jit(solution)/shard_map/ppermute | solution.py:661
  53.7 2.1 %smooth.1 = f32[32,16,256]{2,1,0:T(8,128)} custom-call(f32[20,32,256]{2,1,0:T(8,128)S(1)} %get-tuple-element.55.cor_ref, f32[20,2,256]{2,1,0:T(2,128)S(1)} %collective-permute-done.6.top_ref, f32[20,2,256]{2,1,0:T(2,128)S(1)} %collective-permute-done.7.bottom_ref, f32[7,20,40,256]{3,2,1,0:T(8,128)S(1)} %weigh.1.weight_ref), custom_call_target="tpu_custom_call" | custom-call | tf_op jit(solution)/shard_map/smooth/pallas_call | solution.py:662
  (2 shorter events, 0.0 us)
Async XLA Ops:
  0.6 49.8 %copy-start = (f32[32,16,256]{2,1,0:T(8,128)S(1)}, f32[32,16,256]{2,1,0:T(8,128)}, u32[]{:S(2)}) copy-start(f32[32,16,256]{2,1,0:T(8,128)} %src_in.1) | copy-start | bytes 1572868
  0.6 47.5 %copy-start.1 = (s32[8]{0:T(128)S(1)}, s32[8]{0:T(128)}, u32[]{:S(2)}) copy-start(s32[8]{0:T(128)} %ids_ref.1) | copy-start | bytes 100
  0.7 49.7 %copy-start.3 = (f32[3]{0:T(128)S(1)}, f32[3]{0:T(128)}, u32[]{:S(2)}) copy-start(f32[3]{0:T(128)} %upt_ref.1) | copy-start | bytes 40
  0.7 49.7 %copy-start.2 = (f32[3]{0:T(128)S(1)}, f32[3]{0:T(128)}, u32[]{:S(2)}) copy-start(f32[3]{0:T(128)} %diff_ref.1) | copy-start | bytes 40
  4.0 5.3 %collective-permute-start = (f32[48,256]{1,0:T(8,128)}, f32[48,256]{1,0:T(8,128)S(1)}, u32[]{:S(2)}, u32[]{:S(2)}) collective-permute-start(f32[48,256]{1,0:T(8,128)} %get-tuple-element.32), channel_id=1, source_target_pairs={{0,4},{4,0},{8,12},{12,8},{16,20},{20,16},{24,28},{28,24},{1,5},{5... | collective-permute-start | bytes 147464 | tf_op jit(solution)/shard_map/ppermute | solution.py:577
  7.0 2.3 %collective-permute-start.1 = (f32[48,256]{1,0:T(8,128)}, f32[48,256]{1,0:T(8,128)S(1)}, u32[]{:S(2)}, u32[]{:S(2)}) collective-permute-start(f32[48,256]{1,0:T(8,128)} %get-tuple-element.33), channel_id=1, source_target_pairs={{0,0},{4,8},{8,4},{12,16},{16,12},{20,24},{24,20},{28,28},{1,1},{5... | collective-permute-start | bytes 147464 | tf_op jit(solution)/shard_map/ppermute | solution.py:578
  9.3 26.6 %all-to-all-start = ((bf16[8,8,5248]{2,1,0:T(8,128)(2,1)}), bf16[8,8,5248]{2,1,0:T(8,128)(2,1)S(1)}, u32[]{:S(2)}, u32[]{:S(2)}) async-start(bf16[8,8,5248]{2,1,0:T(8,128)(2,1)} %bitcast.9), calls=%async_computation | async-start | bytes 1343488 | tf_op jit(solution)/shard_map/all_to_all | solution.py:580
  20.0 4.1 %collective-permute-start.2 = (f32[3,24,256]{2,1,0:T(8,128)S(1)}, f32[3,24,256]{2,1,0:T(8,128)S(1)}, u32[]{:S(2)}, u32[]{:S(2)}) collective-permute-start(f32[3,24,256]{2,1,0:T(8,128)S(1)} %get-tuple-element.38), channel_id=1, source_target_pairs={{0,3},{1,0},{2,1},{3,2},{4,7},{5,4},{6,5},{7,6},{8,11},{9,8},{10,9... | collective-permute-start | bytes 221192 | tf_op jit(solution)/shard_map/ppermute | solution.py:598
  20.0 4.6 %collective-permute-start.3 = (f32[3,24,256]{2,1,0:T(8,128)S(1)}, f32[3,24,256]{2,1,0:T(8,128)S(1)}, u32[]{:S(2)}, u32[]{:S(2)}) collective-permute-start(f32[3,24,256]{2,1,0:T(8,128)S(1)} %get-tuple-element.39), channel_id=1, source_target_pairs={{0,1},{1,2},{2,3},{3,0},{4,5},{5,6},{6,7},{7,4},{8,9},{9,10},{10,1... | collective-permute-start | bytes 221192 | tf_op jit(solution)/shard_map/ppermute | solution.py:599
  20.5 7.4 %collective-permute-start.4 = (f32[64,256]{1,0:T(8,128)}, f32[64,256]{1,0:T(8,128)S(1)}, u32[]{:S(2)}, u32[]{:S(2)}) collective-permute-start(f32[64,256]{1,0:T(8,128)} %get-tuple-element.44), channel_id=1, source_target_pairs={{0,4},{4,0},{8,12},{12,8},{16,20},{20,16},{24,28},{28,24},{1,5},{5... | collective-permute-start | bytes 196616 | tf_op jit(solution)/shard_map/ppermute | solution.py:601
  22.6 5.4 %collective-permute-start.5 = (f32[64,256]{1,0:T(8,128)}, f32[64,256]{1,0:T(8,128)S(1)}, u32[]{:S(2)}, u32[]{:S(2)}) collective-permute-start(f32[64,256]{1,0:T(8,128)} %get-tuple-element.45), channel_id=1, source_target_pairs={{0,0},{4,8},{8,4},{12,16},{16,12},{20,24},{24,20},{28,28},{1,1},{5... | collective-permute-start | bytes 196616 | tf_op jit(solution)/shard_map/ppermute | solution.py:602
  49.9 3.0 %collective-permute-start.6 = (f32[20,2,256]{2,1,0:T(2,128)S(1)}, f32[20,2,256]{2,1,0:T(2,128)S(1)}, u32[]{:S(2)}, u32[]{:S(2)}) collective-permute-start(f32[20,2,256]{2,1,0:T(2,128)S(1)} %get-tuple-element.56), channel_id=1, source_target_pairs={{0,3},{1,0},{2,1},{3,2},{4,7},{5,4},{6,5},{7,6},{8,11},{9,8},{10,9... | collective-permute-start | bytes 122888 | tf_op jit(solution)/shard_map/ppermute | solution.py:660
  50.0 3.6 %collective-permute-start.7 = (f32[20,2,256]{2,1,0:T(2,128)S(1)}, f32[20,2,256]{2,1,0:T(2,128)S(1)}, u32[]{:S(2)}, u32[]{:S(2)}) collective-permute-start(f32[20,2,256]{2,1,0:T(2,128)S(1)} %get-tuple-element.57), channel_id=1, source_target_pairs={{0,1},{1,2},{2,3},{3,0},{4,5},{5,6},{6,7},{7,4},{8,9},{9,10},{10,1... | collective-permute-start | bytes 122888 | tf_op jit(solution)/shard_map/ppermute | solution.py:661

commit v3 on v2

v3 whole, which is shorter than its diff:
```python
import functools

import jax
import jax.numpy as jnp
from jax import lax
from jax.experimental import pallas as pl
from jax.experimental.pallas import tpu as pltpu
from jax.sharding import PartitionSpec as P

COARSE_SWEEPS = 4
SMOOTH_SWEEPS = 2
OMEGA = 0.8

VMEM = pl.BlockSpec(memory_space=pltpu.VMEM)
SMEM = pl.BlockSpec(memory_space=pltpu.SMEM)
HBM = pl.BlockSpec(memory_space=pltpu.HBM)
MIB = 1024 * 1024
COLS_LANE = 32
HALF = 64
DIAG_LANE = 60


def params(mib=16):
    return pltpu.CompilerParams(vmem_limit_bytes=mib * MIB)


def wheel(count, step):
    return [(i, (i + step) % count) for i in range(count)]


def pairs(count, odd):
    start = 1 if odd else 0
    table = list(range(count))
    for i in range(start, count - 1, 2):
        table[i], table[i + 1] = i + 1, i
    return list(enumerate(table))


def fetch(pairs_of_refs, sems):
    copies = [
        pltpu.make_async_copy(source, target, sems.at[k])
        for k, (source, target) in enumerate(pairs_of_refs)
    ]
    for copy in copies:
        copy.start()
    return copies


def sort_kernel(
    slot_hbm, len_hbm, ids_hbm, basis_hbm, out_hbm, slot_ref, len_ref, ids_ref, basis_ref, out_ref, sems, *, capacity
):
    entries, voxels = basis_ref.shape
    cells = len_ref.shape[0]
    support = entries // cells
    border = (out_ref.shape[1] - 128 - voxels) // 2
    chunk = voxels // 4
    pieces = [
        (basis_hbm.at[:, pl.ds(k * chunk, chunk)], basis_ref.at[:, pl.ds(k * chunk, chunk)]) for k in range(4)
    ]
    small = [(slot_hbm, slot_ref), (len_hbm, len_ref), (ids_hbm, ids_ref)]
    copies = fetch(small + pieces, sems)
    for copy in copies[:3]:
        copy.wait()
    lane = lax.broadcasted_iota(jnp.int32, (1, entries), 1)
    length = jnp.zeros((1, entries), jnp.int32)
    ident = jnp.zeros((1, entries), jnp.int32)
    for cell in range(cells):
        here = lane // support == cell
        length = jnp.where(here, len_ref[cell], length)
        ident = jnp.where(here, ids_ref[cell], ident)
    live = lane % support < length
    slot = jnp.where(live, slot_ref[...], -1)
    row = lax.broadcasted_iota(jnp.int32, (entries, entries), 0)
    above = jnp.where(row >= entries - capacity, row + capacity - entries, row + capacity)
    below = jnp.where(row < capacity, row - capacity + entries, row - capacity)
    hits = [slot == row, slot == above, slot == below]
    picks = [jnp.where(hit, 1.0, 0.0).astype(jnp.bfloat16) for hit in hits]
    sent = []

    def move(pick, start, size, target):
        out_ref[:, target : target + size] = jnp.dot(
            pick, basis_ref[:, start : start + size], preferred_element_type=jnp.float32
        ).astype(jnp.bfloat16)

    def send(start, size):
        part = pl.ds(start, size)
        copy = pltpu.make_async_copy(out_ref.at[:, part], out_hbm.at[:, part], sems.at[len(copies) + len(sent)])
        copy.start()
        sent.append(copy)

    extra = lax.broadcasted_iota(jnp.int32, (entries, 128), 1)
    tail = jnp.zeros((entries, 128), jnp.float32)
    for k, hit in enumerate(hits):
        low = jnp.sum(jnp.where(hit, ident % 256, 0).astype(jnp.float32), axis=1, keepdims=True)
        high = jnp.sum(jnp.where(hit, ident // 256, 0).astype(jnp.float32), axis=1, keepdims=True)
        tail = jnp.where(extra == 2 * k, low, jnp.where(extra == 2 * k + 1, high, tail))
    out_ref[:, voxels + 2 * border :] = tail.astype(jnp.bfloat16)
    for k in range(4):
        copies[3 + k].wait()
        for start in range(k * chunk, (k + 1) * chunk, 512):
            move(picks[0], start, 512, start)
        send(k * chunk, chunk)
        if k == 0:
            move(picks[1], 0, border, voxels)
    move(picks[2], voxels - border, border, voxels + border)
    send(voxels, 2 * border + 128)
    for copy in sent:
        copy.wait()


LOW, FAR, SOURCE, LABELS, CORNERS, TABLE = 32, 64, 96, 128, 144, 148
MESSAGE = 160


def border_kernel(
    sol_hbm, label_hbm, src_hbm, table_hbm, even_ref, odd_ref, top_ref, bottom_ref,
    sol_ref, label_ref, src_ref, table_ref, sems,
):
    rows, depth, width = sol_ref.shape
    blocks = ((sol_hbm, sol_ref), (label_hbm, label_ref), (src_hbm, src_ref), (table_hbm, table_ref))
    for copy in fetch(blocks, sems):
        copy.wait()
    odd = lax.axis_index("slab") % 2 == 1

    def planes(start):
        parts = [ref[:, start : start + 2, :].astype(jnp.float32) for ref in (sol_ref, label_ref, src_ref, src_ref)]
        block = jnp.transpose(jnp.concatenate(parts, axis=1), (1, 0, 2))
        return [block[k] for k in range(6)]

    near, far, label, label_far, origin, unused = planes(0)
    down = near, far, origin, pack_labels(label, label_far, 16)
    far, near, label_far, label, unused, origin = planes(depth - 2)
    up = near, far, origin, pack_labels(label, label_far, 16)
    table = flat(table_ref[...]).astype(jnp.float32)
    entries = table.shape[1]
    table = jnp.concatenate([table, jnp.zeros((1, width - entries), jnp.float32)], axis=1)
    line = lax.broadcasted_iota(jnp.int32, (16, width), 0) + CORNERS
    table = jnp.where(line == TABLE, table, 0.0)
    for first, second, ref in ((up, down, even_ref), (down, up, odd_ref)):
        near, far, origin, labels = [jnp.where(odd, b, a) for a, b in zip(first, second)]
        high = near.astype(jnp.bfloat16)
        ref[:LOW] = high
        ref[LOW:FAR] = (near - high.astype(jnp.float32)).astype(jnp.bfloat16)
        ref[FAR:SOURCE] = far.astype(jnp.bfloat16)
        ref[SOURCE:LABELS] = origin.astype(jnp.bfloat16)
        ref[LABELS:CORNERS] = labels.astype(jnp.bfloat16)
        ref[CORNERS:] = table.astype(jnp.bfloat16)
    for ref, near, far in ((top_ref, 0, 1), (bottom_ref, rows - 1, rows - 2)):
        ref[0] = sol_ref[near]
        ref[1] = (label_ref[near] + 3 * label_ref[far]).astype(jnp.float32)
        ref[2] = src_ref[near]


def flat(table):
    return jnp.concatenate([table[at : at + 1] for at in range(table.shape[0])], axis=1)


def pack_labels(near, far, lines):
    pair = near + 3.0 * far
    packed = pair[0:lines]
    for k in range(1, pair.shape[0] // lines):
        packed = packed + float(9**k) * pair[lines * k : lines * (k + 1)]
    return packed


def unpack_labels(packed, rows):
    found = []
    for k in range(rows // packed.shape[0]):
        rest = jnp.floor((packed + 0.5) * (1.0 / 9.0))
        found.append(packed - 9.0 * rest)
        packed = rest
    return part_pair(jnp.concatenate(found, axis=0))


def part_pair(pair):
    far = jnp.floor((pair + 0.5) * (1.0 / 3.0))
    return pair - 3.0 * far, far


def from_slab(even_ref, odd_ref, start, stop):
    swap = lax.axis_index("slab") % 2 == 1
    even, odd = even_ref[start:stop].astype(jnp.float32), odd_ref[start:stop].astype(jnp.float32)
    return jnp.where(swap, odd, even), jnp.where(swap, even, odd)


def nearest_planes(even_ref, odd_ref):
    upper, lower = from_slab(even_ref, odd_ref, 0, LOW), from_slab(even_ref, odd_ref, LOW, FAR)
    return upper[0] + lower[0], upper[1] + lower[1]


def corner_kernel(even_in, odd_in, top_in, bottom_in, even_ref, odd_ref, top_ref, bottom_ref, sems):
    for copy in fetch([(even_in, even_ref), (odd_in, odd_ref), (top_in, top_ref), (bottom_in, bottom_ref)], sems):
        copy.wait()
    depth, width = top_ref.shape[1:]
    odd = lax.axis_index("slab") % 2 == 1
    line = lax.broadcasted_iota(jnp.int32, (16, width), 0)
    for ref, upward in ((even_ref, jnp.logical_not(odd)), (odd_ref, odd)):
        block = ref[CORNERS:].astype(jnp.float32)
        for k in range(4):
            edge_ref, low = (top_ref, bottom_ref)[k // 2], k % 2
            high = depth - 1 - low
            pair = jnp.where(upward, edge_ref[1, high : high + 1], edge_ref[1, low : low + 1])
            block = jnp.where(line == k, pair, block)
        ref[CORNERS:] = block.astype(jnp.bfloat16)


def beside(plane, lane):
    rows, width = plane.shape
    left = jnp.where(lane == 0, 0.0, pltpu.roll(plane, 1, 1))
    right = jnp.where(lane == width - 1, 0.0, pltpu.roll(plane, width - 1, 1))
    return left + right + pltpu.roll(plane, 1, 0) + pltpu.roll(plane, rows - 1, 0)


class Grid:
    def __init__(self, diff_ref, upt_ref, labels, top_pairs, bottom_pairs, outside, conduct_ref, uptake_ref):
        self.conduct_ref, self.uptake_ref = conduct_ref, uptake_ref
        self.planes, rows, width = conduct_ref.shape
        own = labels[0].shape[0]
        phases = diff_ref.shape[0]
        row = lax.broadcasted_iota(jnp.int32, (rows, width), 0)
        self.lane = lax.broadcasted_iota(jnp.int32, (rows, width), 1)
        tile = lax.axis_index("tile")
        beyond = (row >= own + 2) & (row < rows - 2)
        beyond = beyond | ((row >= own) & (row < own + 4) & (tile == lax.axis_size("tile") - 1))
        beyond = beyond | ((row >= own + 4) & (tile == 0))
        blank = jnp.zeros((8, width), jnp.float32)
        for z, (label, top, bottom) in enumerate(zip(labels, top_pairs, bottom_pairs)):
            conduct_ref[z, :own] = label
            conduct_ref[z, own:] = blank
            near, far = part_pair(top)
            conduct_ref[z, own : own + 1] = near
            conduct_ref[z, own + 1 : own + 2] = far
            near, far = part_pair(bottom)
            conduct_ref[z, rows - 1 :] = near
            conduct_ref[z, rows - 2 : rows - 1] = far
            label = jnp.where(beyond | outside[z] if z in outside else beyond, -1.0, conduct_ref[z])
            conduct = jnp.zeros(label.shape, jnp.float32)
            uptake = jnp.zeros(label.shape, jnp.float32)
            for phase in range(phases):
                conduct = jnp.where(label == float(phase), diff_ref[phase], conduct)
                uptake = jnp.where(label == float(phase), upt_ref[phase], uptake)
            conduct_ref[z] = conduct
            uptake_ref[z] = uptake

    def in_plane(self, z):
        rows, width = self.conduct_ref.shape[1:]
        plane = self.conduct_ref[z]
        return (
            jnp.where(self.lane == 0, 0.0, pltpu.roll(plane, 1, 1)),
            jnp.where(self.lane == width - 1, 0.0, pltpu.roll(plane, width - 1, 1)),
            pltpu.roll(plane, 1, 0),
            pltpu.roll(plane, rows - 1, 0),
        )


def ends():
    slab = lax.axis_index("slab")
    return slab == lax.axis_size("slab") - 1, slab == 0


def residual_kernel(*refs):
    operands, outputs, scratch = refs[:11], refs[11:18], refs[18:]
    conduct_ref, uptake_ref, sol_ref = scratch[:3]
    local, sems = scratch[3:14], scratch[14]
    diff_ref, upt_ref, diag_ref, off_ref, cols_ref, table_ref, sol_in, label_in, src_in, top_ref, bottom_ref = local
    res_ref, face_ref, plain_ref, packed_ref, tables_ref, column_ref, record_ref = outputs
    for copy in fetch(list(zip(operands, local)), sems):
        copy.wait()
    own, depth, width = sol_in.shape
    rows = conduct_ref.shape[1]
    cells, nnz = off_ref.shape

    line = lax.broadcasted_iota(jnp.int32, record_ref.shape, 0)
    record = jnp.zeros(record_ref.shape, jnp.float32)
    for cell in range(cells):
        record = jnp.where(line == cell, diag_ref[cell], record)
    record_ref[...] = record
    record_ref[:, :nnz] = off_ref[...]
    record_ref[:, COLS_LANE : COLS_LANE + nnz] = cols_ref[...].astype(jnp.float32)
    tables_ref[...] = jnp.broadcast_to(flat(table_ref[...]), tables_ref.shape)
    column_ref[...] = jnp.transpose(tables_ref[...].astype(jnp.float32)).astype(jnp.int32)

    labels = []
    for start in range(0, depth, 8):
        block = jnp.transpose(label_in[:, start : start + 8, :].astype(jnp.float32), (1, 0, 2))
        labels = labels + [block[at] for at in range(8)]
    for k in range(depth // 2):
        packed_ref[k] = pack_labels(labels[2 * k], labels[2 * k + 1], 8)
    top_pairs = [top_ref[1, z : z + 1] for z in range(depth)]
    bottom_pairs = [bottom_ref[1, z : z + 1] for z in range(depth)]
    grid = Grid(diff_ref, upt_ref, labels, top_pairs, bottom_pairs, {}, conduct_ref, uptake_ref)
    blank = jnp.zeros((8, width), jnp.float32)
    for start in range(0, depth, 8):
        block = jnp.transpose(sol_in[:, start : start + 8, :], (1, 0, 2))
        for at in range(8):
            z = start + at
            plain_ref[z] = block[at]
            sol_ref[z, :own] = block[at]
            sol_ref[z, own:] = blank
            sol_ref[z, own : own + 1] = top_ref[0, z : z + 1]
            sol_ref[z, rows - 1 :] = bottom_ref[0, z : z + 1]
            sol_ref[z] = jnp.where(conduct_ref[z] > 0.0, sol_ref[z], 0.0)
    for start in range(0, depth, 8):
        block = jnp.transpose(src_in[:, start : start + 8, :], (1, 0, 2))
        for at in range(8):
            z = start + at
            conduct, value = conduct_ref[z], sol_ref[z]
            near = sum(grid.in_plane(z))
            diagonal = uptake_ref[z] + 2.0 * conduct + 0.5 * near
            flow = conduct * beside(value, grid.lane) + beside(conduct * value, grid.lane)
            applied = (diagonal * value - 0.5 * flow)[:own]
            conduct, value = conduct[:own], value[:own]
            for other in (z - 1, z + 1):
                if 0 <= other < depth:
                    applied = applied + 0.5 * (conduct + conduct_ref[other, :own]) * (value - sol_ref[other, :own])
            left = block[at] - applied
            res_ref[z] = left.astype(jnp.bfloat16)
            if z in (0, depth - 1):
                side = 0 if z == 0 else 3
                face_ref[side] = left
                face_ref[side + 1] = conduct
                face_ref[side + 2] = value


def weigh_kernel(
    diff_ref, upt_ref, packed_ref, src_in, even_ref, odd_ref, top_ref, bottom_ref, weight_ref,
    conduct_ref, uptake_ref,
):
    own, depth, width = src_in.shape
    planes, rows = conduct_ref.shape[0:2]
    labels = []
    for k in range(depth // 2):
        labels = labels + list(unpack_labels(packed_ref[k], own))
    high, low = from_slab(even_ref, odd_ref, LABELS, CORNERS)
    (high_near, high_far), (low_near, low_far) = unpack_labels(high, own), unpack_labels(low, own)
    labels = labels + [high_near, high_far, low_far, low_near]
    high, low = from_slab(even_ref, odd_ref, CORNERS, MESSAGE)
    top_pairs = [top_ref[1, z : z + 1] for z in range(depth)] + [high[0:1], high[1:2], low[1:2], low[0:1]]
    bottom_pairs = [bottom_ref[1, z : z + 1] for z in range(depth)] + [high[2:3], high[3:4], low[3:4], low[2:3]]
    above, below = ends()
    outside = {depth: above, depth + 1: above, depth + 2: below, depth + 3: below}
    grid = Grid(diff_ref, upt_ref, labels, top_pairs, bottom_pairs, outside, conduct_ref, uptake_ref)
    blank = jnp.zeros((8, width), jnp.float32)
    outer = dict(zip((depth, planes - 1), from_slab(even_ref, odd_ref, SOURCE, LABELS)))
    for start in (0, 8, planes - 1, depth):
        if start < depth:
            block = jnp.transpose(src_in[:, start : start + 8, :], (1, 0, 2))
            sources = {start + at: block[at] for at in range(8)}
        else:
            sources = {start: outer[start]}
        for z, source in sources.items():
            conduct = conduct_ref[z]
            near = grid.in_plane(z) + (conduct_ref[(z - 1) % planes], conduct_ref[(z + 1) % planes])
            diagonal = uptake_ref[z] + 3.0 * conduct + 0.5 * sum(near[1:], near[0])
            inside = conduct > 0.0
            scale = jnp.where(inside, OMEGA / jnp.where(inside, diagonal, 1.0), 0.0)
            for k, other in enumerate(near):
                weight_ref[k, z] = jnp.where(other > 0.0, 0.5 * scale * (conduct + other), 0.0)
            weight_ref[6, z, :own] = scale[:own] * source
            weight_ref[6, z, own:] = blank
            if z < depth:
                weight_ref[6, z, own : own + 1] = scale[own : own + 1] * top_ref[2, z : z + 1]
                weight_ref[6, z, rows - 1 :] = scale[rows - 1 :] * bottom_ref[2, z : z + 1]


def owners_of(basis_ref, base):
    tail = basis_ref[:, base:].astype(jnp.float32)
    return [
        (tail[:, 2 * k : 2 * k + 1] + 256.0 * tail[:, 2 * k + 1 : 2 * k + 2]).astype(jnp.int32)
        for k in range(3)
    ]


def restrict_kernel(diff_ref, column_ref, record_ref, even_ref, odd_ref, face_ref, res_ref, basis_ref, out_ref):
    depth, own, width = res_ref.shape
    entries = basis_ref.shape[0]
    pick = column_ref[:, 0:1] == lax.broadcasted_iota(jnp.int32, (entries, own), 1)
    pick = jnp.where(pick, 1.0, 0.0).astype(jnp.bfloat16)
    values = nearest_planes(even_ref, odd_ref)
    packed = from_slab(even_ref, odd_ref, LABELS, CORNERS)
    faces = {}
    for z, side, at in ((0, 0, 1), (depth - 1, 3, 0)):
        label = unpack_labels(packed[at], own)[0]
        beyond = jnp.zeros(label.shape, jnp.float32)
        for phase in range(diff_ref.shape[0]):
            beyond = jnp.where(label == float(phase), diff_ref[phase], beyond)
        beyond = jnp.where(ends()[at], 0.0, beyond)
        value = jnp.where(ends()[at], 0.0, values[at])
        applied = 0.5 * (face_ref[side + 1] + beyond) * (face_ref[side + 2] - value)
        faces[z] = (face_ref[side] - applied).astype(jnp.bfloat16)
    total = jnp.zeros((entries, width), jnp.float32)
    for z in range(depth):
        plane = faces[z] if z in faces else res_ref[z]
        piece = jnp.dot(pick, plane, preferred_element_type=jnp.float32)
        total = total + piece * basis_ref[:, z * width : (z + 1) * width].astype(jnp.float32)
    product = jnp.sum(total, axis=1, keepdims=True)
    ident = owners_of(basis_ref, basis_ref.shape[1] - 128)[0]
    copies, lines, lanes = out_ref.shape
    lane = lax.broadcasted_iota(jnp.int32, (entries, lanes), 1)
    line = lax.broadcasted_iota(jnp.int32, (8, lanes), 0)
    for base in range(0, lines, 8):
        block = record_ref[...] if base == 0 else jnp.zeros((8, lanes), jnp.float32)
        for row in range(8):
            share = jnp.where(ident == (base + row) * HALF + lane - HALF, product, 0.0)
            share = jnp.sum(jnp.where(lane >= HALF, share, 0.0), axis=0, keepdims=True)
            block = jnp.where((line == row) & (lane[:8] >= HALF), share, block)

        def put(copy, carry):
            out_ref[copy, base : base + 8, :] = block
            return carry

        lax.fori_loop(0, copies, put, 0, unroll=8)


def solve(got_ref, count, nnz):
    devices, lines, lanes = got_ref.shape
    summed = got_ref[0]
    if devices <= 64:
        for device in range(1, devices):
            summed = summed + got_ref[device]
    else:
        summed = lax.fori_loop(1, devices, lambda d, total: total + got_ref[d], summed)
    rhs = jnp.concatenate([summed[at : at + 1, HALF:] for at in range(count // HALF)], axis=1)
    record = jnp.transpose(got_ref[:, 0:8, :].reshape(count, lanes))
    line = lax.broadcasted_iota(jnp.int32, (COLS_LANE, lanes), 0)
    inverse = 1.0 / record[DIAG_LANE : DIAG_LANE + 1]
    chunks = range(0, count, lanes)
    values = [jnp.where(line < nnz, record[:COLS_LANE, at : at + lanes], 0.0) for at in chunks]
    places = [
        jnp.where(line < nnz, record[COLS_LANE : 2 * COLS_LANE, at : at + lanes], 0.0).astype(jnp.int32)
        for at in chunks
    ]
    state = rhs * inverse
    for repeat in range(COARSE_SWEEPS - 1):
        sources = [jnp.broadcast_to(state[:, at : at + lanes], (COLS_LANE, lanes)) for at in chunks]
        pulled = []
        for value, place in zip(values, places):
            found = jnp.zeros((COLS_LANE, lanes), jnp.float32)
            for k, source in enumerate(sources):
                taken = jnp.take_along_axis(source, place % lanes, axis=1, mode="promise_in_bounds")
                found = jnp.where(place // lanes == k, taken, found)
            pulled.append(jnp.sum(value * found, axis=0, keepdims=True))
        state = (rhs - jnp.concatenate(pulled, axis=1)) * inverse
    return state


def prolong_kernel(
    ids_ref, tables_ref, even_ref, odd_ref, got_ref, basis_ref, plain_ref, cor_ref, top_ref, bottom_ref,
    correction_ref, *, nnz, depth,
):
    planes, own, width = cor_ref.shape
    entries = tables_ref.shape[1]
    cells = ids_ref.shape[0]
    count = cells * got_ref.shape[0]
    state = solve(got_ref, count, nnz)

    line = lax.broadcasted_iota(jnp.int32, (cells, 1), 0)
    mine = jnp.zeros((cells, 1), jnp.int32)
    for cell in range(cells):
        mine = jnp.where(line == cell, ids_ref[cell], mine)

    def look_up(ident):
        hit = ident == lax.broadcasted_iota(jnp.int32, (ident.shape[0], count), 1)
        return jnp.sum(jnp.where(hit, state, 0.0), axis=1, keepdims=True)

    diagonal = line == lax.broadcasted_iota(jnp.int32, (cells, cells), 1)
    correction_ref[...] = jnp.sum(jnp.where(diagonal, look_up(mine), 0.0), axis=0, keepdims=True)
    near_high, near_low = nearest_planes(even_ref, odd_ref)
    far_high, far_low = from_slab(even_ref, odd_ref, FAR, SOURCE)
    wide = {depth: near_high, depth + 1: far_high, depth + 2: far_low, depth + 3: near_low}
    high, low = from_slab(even_ref, odd_ref, CORNERS, MESSAGE)
    line = TABLE - CORNERS
    table_high, table_low = high[line : line + 1, :entries], low[line : line + 1, :entries]
    tables = (tables_ref[0:1], table_high.astype(jnp.int32), table_low.astype(jnp.int32))
    base = depth * width
    owners = owners_of(basis_ref, basis_ref.shape[1] - 128)
    for group, owner in enumerate(owners):
        pick = tables[group] == lax.broadcasted_iota(jnp.int32, (own, entries), 0)
        pick = jnp.where(pick, 1.0, 0.0).astype(jnp.bfloat16)
        factor = look_up(owner)
        if group == 0:
            places = [(z, z * width) for z in range(depth)]
        else:
            at = depth + 2 * (group - 1)
            places = [(at + k, base + (at + k - depth) * width) for k in range(2)]
        for z, start in places:
            part = (basis_ref[:, start : start + width].astype(jnp.float32) * factor).astype(jnp.bfloat16)
            added = jnp.dot(pick, part, preferred_element_type=jnp.float32)
            value = (plain_ref[z] if z < depth else wide[z]) + added
            cor_ref[z] = value
            top_ref[z] = value[:2]
            bottom_ref[z] = value[own - 2 :]


def smooth_kernel(cor_ref, top_ref, bottom_ref, weight_ref, out_ref, ext_ref, mid_ref):
    planes, rows, width = ext_ref.shape
    own, depth, unused = out_ref.shape
    blank = jnp.zeros((8, width), jnp.float32)
    for z in range(planes):
        ext_ref[z, :own] = cor_ref[z]
        ext_ref[z, own:] = blank
        ext_ref[z, own : own + 2] = top_ref[z]
        ext_ref[z, rows - 2 :] = bottom_ref[z]

    def sweep(ref, z, upto):
        value = ref[z]
        near = (
            pltpu.roll(value, 1, 1)[:upto],
            pltpu.roll(value, width - 1, 1)[:upto],
            pltpu.roll(value, 1, 0)[:upto],
            pltpu.roll(value, rows - 1, 0)[:upto],
            ref[(z - 1) % planes, :upto],
            ref[(z + 1) % planes, :upto],
        )
        total = (1.0 - OMEGA) * value[:upto] + weight_ref[6, z, :upto]
        for k in range(6):
            total = total + weight_ref[k, z, :upto] * near[k]
        return total

    for z in [planes - 1] + list(range(depth + 1)):
        mid_ref[z] = sweep(ext_ref, z, rows)
    for start in range(0, depth, 8):
        for z in range(start, start + 8):
            ext_ref[z, :own] = sweep(mid_ref, z, own)
        out_ref[:, start : start + 8, :] = jnp.transpose(ext_ref[start : start + 8, :own], (1, 0, 2))


def shards(
    solution,
    source,
    phase_label,
    phase_diffusivity,
    phase_uptake,
    send_tiles,
    support_slot,
    support_len,
    coarse_ids,
    basis_values,
    coarse_diag,
    coarse_off,
    coarse_cols,
):
    f32, i32, bf16 = jnp.float32, jnp.int32, jnp.bfloat16
    rows, depth, width = solution.shape
    voxels = depth * width
    slabs, tiles = lax.axis_size("slab"), lax.axis_size("tile")
    devices = slabs * tiles
    capacity = send_tiles.shape[3]
    cells, support, unused = basis_values.shape
    entries = cells * support
    count = cells * devices
    nnz = coarse_off.shape[1]
    shape = jax.ShapeDtypeStruct
    planes, tall = depth + 4, rows + 8
    block = (rows, depth, width)
    table = send_tiles.reshape(slabs, capacity)
    wide = voxels + 4 * width + 128
    outgoing = pl.pallas_call(
        functools.partial(sort_kernel, capacity=capacity),
        out_shape=shape((entries, wide), bf16),
        in_specs=[HBM] * 4,
        out_specs=HBM,
        scratch_shapes=[
            pltpu.VMEM((1, entries), i32),
            pltpu.SMEM((cells,), i32),
            pltpu.SMEM((cells,), i32),
            pltpu.VMEM((entries, voxels), bf16),
            pltpu.VMEM((entries, wide), bf16),
            pltpu.SemaphoreType.DMA((12,)),
        ],
        compiler_params=params(60),
        name="sort_basis",
    )(
        support_slot.reshape(1, entries),
        support_len.reshape(cells),
        coarse_ids,
        basis_values.reshape(entries, voxels),
    )
    basis = lax.all_to_all(
        outgoing.reshape(slabs, capacity, wide), "slab", split_axis=0, concat_axis=0, tiled=True
    ).reshape(entries, wide)

    outgoing, solution, phase_label, source, table = lax.optimization_barrier(
        (outgoing, solution, phase_label, source, table)
    )

    def pinned(*arrays):
        return [pltpu.with_memory_space_constraint(array, pltpu.HBM) for array in arrays]

    message = shape((MESSAGE, width), bf16)
    edge = shape((3, depth, width), f32)
    even, odd, top, bottom = pl.pallas_call(
        border_kernel,
        out_shape=(message, message, edge, edge),
        in_specs=[HBM] * 4,
        out_specs=(VMEM,) * 4,
        scratch_shapes=[
            pltpu.VMEM(block, f32),
            pltpu.VMEM(block, i32),
            pltpu.VMEM(block, f32),
            pltpu.VMEM((slabs, capacity), i32),
            pltpu.SemaphoreType.DMA((4,)),
        ],
        compiler_params=params(8),
        name="border",
    )(*pinned(solution, phase_label, source, table))
    top = lax.ppermute(top, "tile", wheel(tiles, -1))
    bottom = lax.ppermute(bottom, "tile", wheel(tiles, 1))
    even, odd = pl.pallas_call(
        corner_kernel,
        out_shape=(message, message),
        in_specs=[HBM] * 4,
        out_specs=(VMEM,) * 2,
        scratch_shapes=[pltpu.VMEM(edge.shape, f32)] * 2 + [pltpu.SemaphoreType.DMA((4,))],
        compiler_params=params(8),
        name="corner",
    )(even, odd, top, bottom)
    even = lax.ppermute(even, "slab", pairs(slabs, False))
    odd = lax.ppermute(odd, "slab", pairs(slabs, True))
    row_top, row_bottom = top, bottom

    wide_block = pltpu.VMEM((planes, tall, width), f32)
    operands = [
        phase_diffusivity, phase_uptake, coarse_diag, coarse_off, coarse_cols, table,
        solution, phase_label, source, top, bottom,
    ]
    residual, face, plain, packed, tables, column, record = pl.pallas_call(
        residual_kernel,
        out_shape=(
            shape((depth, rows, width), bf16),
            shape((6, rows, width), f32),
            shape((depth, rows, width), f32),
            shape((depth // 2, 8, width), f32),
            shape((8, entries), i32),
            shape((entries, 8), i32),
            shape((cells, 128), f32),
        ),
        in_specs=[HBM] * 11,
        out_specs=(VMEM,) * 7,
        scratch_shapes=[pltpu.VMEM((depth, tall, width), f32)] * 3
        + [pltpu.SMEM(array.shape, array.dtype) for array in operands[:3]]
        + [pltpu.VMEM(array.shape, array.dtype) for array in operands[3:]]
        + [pltpu.SemaphoreType.DMA((11,))],
        compiler_params=params(12),
        name="residual",
    )(*pinned(*operands[:9]), *operands[9:])

    lines = max(8, count // HALF)
    payload = pl.pallas_call(
        restrict_kernel,
        out_shape=shape((devices, lines, 128), f32),
        in_specs=[SMEM] + [VMEM] * 7,
        out_specs=VMEM,
        compiler_params=params(8),
        name="restrict",
    )(phase_diffusivity, column, record, even, odd, face, residual, basis)
    got = lax.all_to_all(payload, ("slab", "tile"), split_axis=0, concat_axis=0, tiled=True)

    edge = shape((planes, 2, width), f32)
    corrected, top, bottom, coarse_correction = pl.pallas_call(
        functools.partial(prolong_kernel, nnz=nnz, depth=depth),
        out_shape=(shape((planes, rows, width), f32), edge, edge, shape((1, cells), f32)),
        in_specs=[SMEM] + [VMEM] * 6,
        out_specs=(VMEM, VMEM, VMEM, VMEM),
        compiler_params=params(12 + count * count // (8 * MIB)),
        name="prolong",
    )(coarse_ids, tables, even, odd, got, basis, plain)
    corrected, packed = lax.optimization_barrier((corrected, packed))
    weights = pl.pallas_call(
        weigh_kernel,
        out_shape=shape((7, planes, tall, width), f32),
        in_specs=[SMEM, SMEM] + [VMEM] * 6,
        out_specs=VMEM,
        scratch_shapes=[wide_block] * 2,
        compiler_params=params(12),
        name="weigh",
    )(phase_diffusivity, phase_uptake, packed, source, even, odd, row_top, row_bottom)
    top = lax.ppermute(top, "tile", wheel(tiles, -1))
    bottom = lax.ppermute(bottom, "tile", wheel(tiles, 1))
    smooth = pl.pallas_call(
        smooth_kernel,
        out_shape=shape((rows, depth, width), f32),
        in_specs=[VMEM] * 4,
        out_specs=VMEM,
        scratch_shapes=[wide_block] * 2,
        compiler_params=params(16),
        name="smooth",
    )(corrected, top, bottom, weights)
    return smooth, coarse_correction.reshape(cells)


def solution(mesh):
    placed = (
        P("tile", "slab", None),
        P("tile", "slab", None),
        P("tile", "slab", None),
        P(),
        P(),
        P("slab", "tile", None, None),
        P("slab", "tile", None),
        P("slab", "tile", None),
        P(("slab", "tile")),
        P(("slab", "tile"), None, None),
        P(("slab", "tile")),
        P(("slab", "tile"), None),
        P(("slab", "tile"), None),
    )
    return jax.shard_map(
        shards,
        mesh=mesh,
        in_specs=placed,
        out_specs=(P("tile", "slab", None), P(("slab", "tile"))),
        check_vma=False,
    )
```

time: 56.5 us -> 50 us (0.88)
  starting transfers between devices: 18.7 us -> 11.2 us
  Pallas kernels: 14.4 us -> 15.2 us
    ppermute x2 -> x0, starting transfers between devices: 3.51 us -> none  [the longest x1 2.02 us: shards(): late_even = lax.ppermute(late_even, 'slab', pairs(slabs, False))]
    all_to_all x1, starting transfers between devices: 9.67 us -> 7.26 us  [shards(): lax.all_to_all(outgoing.reshape(slabs, capacity, wide), 'slab', split_axi...]
    ppermute x2, waiting for transfers between devices: 0.01 us -> 1.8 us  [shards(): top = lax.ppermute(top, 'tile', wheel(tiles, -1))]
    all_to_all x1, waiting for transfers between devices: 7.94 us -> 6.27 us  [shards(): lax.all_to_all(outgoing.reshape(slabs, capacity, wide), 'slab', split_axi...]
    ppermute x2, waiting for transfers between devices: 1.4 us -> 2.5 us  [shards(): bottom = lax.ppermute(bottom, 'tile', wheel(tiles, 1))]
    ppermute x1, starting transfers between devices: 3 us -> 2.01 us  [shards(): even = lax.ppermute(even, 'slab', pairs(slabs, False))]
    ppermute x1, waiting for transfers between devices: 0.83 us -> 0.01 us  [shards(): even = lax.ppermute(even, 'slab', pairs(slabs, False))]
    ppermute x1, starting transfers between devices: 1.44 us -> 0.65 us  [shards(): odd = lax.ppermute(odd, 'slab', pairs(slabs, True))]
  transfers between devices with their start and end apart: 9 -> 7, of which waited for: 4 -> 4; matrix products, arithmetic and copies ran while one was open for 0% -> 0% of each run, Pallas kernels for 12% -> 16%
where the time goes in v3:
time: 50 us; the launch traced here: 49.4 us
  Pallas kernels  15.2 us (30%)
  blocking collectives  11.7 us (23%)
  starting transfers between devices  11.2 us (22%)
  waiting for transfers between devices  10.6 us (21%)
  between operations  0.75 us (2%)
    all_to_all x1, blocking collectives, shards(): lax.all_to_all(payload, ('slab', 'tile'), split_axis=0, concat_axis=0, ti...  11.7 us
    all_to_all x1, starting transfers between devices, shards(): lax.all_to_all(outgoing.reshape(slabs, capacity, wide), 'slab', split_axi...  7.26 us
    all_to_all x1, waiting for transfers between devices, shards(): lax.all_to_all(outgoing.reshape(slabs, capacity, wide), 'slab', split_axi...  6.27 us
    pallas_call x1, Pallas kernels, shards(): pl.pallas_call(residual_kernel, out_shape=(shape((depth, rows, width), bf...  3.2 us
    pallas_call x1, Pallas kernels, shards(): pl.pallas_call(functools.partial(sort_kernel, capacity=capacity), out_sha...  2.51 us
    ppermute x2, waiting for transfers between devices, shards(): bottom = lax.ppermute(bottom, 'tile', wheel(tiles, 1))  2.5 us
    pallas_call x1, Pallas kernels, shards(): pl.pallas_call(weigh_kernel, out_shape=shape((7, planes, tall, width), f3...  2.48 us
    pallas_call x1, Pallas kernels, shards(): pl.pallas_call(smooth_kernel, out_shape=shape((rows, depth, width), f32),...  2.13 us
  transfers between devices with their start and end apart: 7, of which 4 were waited for; matrix products, arithmetic and copies ran while one was open for 0% of the time, Pallas kernels for 16%

profile of v3, /device:TPU:0, one launch (start us, length us, event | category | flops | bytes accessed | tf_op | source)
XLA Modules:
  0.0 49.4 jit_solution(8385679458893068163)
XLA Ops:
  0.6 0.0 copy-start.2
  0.6 0.0 copy-start
  0.7 0.0 copy-start.1
  0.7 0.0 copy-start.3
  0.7 2.5 %sort_basis.1 = bf16[64,5248]{1,0:T(8,128)(2,1)} custom-call(s32[1,64]{1,0:T(1,128)} %bitcast.13, s32[8]{0:T(128)} %bitcast.14, s32[8]{0:T(128)} %ids_ref.1, bf16[64,4096]{1,0:T(8,128)(2,1)} %bitcast.10), custom_call_target="tpu_custom_call" | custom-call | tf_op jit(solution)/shard_map/sort_basis/pallas_call | solution.py:558
  3.2 7.3 %all-to-all-start = ((bf16[8,8,5248]{2,1,0:T(8,128)(2,1)}), bf16[8,8,5248]{2,1,0:T(8,128)(2,1)S(1)}, u32[]{:S(2)}, u32[]{:S(2)}) async-start(bf16[8,8,5248]{2,1,0:T(8,128)(2,1)} %bitcast.9), calls=%async_computation | async-start | bytes 1343488 | tf_op jit(solution)/shard_map/all_to_all | solution.py:579
  10.5 1.7 %border.1 = (bf16[160,256]{1,0:T(8,128)(2,1)S(1)}, bf16[160,256]{1,0:T(8,128)(2,1)S(1)}, f32[3,16,256]{2,1,0:T(8,128)S(1)}, f32[3,16,256]{2,1,0:T(8,128)S(1)}) custom-call(f32[32,16,256]{2,1,0:T(8,128)} %refs_6_, s32[32,16,256]{2,1,0:T(8,128)} %refs_7_, f32[32,16,256]{2,1,0:T(8,128)} %src_in, s32[8,8]{1,0:T(8,128)} %bitcast.11), custom_call_target="tpu_custom_call" | custom-call | tf_op jit(solution)/shard_map/border/pallas_call | solution.py:592
  12.2 0.7 %collective-permute-start = (f32[3,16,256]{2,1,0:T(8,128)S(1)}, f32[3,16,256]{2,1,0:T(8,128)S(1)}, u32[]{:S(2)}, u32[]{:S(2)}) collective-permute-start(f32[3,16,256]{2,1,0:T(8,128)S(1)} %get-tuple-element.29), channel_id=1, source_target_pairs={{0,3},{1,0},{2,1},{3,2},{4,7},{5,4},{6,5},{7,6},{8,11},{9,8},{10,9... | collective-permute-start | bytes 147464 | tf_op jit(solution)/shard_map/ppermute | solution.py:607
  12.9 0.0 collective-permute-start.1
  12.9 1.8 %collective-permute-done.refs_9_.top_in.top_ref = f32[3,16,256]{2,1,0:T(8,128)S(1)} collective-permute-done((f32[3,16,256]{2,1,0:T(8,128)S(1)}, f32[3,16,256]{2,1,0:T(8,128)S(1)}, u32[]{:S(2)}, u32[]{:S(2)}) %collective-permute-start) | collective-permute-done | bytes 49184 | tf_op jit(solution)/shard_map/ppermute | solution.py:607
  14.7 1.7 %collective-permute-done.1.refs_10_.bottom_in.bottom_ref = f32[3,16,256]{2,1,0:T(8,128)S(1)} collective-permute-done((f32[3,16,256]{2,1,0:T(8,128)S(1)}, f32[3,16,256]{2,1,0:T(8,128)S(1)}, u32[]{:S(2)}, u32[]{:S(2)}) %collective-permute-start.1) | collective-permute-done | bytes 49184 | tf_op jit(solution)/shard_map/ppermute | solution.py:608
  16.4 0.4 corner.1
  16.8 2.0 %collective-permute-start.2 = (bf16[160,256]{1,0:T(8,128)(2,1)S(1)}, bf16[160,256]{1,0:T(8,128)(2,1)S(1)}, u32[]{:S(2)}, u32[]{:S(2)}) collective-permute-start(bf16[160,256]{1,0:T(8,128)(2,1)S(1)} %get-tuple-element.34), channel_id=1, source_target_pairs={{0,4},{4,0},{8,12},{12,8},{16,20},{20,16},{24,28},{28,24},{1,5},{5... | collective-permute-start | bytes 245768 | tf_op jit(solution)/shard_map/ppermute | solution.py:618
  18.8 0.7 %collective-permute-start.3 = (bf16[160,256]{1,0:T(8,128)(2,1)S(1)}, bf16[160,256]{1,0:T(8,128)(2,1)S(1)}, u32[]{:S(2)}, u32[]{:S(2)}) collective-permute-start(bf16[160,256]{1,0:T(8,128)(2,1)S(1)} %get-tuple-element.35), channel_id=1, source_target_pairs={{0,0},{4,8},{8,4},{12,16},{16,12},{20,24},{24,20},{28,28},{1,1},{5... | collective-permute-start | bytes 245768 | tf_op jit(solution)/shard_map/ppermute | solution.py:619
  19.5 3.2 %residual.1 = (bf16[16,32,256]{2,1,0:T(8,128)(2,1)S(1)}, f32[6,32,256]{2,1,0:T(8,128)S(1)}, f32[16,32,256]{2,1,0:T(8,128)S(1)}, f32[8,8,256]{2,1,0:T(8,128)S(1)}...) custom-call(f32[3]{0:T(128)} %diff_ref.3, f32[3]{0:T(128)} %upt_ref.1, f32[8]{0:T(128)} %refs_2_.1, ...), custom_call_target="tpu_custom_call" | custom-call | tf_op jit(solution)/shard_map/residual/pallas_call | solution.py:627
  22.7 0.0 collective-permute-done.2.even_ref
  22.7 0.0 collective-permute-done.3.odd_ref
  22.7 6.3 %all-to-all-done = bf16[8,8,5248]{2,1,0:T(8,128)(2,1)S(1)} async-done(((bf16[8,8,5248]{2,1,0:T(8,128)(2,1)}), bf16[8,8,5248]{2,1,0:T(8,128)(2,1)S(1)}, u32[]{:S(2)}, u32[]{:S(2)}) %all-to-all-start) | async-done | bytes 671776 | tf_op jit(solution)/shard_map/all_to_all | solution.py:579
  29.0 0.0 copy-done.1
  29.0 1.0 %restrict.1 = f32[32,8,128]{2,1,0:T(8,128)S(1)} custom-call(f32[3]{0:T(128)S(1)} %copy-done.1, s32[64,8]{1,0:T(8,128)S(1)} %get-tuple-element.36.column_ref, f32[8,128]{1,0:T(8,128)S(1)} %get-tuple-element.37.record_ref, bf16[160,256]{1,0:T(8,128)(2,1)S(1)} %collective-permute-done.2.even_ref, bf16[160,256]{1,0:T(8,128)(2,1)S(1)} %collective-permute-done.3.odd_ref, ...), custom_call_target="tpu_custom_call" | custom-call | tf_op jit(solution)/shard_map/restrict/pallas_call | solution.py:649
  30.0 11.7 %all_to_all.10.got_ref = f32[32,8,128]{2,1,0:T(8,128)S(1)} all-to-all(f32[32,8,128]{2,1,0:T(8,128)S(1)} %restrict.1), channel_id=1, replica_groups=mesh['slab'=8,'tile'=4] {'slab','tile'}, dimensions={0} | all-to-all | bytes 262144 | tf_op jit(solution)/shard_map/all_to_all | solution.py:657
  41.7 0.0 copy-done.2
  41.8 1.8 %prolong.1 = (f32[20,32,256]{2,1,0:T(8,128)S(1)}, f32[20,2,256]{2,1,0:T(2,128)S(1)}, f32[20,2,256]{2,1,0:T(2,128)S(1)}, f32[1,8]{1,0:T(1,128)}) custom-call(s32[8]{0:T(128)S(1)} %copy-done.2, s32[8,64]{1,0:T(8,128)S(1)} %get-tuple-element.31.tables_ref, bf16[160,256]{1,0:T(8,128)(2,1)S(1)} %collective-permute-done.2.even_ref, ...), custom_call_target="tpu_custom_call" | custom-call | tf_op jit(solution)/shard_map/prolong/pallas_call | solution.py:660
  43.5 0.2 collective-permute-start.4
  43.7 0.3 collective-permute-start.5
  44.0 0.0 copy-done
  44.0 0.0 copy-done.3
  44.0 2.5 %weigh.1.weight_ref = f32[7,20,40,256]{3,2,1,0:T(8,128)S(1)} custom-call(f32[3]{0:T(128)S(1)} %copy-done.1, f32[3]{0:T(128)S(1)} %copy-done.3, f32[8,8,256]{2,1,0:T(8,128)S(1)} %get-tuple-element.46.packed_ref, f32[32,16,256]{2,1,0:T(8,128)S(1)} %copy-done, bf16[160,256]{1,0:T(8,128)(2,1)S(1)} %collective-permute-done.2.even_ref, ...), custom_call_target="tpu_custom_call" | custom-call | tf_op jit(solution)/shard_map/weigh/pallas_call | solution.py:669
  46.5 0.0 collective-permute-done.4.top_ref
  46.5 0.8 %collective-permute-done.5.bottom_ref = f32[20,2,256]{2,1,0:T(2,128)S(1)} collective-permute-done((f32[20,2,256]{2,1,0:T(2,128)S(1)}, f32[20,2,256]{2,1,0:T(2,128)S(1)}, u32[]{:S(2)}, u32[]{:S(2)}) %collective-permute-start.5) | collective-permute-done | bytes 40992 | tf_op jit(solution)/shard_map/ppermute | solution.py:679
  47.3 2.1 %smooth.1 = f32[32,16,256]{2,1,0:T(8,128)} custom-call(f32[20,32,256]{2,1,0:T(8,128)S(1)} %get-tuple-element.43.cor_ref, f32[20,2,256]{2,1,0:T(2,128)S(1)} %collective-permute-done.4.top_ref, f32[20,2,256]{2,1,0:T(2,128)S(1)} %collective-permute-done.5.bottom_ref, f32[7,20,40,256]{3,2,1,0:T(8,128)S(1)} %weigh.1.weight_ref), custom_call_target="tpu_custom_call" | custom-call | tf_op jit(solution)/shard_map/smooth/pallas_call | solution.py:680
Async XLA Ops:
  0.6 41.1 %copy-start.2 = (s32[8]{0:T(128)S(1)}, s32[8]{0:T(128)}, u32[]{:S(2)}) copy-start(s32[8]{0:T(128)} %ids_ref.1) | copy-start | bytes 100
  0.6 43.4 %copy-start = (f32[32,16,256]{2,1,0:T(8,128)S(1)}, f32[32,16,256]{2,1,0:T(8,128)}, u32[]{:S(2)}) copy-start(f32[32,16,256]{2,1,0:T(8,128)} %src_in) | copy-start | bytes 1572868
  0.7 28.3 %copy-start.1 = (f32[3]{0:T(128)S(1)}, f32[3]{0:T(128)}, u32[]{:S(2)}) copy-start(f32[3]{0:T(128)} %diff_ref.3) | copy-start | bytes 40
  0.7 43.4 %copy-start.3 = (f32[3]{0:T(128)S(1)}, f32[3]{0:T(128)}, u32[]{:S(2)}) copy-start(f32[3]{0:T(128)} %upt_ref.1) | copy-start | bytes 40
  3.2 25.8 %all-to-all-start = ((bf16[8,8,5248]{2,1,0:T(8,128)(2,1)}), bf16[8,8,5248]{2,1,0:T(8,128)(2,1)S(1)}, u32[]{:S(2)}, u32[]{:S(2)}) async-start(bf16[8,8,5248]{2,1,0:T(8,128)(2,1)} %bitcast.9), calls=%async_computation | async-start | bytes 1343488 | tf_op jit(solution)/shard_map/all_to_all | solution.py:579
  12.2 2.5 %collective-permute-start = (f32[3,16,256]{2,1,0:T(8,128)S(1)}, f32[3,16,256]{2,1,0:T(8,128)S(1)}, u32[]{:S(2)}, u32[]{:S(2)}) collective-permute-start(f32[3,16,256]{2,1,0:T(8,128)S(1)} %get-tuple-element.29), channel_id=1, source_target_pairs={{0,3},{1,0},{2,1},{3,2},{4,7},{5,4},{6,5},{7,6},{8,11},{9,8},{10,9... | collective-permute-start | bytes 147464 | tf_op jit(solution)/shard_map/ppermute | solution.py:607
  12.9 3.5 %collective-permute-start.1 = (f32[3,16,256]{2,1,0:T(8,128)S(1)}, f32[3,16,256]{2,1,0:T(8,128)S(1)}, u32[]{:S(2)}, u32[]{:S(2)}) collective-permute-start(f32[3,16,256]{2,1,0:T(8,128)S(1)} %get-tuple-element.30), channel_id=1, source_target_pairs={{0,1},{1,2},{2,3},{3,0},{4,5},{5,6},{6,7},{7,4},{8,9},{9,10},{10,1... | collective-permute-start | bytes 147464 | tf_op jit(solution)/shard_map/ppermute | solution.py:608
  16.8 5.9 %collective-permute-start.2 = (bf16[160,256]{1,0:T(8,128)(2,1)S(1)}, bf16[160,256]{1,0:T(8,128)(2,1)S(1)}, u32[]{:S(2)}, u32[]{:S(2)}) collective-permute-start(bf16[160,256]{1,0:T(8,128)(2,1)S(1)} %get-tuple-element.34), channel_id=1, source_target_pairs={{0,4},{4,0},{8,12},{12,8},{16,20},{20,16},{24,28},{28,24},{1,5},{5... | collective-permute-start | bytes 245768 | tf_op jit(solution)/shard_map/ppermute | solution.py:618
  18.8 3.9 %collective-permute-start.3 = (bf16[160,256]{1,0:T(8,128)(2,1)S(1)}, bf16[160,256]{1,0:T(8,128)(2,1)S(1)}, u32[]{:S(2)}, u32[]{:S(2)}) collective-permute-start(bf16[160,256]{1,0:T(8,128)(2,1)S(1)} %get-tuple-element.35), channel_id=1, source_target_pairs={{0,0},{4,8},{8,4},{12,16},{16,12},{20,24},{24,20},{28,28},{1,1},{5... | collective-permute-start | bytes 245768 | tf_op jit(solution)/shard_map/ppermute | solution.py:619
  43.5 3.0 %collective-permute-start.4 = (f32[20,2,256]{2,1,0:T(2,128)S(1)}, f32[20,2,256]{2,1,0:T(2,128)S(1)}, u32[]{:S(2)}, u32[]{:S(2)}) collective-permute-start(f32[20,2,256]{2,1,0:T(2,128)S(1)} %get-tuple-element.44), channel_id=1, source_target_pairs={{0,3},{1,0},{2,1},{3,2},{4,7},{5,4},{6,5},{7,6},{8,11},{9,8},{10,9... | collective-permute-start | bytes 122888 | tf_op jit(solution)/shard_map/ppermute | solution.py:678
  43.7 3.6 %collective-permute-start.5 = (f32[20,2,256]{2,1,0:T(2,128)S(1)}, f32[20,2,256]{2,1,0:T(2,128)S(1)}, u32[]{:S(2)}, u32[]{:S(2)}) collective-permute-start(f32[20,2,256]{2,1,0:T(2,128)S(1)} %get-tuple-element.45), channel_id=1, source_target_pairs={{0,1},{1,2},{2,3},{3,0},{4,5},{5,6},{6,7},{7,4},{8,9},{9,10},{10,1... | collective-permute-start | bytes 122888 | tf_op jit(solution)/shard_map/ppermute | solution.py:679

commit v4 on v3

--- a/solution.py
+++ b/solution.py
@@ -46,13 +46,15 @@
     return copies
 
 
-def sort_kernel(
-    slot_hbm, len_hbm, ids_hbm, basis_hbm, out_hbm, slot_ref, len_ref, ids_ref, basis_ref, out_ref, sems, *, capacity
-):
+def sort_kernel(slot_hbm, len_hbm, ids_hbm, basis_hbm, *refs, capacity):
+    slot_ref, len_ref, ids_ref, basis_ref, sems = refs[-5:]
+    outs = refs[:-5]
     entries, voxels = basis_ref.shape
+    lines = entries // len(outs)
     cells = len_ref.shape[0]
     support = entries // cells
-    border = (out_ref.shape[1] - 128 - voxels) // 2
+    wide = outs[0].shape[1]
+    border = (wide - 128 - voxels) // 2
     chunk = voxels // 4
     pieces = [
         (basis_hbm.at[:, pl.ds(k * chunk, chunk)], basis_ref.at[:, pl.ds(k * chunk, chunk)]) for k in range(4)
@@ -71,22 +73,21 @@
     live = lane % support < length
     slot = jnp.where(live, slot_ref[...], -1)
     row = lax.broadcasted_iota(jnp.int32, (entries, entries), 0)
+    if len(outs) > 1:
+        row = row ^ (lax.axis_index("slab") * capacity)
     above = jnp.where(row >= entries - capacity, row + capacity - entries, row + capacity)
     below = jnp.where(row < capacity, row - capacity + entries, row - capacity)
     hits = [slot == row, slot == above, slot == below]
     picks = [jnp.where(hit, 1.0, 0.0).astype(jnp.bfloat16) for hit in hits]
-    sent = []
+
+    def put(block, start):
+        for k, out in enumerate(outs):
+            part = block[k * lines : (k + 1) * lines]
+            out[:, start : start + block.shape[1]] = part.astype(jnp.bfloat16)
 
     def move(pick, start, size, target):
-        out_ref[:, target : target + size] = jnp.dot(
-            pick, basis_ref[:, start : start + size], preferred_element_type=jnp.float32
-        ).astype(jnp.bfloat16)
-
-    def send(start, size):
-        part = pl.ds(start, size)
-        copy = pltpu.make_async_copy(out_ref.at[:, part], out_hbm.at[:, part], sems.at[len(copies) + len(sent)])
-        copy.start()
-        sent.append(copy)
+        block = basis_ref[:, start : start + size]
+        put(jnp.dot(pick, block, preferred_element_type=jnp.float32), target)
 
     extra = lax.broadcasted_iota(jnp.int32, (entries, 128), 1)
     tail = jnp.zeros((entries, 128), jnp.float32)
@@ -94,18 +95,26 @@
         low = jnp.sum(jnp.where(hit, ident % 256, 0).astype(jnp.float32), axis=1, keepdims=True)
         high = jnp.sum(jnp.where(hit, ident // 256, 0).astype(jnp.float32), axis=1, keepdims=True)
         tail = jnp.where(extra == 2 * k, low, jnp.where(extra == 2 * k + 1, high, tail))
-    out_ref[:, voxels + 2 * border :] = tail.astype(jnp.bfloat16)
+    put(tail, voxels + 2 * border)
     for k in range(4):
         copies[3 + k].wait()
         for start in range(k * chunk, (k + 1) * chunk, 512):
             move(picks[0], start, 512, start)
-        send(k * chunk, chunk)
         if k == 0:
             move(picks[1], 0, border, voxels)
     move(picks[2], voxels - border, border, voxels + border)
-    send(voxels, 2 * border + 128)
-    for copy in sent:
-        copy.wait()
+
+
+def shuffle(table, slab, slots, capacity):
+    lane = lax.broadcasted_iota(jnp.int32, table.shape, 1)
+    size = table.shape[1]
+    bit = 1
+    while bit < slots:
+        shift = bit * capacity
+        other = jnp.where((lane // shift) % 2 == 1, pltpu.roll(table, shift, 1), pltpu.roll(table, size - shift, 1))
+        table = jnp.where((slab // bit) % 2 == 1, other, table)
+        bit *= 2
+    return table
 
 
 LOW, FAR, SOURCE, LABELS, CORNERS, TABLE = 32, 64, 96, 128, 144, 148
@@ -114,7 +123,7 @@
 
 def border_kernel(
     sol_hbm, label_hbm, src_hbm, table_hbm, even_ref, odd_ref, top_ref, bottom_ref,
-    sol_ref, label_ref, src_ref, table_ref, sems,
+    sol_ref, label_ref, src_ref, table_ref, sems, *, direct,
 ):
     rows, depth, width = sol_ref.shape
     blocks = ((sol_hbm, sol_ref), (label_hbm, label_ref), (src_hbm, src_ref), (table_hbm, table_ref))
@@ -131,13 +140,18 @@
     down = near, far, origin, pack_labels(label, label_far, 16)
     far, near, label_far, label, unused, origin = planes(depth - 2)
     up = near, far, origin, pack_labels(label, label_far, 16)
+    slots, capacity = table_ref.shape
     table = flat(table_ref[...]).astype(jnp.float32)
-    entries = table.shape[1]
-    table = jnp.concatenate([table, jnp.zeros((1, width - entries), jnp.float32)], axis=1)
+    table = jnp.concatenate([table, jnp.zeros((1, width - table.shape[1]), jnp.float32)], axis=1)
+    tables = [table, table]
+    if direct:
+        slab, slabs = lax.axis_index("slab"), lax.axis_size("slab")
+        tables = [shuffle(table, (slab + step) % slabs, slots, capacity) for step in (1, slabs - 1)]
     line = lax.broadcasted_iota(jnp.int32, (16, width), 0) + CORNERS
-    table = jnp.where(line == TABLE, table, 0.0)
+    up = up + (jnp.where(line == TABLE, tables[0], 0.0),)
+    down = down + (jnp.where(line == TABLE, tables[1], 0.0),)
     for first, second, ref in ((up, down, even_ref), (down, up, odd_ref)):
-        near, far, origin, labels = [jnp.where(odd, b, a) for a, b in zip(first, second)]
+        near, far, origin, labels, table = [jnp.where(odd, b, a) for a, b in zip(first, second)]
         high = near.astype(jnp.bfloat16)
         ref[:LOW] = high
         ref[LOW:FAR] = (near - high.astype(jnp.float32)).astype(jnp.bfloat16)
@@ -212,11 +226,10 @@
 
 
 class Grid:
-    def __init__(self, diff_ref, upt_ref, labels, top_pairs, bottom_pairs, outside, conduct_ref, uptake_ref):
+    def __init__(self, diffs, uptakes, labels, top_pairs, bottom_pairs, outside, conduct_ref, uptake_ref):
         self.conduct_ref, self.uptake_ref = conduct_ref, uptake_ref
         self.planes, rows, width = conduct_ref.shape
         own = labels[0].shape[0]
-        phases = diff_ref.shape[0]
         row = lax.broadcasted_iota(jnp.int32, (rows, width), 0)
         self.lane = lax.broadcasted_iota(jnp.int32, (rows, width), 1)
         tile = lax.axis_index("tile")
@@ -236,9 +249,9 @@
             label = jnp.where(beyond | outside[z] if z in outside else beyond, -1.0, conduct_ref[z])
             conduct = jnp.zeros(label.shape, jnp.float32)
             uptake = jnp.zeros(label.shape, jnp.float32)
-            for phase in range(phases):
-                conduct = jnp.where(label == float(phase), diff_ref[phase], conduct)
-                uptake = jnp.where(label == float(phase), upt_ref[phase], uptake)
+            for phase, (diff, upt) in enumerate(zip(diffs, uptakes)):
+                conduct = jnp.where(label == float(phase), diff, conduct)
+                uptake = jnp.where(label == float(phase), upt, uptake)
             conduct_ref[z] = conduct
             uptake_ref[z] = uptake
 
@@ -258,27 +271,42 @@
     return slab == lax.axis_size("slab") - 1, slab == 0
 
 
-def residual_kernel(*refs):
-    operands, outputs, scratch = refs[:11], refs[11:18], refs[18:]
+def residual_kernel(*refs, direct):
+    operands, outputs, scratch = refs[:12], refs[12:20], refs[20:]
     conduct_ref, uptake_ref, sol_ref = scratch[:3]
-    local, sems = scratch[3:14], scratch[14]
-    diff_ref, upt_ref, diag_ref, off_ref, cols_ref, table_ref, sol_in, label_in, src_in, top_ref, bottom_ref = local
-    res_ref, face_ref, plain_ref, packed_ref, tables_ref, column_ref, record_ref = outputs
+    local, sems = scratch[3:15], scratch[15]
+    diff_ref, upt_ref, diag_ref, ids_ref = local[:4]
+    off_ref, cols_ref, table_ref, sol_in, label_in, src_in, top_ref, bottom_ref = local[4:]
+    res_ref, face_ref, plain_ref, packed_ref, tables_ref, column_ref, record_ref, scalar_ref = outputs
     for copy in fetch(list(zip(operands, local)), sems):
         copy.wait()
     own, depth, width = sol_in.shape
     rows = conduct_ref.shape[1]
     cells, nnz = off_ref.shape
 
+    for phase in range(diff_ref.shape[0]):
+        scalar_ref[0, phase] = jnp.full((8, 128), diff_ref[phase])
+        scalar_ref[1, phase] = jnp.full((8, 128), upt_ref[phase])
     line = lax.broadcasted_iota(jnp.int32, record_ref.shape, 0)
+    mine = jnp.zeros(record_ref.shape, jnp.int32)
+    for cell in range(cells):
+        mine = jnp.where(line == cell, ids_ref[cell], mine)
+    scalar_ref[2, 0] = mine.astype(jnp.float32)
     record = jnp.zeros(record_ref.shape, jnp.float32)
     for cell in range(cells):
         record = jnp.where(line == cell, diag_ref[cell], record)
     record_ref[...] = record
     record_ref[:, :nnz] = off_ref[...]
     record_ref[:, COLS_LANE : COLS_LANE + nnz] = cols_ref[...].astype(jnp.float32)
-    tables_ref[...] = jnp.broadcast_to(flat(table_ref[...]), tables_ref.shape)
-    column_ref[...] = jnp.transpose(tables_ref[...].astype(jnp.float32)).astype(jnp.int32)
+    slots, capacity = table_ref.shape
+    entries = slots * capacity
+    table = flat(table_ref[...]).astype(jnp.float32)
+    table = jnp.concatenate([table, jnp.zeros((1, 128 - entries), jnp.float32)], axis=1)
+    if direct:
+        table = shuffle(table, lax.axis_index("slab"), slots, capacity)
+    table = jnp.broadcast_to(table, (8, 128))
+    tables_ref[...] = table[:, :entries].astype(jnp.int32)
+    column_ref[...] = jnp.transpose(table)[:entries].astype(jnp.int32)
 
     labels = []
     for start in range(0, depth, 8):
@@ -288,7 +316,9 @@
         packed_ref[k] = pack_labels(labels[2 * k], labels[2 * k + 1], 8)
     top_pairs = [top_ref[1, z : z + 1] for z in range(depth)]
     bottom_pairs = [bottom_ref[1, z : z + 1] for z in range(depth)]
-    grid = Grid(diff_ref, upt_ref, labels, top_pairs, bottom_pairs, {}, conduct_ref, uptake_ref)
+    phases = range(diff_ref.shape[0])
+    diffs, uptakes = [diff_ref[phase] for phase in phases], [upt_ref[phase] for phase in phases]
+    grid = Grid(diffs, uptakes, labels, top_pairs, bottom_pairs, {}, conduct_ref, uptake_ref)
     blank = jnp.zeros((8, width), jnp.float32)
     for start in range(0, depth, 8):
         block = jnp.transpose(sol_in[:, start : start + 8, :], (1, 0, 2))
@@ -322,8 +352,16 @@
                 face_ref[side + 2] = value
 
 
+def phase_rows(scalar_ref, kind, width):
+    found = []
+    for phase in range(scalar_ref.shape[1]):
+        row = scalar_ref[kind, phase, 0:1]
+        found.append(jnp.concatenate([row] * (width // row.shape[1]), axis=1))
+    return found
+
+
 def weigh_kernel(
-    diff_ref, upt_ref, packed_ref, src_in, even_ref, odd_ref, top_ref, bottom_ref, weight_ref,
+    scalar_ref, packed_ref, src_in, even_ref, odd_ref, top_ref, bottom_ref, weight_ref,
     conduct_ref, uptake_ref,
 ):
     own, depth, width = src_in.shape
@@ -339,7 +377,8 @@
     bottom_pairs = [bottom_ref[1, z : z + 1] for z in range(depth)] + [high[2:3], high[3:4], low[3:4], low[2:3]]
     above, below = ends()
     outside = {depth: above, depth + 1: above, depth + 2: below, depth + 3: below}
-    grid = Grid(diff_ref, upt_ref, labels, top_pairs, bottom_pairs, outside, conduct_ref, uptake_ref)
+    diffs, uptakes = phase_rows(scalar_ref, 0, width), phase_rows(scalar_ref, 1, width)
+    grid = Grid(diffs, uptakes, labels, top_pairs, bottom_pairs, outside, conduct_ref, uptake_ref)
     blank = jnp.zeros((8, width), jnp.float32)
     outer = dict(zip((depth, planes - 1), from_slab(even_ref, odd_ref, SOURCE, LABELS)))
     for start in (0, 8, planes - 1, depth):
@@ -363,27 +402,34 @@
                 weight_ref[6, z, rows - 1 :] = scale[rows - 1 :] * bottom_ref[2, z : z + 1]
 
 
-def owners_of(basis_ref, base):
-    tail = basis_ref[:, base:].astype(jnp.float32)
+def rows_of(basis, start, size):
+    parts = [ref[:, start : start + size].astype(jnp.float32) for ref in basis]
+    return parts[0] if len(parts) == 1 else jnp.concatenate(parts, axis=0)
+
+
+def owners_of(basis):
+    tail = rows_of(basis, basis[0].shape[1] - 128, 128)
     return [
         (tail[:, 2 * k : 2 * k + 1] + 256.0 * tail[:, 2 * k + 1 : 2 * k + 2]).astype(jnp.int32)
         for k in range(3)
     ]
 
 
-def restrict_kernel(diff_ref, column_ref, record_ref, even_ref, odd_ref, face_ref, res_ref, basis_ref, out_ref):
+def restrict_kernel(scalar_ref, column_ref, record_ref, even_ref, odd_ref, face_ref, res_ref, *refs):
+    basis, out_ref = refs[-2::-1], refs[-1]
     depth, own, width = res_ref.shape
-    entries = basis_ref.shape[0]
+    entries = column_ref.shape[0]
     pick = column_ref[:, 0:1] == lax.broadcasted_iota(jnp.int32, (entries, own), 1)
     pick = jnp.where(pick, 1.0, 0.0).astype(jnp.bfloat16)
     values = nearest_planes(even_ref, odd_ref)
     packed = from_slab(even_ref, odd_ref, LABELS, CORNERS)
+    diffs = phase_rows(scalar_ref, 0, width)
     faces = {}
     for z, side, at in ((0, 0, 1), (depth - 1, 3, 0)):
         label = unpack_labels(packed[at], own)[0]
         beyond = jnp.zeros(label.shape, jnp.float32)
-        for phase in range(diff_ref.shape[0]):
-            beyond = jnp.where(label == float(phase), diff_ref[phase], beyond)
+        for phase, diff in enumerate(diffs):
+            beyond = jnp.where(label == float(phase), diff, beyond)
         beyond = jnp.where(ends()[at], 0.0, beyond)
         value = jnp.where(ends()[at], 0.0, values[at])
         applied = 0.5 * (face_ref[side + 1] + beyond) * (face_ref[side + 2] - value)
@@ -392,9 +438,9 @@
     for z in range(depth):
         plane = faces[z] if z in faces else res_ref[z]
         piece = jnp.dot(pick, plane, preferred_element_type=jnp.float32)
-        total = total + piece * basis_ref[:, z * width : (z + 1) * width].astype(jnp.float32)
+        total = total + piece * rows_of(basis, z * width, width)
     product = jnp.sum(total, axis=1, keepdims=True)
-    ident = owners_of(basis_ref, basis_ref.shape[1] - 128)[0]
+    ident = owners_of(basis)[0]
     copies, lines, lanes = out_ref.shape
     lane = lax.broadcasted_iota(jnp.int32, (entries, lanes), 1)
     line = lax.broadcasted_iota(jnp.int32, (8, lanes), 0)
@@ -444,20 +490,17 @@
     return state
 
 
-def prolong_kernel(
-    ids_ref, tables_ref, even_ref, odd_ref, got_ref, basis_ref, plain_ref, cor_ref, top_ref, bottom_ref,
-    correction_ref, *, nnz, depth,
-):
+def prolong_kernel(scalar_ref, tables_ref, even_ref, odd_ref, got_ref, plain_ref, *refs, nnz):
+    basis = refs[-5::-1]
+    cor_ref, top_ref, bottom_ref, correction_ref = refs[-4:]
     planes, own, width = cor_ref.shape
+    depth = plain_ref.shape[0]
     entries = tables_ref.shape[1]
-    cells = ids_ref.shape[0]
+    cells = correction_ref.shape[1]
     count = cells * got_ref.shape[0]
     state = solve(got_ref, count, nnz)
-
     line = lax.broadcasted_iota(jnp.int32, (cells, 1), 0)
-    mine = jnp.zeros((cells, 1), jnp.int32)
-    for cell in range(cells):
-        mine = jnp.where(line == cell, ids_ref[cell], mine)
+    mine = scalar_ref[2, 0, :, 0:1].astype(jnp.int32)
 
     def look_up(ident):
         hit = ident == lax.broadcasted_iota(jnp.int32, (ident.shape[0], count), 1)
@@ -473,7 +516,7 @@
     table_high, table_low = high[line : line + 1, :entries], low[line : line + 1, :entries]
     tables = (tables_ref[0:1], table_high.astype(jnp.int32), table_low.astype(jnp.int32))
     base = depth * width
-    owners = owners_of(basis_ref, basis_ref.shape[1] - 128)
+    owners = owners_of(basis)
     for group, owner in enumerate(owners):
         pick = tables[group] == lax.broadcasted_iota(jnp.int32, (own, entries), 0)
         pick = jnp.where(pick, 1.0, 0.0).astype(jnp.bfloat16)
@@ -484,7 +527,7 @@
             at = depth + 2 * (group - 1)
             places = [(at + k, base + (at + k - depth) * width) for k in range(2)]
         for z, start in places:
-            part = (basis_ref[:, start : start + width].astype(jnp.float32) * factor).astype(jnp.bfloat16)
+            part = (rows_of(basis, start, width) * factor).astype(jnp.bfloat16)
             added = jnp.dot(pick, part, preferred_element_type=jnp.float32)
             value = (plain_ref[z] if z < depth else wide[z]) + added
             cor_ref[z] = value
@@ -492,7 +535,7 @@
             bottom_ref[z] = value[own - 2 :]
 
 
-def smooth_kernel(cor_ref, top_ref, bottom_ref, weight_ref, out_ref, ext_ref, mid_ref):
+def smooth_kernel(cor_ref, top_ref, bottom_ref, weight_ref, out_hbm, ext_ref, mid_ref, out_ref, sems):
     planes, rows, width = ext_ref.shape
     own, depth, unused = out_ref.shape
     blank = jnp.zeros((8, width), jnp.float32)
@@ -519,10 +562,16 @@
 
     for z in [planes - 1] + list(range(depth + 1)):
         mid_ref[z] = sweep(ext_ref, z, rows)
+    copies = []
     for start in range(0, depth, 8):
         for z in range(start, start + 8):
             ext_ref[z, :own] = sweep(mid_ref, z, own)
         out_ref[:, start : start + 8, :] = jnp.transpose(ext_ref[start : start + 8, :own], (1, 0, 2))
+        part = pl.ds(start, 8)
+        copies.append(pltpu.make_async_copy(out_ref.at[:, part], out_hbm.at[:, part], sems.at[start // 8]))
+        copies[-1].start()
+    for copy in copies:
+        copy.wait()
 
 
 def shards(
@@ -555,42 +604,50 @@
     block = (rows, depth, width)
     table = send_tiles.reshape(slabs, capacity)
     wide = voxels + 4 * width + 128
+
+    def pinned(*arrays):
+        return [pltpu.with_memory_space_constraint(array, pltpu.HBM) for array in arrays]
+
+    direct = False
+    parts = slabs if direct else 1
     outgoing = pl.pallas_call(
         functools.partial(sort_kernel, capacity=capacity),
-        out_shape=shape((entries, wide), bf16),
+        out_shape=(shape((entries // parts, wide), bf16),) * parts,
         in_specs=[HBM] * 4,
-        out_specs=HBM,
+        out_specs=(VMEM,) * parts,
         scratch_shapes=[
             pltpu.VMEM((1, entries), i32),
             pltpu.SMEM((cells,), i32),
             pltpu.SMEM((cells,), i32),
             pltpu.VMEM((entries, voxels), bf16),
-            pltpu.VMEM((entries, wide), bf16),
-            pltpu.SemaphoreType.DMA((12,)),
+            pltpu.SemaphoreType.DMA((7,)),
         ],
-        compiler_params=params(60),
+        compiler_params=params(12),
         name="sort_basis",
     )(
-        support_slot.reshape(1, entries),
-        support_len.reshape(cells),
-        coarse_ids,
-        basis_values.reshape(entries, voxels),
+        *pinned(
+            support_slot.reshape(1, entries),
+            support_len.reshape(cells),
+            coarse_ids,
+            basis_values.reshape(entries, voxels),
+        )
     )
-    basis = lax.all_to_all(
-        outgoing.reshape(slabs, capacity, wide), "slab", split_axis=0, concat_axis=0, tiled=True
-    ).reshape(entries, wide)
-
+    if direct:
+        basis = [
+            lax.ppermute(outgoing[s], "slab", [(i, i ^ s) for i in range(slabs)]) for s in range(slabs - 1, 0, -1)
+        ] + [outgoing[0]]
+    else:
+        basis = lax.all_to_all(
+            outgoing[0].reshape(slabs, capacity, wide), "slab", split_axis=0, concat_axis=0, tiled=True
+        )
+        basis = [basis.reshape(entries, wide)]
     outgoing, solution, phase_label, source, table = lax.optimization_barrier(
         (outgoing, solution, phase_label, source, table)
     )
-
-    def pinned(*arrays):
-        return [pltpu.with_memory_space_constraint(array, pltpu.HBM) for array in arrays]
-
     message = shape((MESSAGE, width), bf16)
     edge = shape((3, depth, width), f32)
     even, odd, top, bottom = pl.pallas_call(
-        border_kernel,
+        functools.partial(border_kernel, direct=direct),
         out_shape=(message, message, edge, edge),
         in_specs=[HBM] * 4,
         out_specs=(VMEM,) * 4,
@@ -621,11 +678,12 @@
 
     wide_block = pltpu.VMEM((planes, tall, width), f32)
     operands = [
-        phase_diffusivity, phase_uptake, coarse_diag, coarse_off, coarse_cols, table,
+        phase_diffusivity, phase_uptake, coarse_diag, coarse_ids, coarse_off, coarse_cols, table,
         solution, phase_label, source, top, bottom,
     ]
-    residual, face, plain, packed, tables, column, record = pl.pallas_call(
-        residual_kernel,
+    phases = phase_diffusivity.shape[0]
+    residual, face, plain, packed, tables, column, record, scalars = pl.pallas_call(
+        functools.partial(residual_kernel, direct=direct),
         out_shape=(
             shape((depth, rows, width), bf16),
             shape((6, rows, width), f32),
@@ -634,55 +692,56 @@
             shape((8, entries), i32),
             shape((entries, 8), i32),
             shape((cells, 128), f32),
+            shape((3, phases, 8, 128), f32),
         ),
-        in_specs=[HBM] * 11,
-        out_specs=(VMEM,) * 7,
+        in_specs=[HBM] * 12,
+        out_specs=(VMEM,) * 8,
         scratch_shapes=[pltpu.VMEM((depth, tall, width), f32)] * 3
-        + [pltpu.SMEM(array.shape, array.dtype) for array in operands[:3]]
-        + [pltpu.VMEM(array.shape, array.dtype) for array in operands[3:]]
-        + [pltpu.SemaphoreType.DMA((11,))],
+        + [pltpu.SMEM(array.shape, array.dtype) for array in operands[:4]]
+        + [pltpu.VMEM(array.shape, array.dtype) for array in operands[4:]]
+        + [pltpu.SemaphoreType.DMA((12,))],
         compiler_params=params(12),
         name="residual",
-    )(*pinned(*operands[:9]), *operands[9:])
+    )(*pinned(*operands[:10]), *operands[10:])
 
     lines = max(8, count // HALF)
     payload = pl.pallas_call(
         restrict_kernel,
         out_shape=shape((devices, lines, 128), f32),
-        in_specs=[SMEM] + [VMEM] * 7,
+        in_specs=[VMEM] * (7 + parts),
         out_specs=VMEM,
         compiler_params=params(8),
         name="restrict",
-    )(phase_diffusivity, column, record, even, odd, face, residual, basis)
+    )(scalars, column, record, even, odd, face, residual, *basis)
     got = lax.all_to_all(payload, ("slab", "tile"), split_axis=0, concat_axis=0, tiled=True)
 
     edge = shape((planes, 2, width), f32)
     corrected, top, bottom, coarse_correction = pl.pallas_call(
-        functools.partial(prolong_kernel, nnz=nnz, depth=depth),
+        functools.partial(prolong_kernel, nnz=nnz),
         out_shape=(shape((planes, rows, width), f32), edge, edge, shape((1, cells), f32)),
-        in_specs=[SMEM] + [VMEM] * 6,
+        in_specs=[VMEM] * (6 + parts),
         out_specs=(VMEM, VMEM, VMEM, VMEM),
         compiler_params=params(12 + count * count // (8 * MIB)),
         name="prolong",
-    )(coarse_ids, tables, even, odd, got, basis, plain)
+    )(scalars, tables, even, odd, got, plain, *basis)
     corrected, packed = lax.optimization_barrier((corrected, packed))
     weights = pl.pallas_call(
         weigh_kernel,
         out_shape=shape((7, planes, tall, width), f32),
-        in_specs=[SMEM, SMEM] + [VMEM] * 6,
+        in_specs=[VMEM] * 7,
         out_specs=VMEM,
         scratch_shapes=[wide_block] * 2,
         compiler_params=params(12),
         name="weigh",
-    )(phase_diffusivity, phase_uptake, packed, source, even, odd, row_top, row_bottom)
+    )(scalars, packed, source, even, odd, row_top, row_bottom)
     top = lax.ppermute(top, "tile", wheel(tiles, -1))
     bottom = lax.ppermute(bottom, "tile", wheel(tiles, 1))
     smooth = pl.pallas_call(
         smooth_kernel,
         out_shape=shape((rows, depth, width), f32),
         in_specs=[VMEM] * 4,
-        out_specs=VMEM,
-        scratch_shapes=[wide_block] * 2,
+        out_specs=HBM,
+        scratch_shapes=[wide_block] * 2 + [pltpu.VMEM(block, f32), pltpu.SemaphoreType.DMA((depth // 8,))],
         compiler_params=params(16),
         name="smooth",
     )(corrected, top, bottom, weights)

time: 50 us -> 48.5 us (0.970)
  Pallas kernels: 15.2 us -> 13.4 us
  waiting for transfers between devices: 10.6 us -> 11.1 us
    ppermute x2, waiting for transfers between devices: 2.5 us -> 3.07 us  [shards(): bottom = lax.ppermute(bottom, 'tile', wheel(tiles, 1))]
    pallas_call x1, Pallas kernels: 2.48 us -> 1.92 us  [shards(): pl.pallas_call(weigh_kernel, out_shape=shape((7, planes, tall, width), f3...]
    pallas_call x1, Pallas kernels: 1 us -> 0.48 us  [shards(): pl.pallas_call(restrict_kernel, out_shape=shape((devices, lines, 128), f3...]
  transfers between devices with their start and end apart: 7 -> 7, of which waited for: 4 -> 4; matrix products, arithmetic and copies ran while one was open for 0% -> 0% of each run, Pallas kernels for 16% -> 15%
where the time goes in v4:
time: 48.5 us; the launch traced here: 48.2 us
  Pallas kernels  13.4 us (28%)
  blocking collectives  11.7 us (24%)
  starting transfers between devices  11.2 us (23%)
  waiting for transfers between devices  11.1 us (23%)
  between operations  0.72 us (1%)
    all_to_all x1, blocking collectives, shards(): lax.all_to_all(payload, ('slab', 'tile'), split_axis=0, concat_axis=0, ti...  11.7 us
    all_to_all x1, starting transfers between devices, shards(): lax.all_to_all(outgoing[0].reshape(slabs, capacity, wide), 'slab', split_...  7.26 us
    all_to_all x1, waiting for transfers between devices, shards(): lax.all_to_all(outgoing[0].reshape(slabs, capacity, wide), 'slab', split_...  6.26 us
    pallas_call x1, Pallas kernels, shards(): pl.pallas_call(functools.partial(residual_kernel, direct=direct), out_sha...  3.19 us
    ppermute x2, waiting for transfers between devices, shards(): bottom = lax.ppermute(bottom, 'tile', wheel(tiles, 1))  3.07 us
    pallas_call x1, Pallas kernels, shards(): pl.pallas_call(functools.partial(sort_kernel, capacity=capacity), out_sha...  2.61 us
    ppermute x1, starting transfers between devices, shards(): even = lax.ppermute(even, 'slab', pairs(slabs, False))  2.01 us
    pallas_call x1, Pallas kernels, shards(): pl.pallas_call(weigh_kernel, out_shape=shape((7, planes, tall, width), f3...  1.92 us
  transfers between devices with their start and end apart: 7, of which 4 were waited for; matrix products, arithmetic and copies ran while one was open for 0% of the time, Pallas kernels for 15%

profile of v4, /device:TPU:0, one launch (start us, length us, event | category | flops | bytes accessed | tf_op | source)
XLA Modules:
  0.0 48.2 jit_solution(3466675559638517925)
XLA Ops:
  0.6 0.0 copy-start
  0.6 2.6 %sort_basis.1 = bf16[64,5248]{1,0:T(8,128)(2,1)} custom-call(s32[1,64]{1,0:T(1,128)} %bitcast.12, s32[8]{0:T(128)} %bitcast.13, s32[8]{0:T(128)} %refs_3_.1, bf16[64,4096]{1,0:T(8,128)(2,1)} %bitcast.9), custom_call_target="tpu_custom_call" | custom-call | tf_op jit(solution)/shard_map/sort_basis/pallas_call | solution.py:613
  3.3 7.3 %all-to-all-start = ((bf16[8,8,5248]{2,1,0:T(8,128)(2,1)}), bf16[8,8,5248]{2,1,0:T(8,128)(2,1)S(1)}, u32[]{:S(2)}, u32[]{:S(2)}) async-start(bf16[8,8,5248]{2,1,0:T(8,128)(2,1)} %bitcast.4), calls=%async_computation | async-start | bytes 1343488 | tf_op jit(solution)/shard_map/all_to_all | solution.py:640
  10.5 1.7 %border.1 = (bf16[160,256]{1,0:T(8,128)(2,1)S(1)}, bf16[160,256]{1,0:T(8,128)(2,1)S(1)}, f32[3,16,256]{2,1,0:T(8,128)S(1)}, f32[3,16,256]{2,1,0:T(8,128)S(1)}) custom-call(f32[32,16,256]{2,1,0:T(8,128)} %refs_7_, s32[32,16,256]{2,1,0:T(8,128)} %refs_8_, f32[32,16,256]{2,1,0:T(8,128)} %src_in, s32[8,8]{1,0:T(8,128)} %bitcast.10), custom_call_target="tpu_custom_call" | custom-call | tf_op jit(solution)/shard_map/border/pallas_call | solution.py:649
  12.3 0.7 %collective-permute-start = (f32[3,16,256]{2,1,0:T(8,128)S(1)}, f32[3,16,256]{2,1,0:T(8,128)S(1)}, u32[]{:S(2)}, u32[]{:S(2)}) collective-permute-start(f32[3,16,256]{2,1,0:T(8,128)S(1)} %get-tuple-element.30), channel_id=1, source_target_pairs={{0,3},{1,0},{2,1},{3,2},{4,7},{5,4},{6,5},{7,6},{8,11},{9,8},{10,9... | collective-permute-start | bytes 147464 | tf_op jit(solution)/shard_map/ppermute | solution.py:664
  13.0 0.0 collective-permute-start.1
  13.0 1.8 %collective-permute-done.refs_10_.top_in.top_ref = f32[3,16,256]{2,1,0:T(8,128)S(1)} collective-permute-done((f32[3,16,256]{2,1,0:T(8,128)S(1)}, f32[3,16,256]{2,1,0:T(8,128)S(1)}, u32[]{:S(2)}, u32[]{:S(2)}) %collective-permute-start) | collective-permute-done | bytes 49184 | tf_op jit(solution)/shard_map/ppermute | solution.py:664
  14.8 1.7 %collective-permute-done.1.refs_11_.bottom_in.bottom_ref = f32[3,16,256]{2,1,0:T(8,128)S(1)} collective-permute-done((f32[3,16,256]{2,1,0:T(8,128)S(1)}, f32[3,16,256]{2,1,0:T(8,128)S(1)}, u32[]{:S(2)}, u32[]{:S(2)}) %collective-permute-start.1) | collective-permute-done | bytes 49184 | tf_op jit(solution)/shard_map/ppermute | solution.py:665
  16.5 0.4 corner.1
  16.9 2.0 %collective-permute-start.2 = (bf16[160,256]{1,0:T(8,128)(2,1)S(1)}, bf16[160,256]{1,0:T(8,128)(2,1)S(1)}, u32[]{:S(2)}, u32[]{:S(2)}) collective-permute-start(bf16[160,256]{1,0:T(8,128)(2,1)S(1)} %get-tuple-element.36), channel_id=1, source_target_pairs={{0,4},{4,0},{8,12},{12,8},{16,20},{20,16},{24,28},{28,24},{1,5},{5... | collective-permute-start | bytes 245768 | tf_op jit(solution)/shard_map/ppermute | solution.py:675
  18.9 0.7 %collective-permute-start.3 = (bf16[160,256]{1,0:T(8,128)(2,1)S(1)}, bf16[160,256]{1,0:T(8,128)(2,1)S(1)}, u32[]{:S(2)}, u32[]{:S(2)}) collective-permute-start(bf16[160,256]{1,0:T(8,128)(2,1)S(1)} %get-tuple-element.37), channel_id=1, source_target_pairs={{0,0},{4,8},{8,4},{12,16},{16,12},{20,24},{24,20},{28,28},{1,1},{5... | collective-permute-start | bytes 245768 | tf_op jit(solution)/shard_map/ppermute | solution.py:676
  19.6 3.2 %residual.1 = (bf16[16,32,256]{2,1,0:T(8,128)(2,1)S(1)}, f32[6,32,256]{2,1,0:T(8,128)S(1)}, f32[16,32,256]{2,1,0:T(8,128)S(1)}, f32[8,8,256]{2,1,0:T(8,128)S(1)}...) custom-call(f32[3]{0:T(128)} %refs_0_.1, f32[3]{0:T(128)} %refs_1_.1, ...), custom_call_target="tpu_custom_call" | custom-call | tf_op jit(solution)/shard_map/residual/pallas_call | solution.py:685
  22.8 0.0 collective-permute-done.2.even_ref
  22.8 0.0 collective-permute-done.3.odd_ref
  22.8 6.3 %all-to-all-done = bf16[8,8,5248]{2,1,0:T(8,128)(2,1)S(1)} async-done(((bf16[8,8,5248]{2,1,0:T(8,128)(2,1)}), bf16[8,8,5248]{2,1,0:T(8,128)(2,1)S(1)}, u32[]{:S(2)}, u32[]{:S(2)}) %all-to-all-start) | async-done | bytes 671776 | tf_op jit(solution)/shard_map/all_to_all | solution.py:640
  29.0 0.5 %restrict.1 = f32[32,8,128]{2,1,0:T(8,128)S(1)} custom-call(f32[3,3,8,128]{3,2,1,0:T(8,128)S(1)} %get-tuple-element.32.scalar_ref, s32[64,8]{1,0:T(8,128)S(1)} %get-tuple-element.38.column_ref, f32[8,128]{1,0:T(8,128)S(1)} %get-tuple-element.39.record_ref, bf16[160,256]{1,0:T(8,128)(2,1)S(1)} %collective-permute-done.2.even_ref, ...), custom_call_target="tpu_custom_call" | custom-call | tf_op jit(solution)/shard_map/restrict/pallas_call | solution.py:708
  29.5 11.7 %all_to_all.10.got_ref = f32[32,8,128]{2,1,0:T(8,128)S(1)} all-to-all(f32[32,8,128]{2,1,0:T(8,128)S(1)} %restrict.1), channel_id=1, replica_groups=mesh['slab'=8,'tile'=4] {'slab','tile'}, dimensions={0} | all-to-all | bytes 262144 | tf_op jit(solution)/shard_map/all_to_all | solution.py:716
  41.3 1.3 %prolong.1 = (f32[20,32,256]{2,1,0:T(8,128)S(1)}, f32[20,2,256]{2,1,0:T(2,128)S(1)}, f32[20,2,256]{2,1,0:T(2,128)S(1)}, f32[1,8]{1,0:T(1,128)}) custom-call(f32[3,3,8,128]{3,2,1,0:T(8,128)S(1)} %get-tuple-element.32.scalar_ref, s32[8,64]{1,0:T(8,128)S(1)} %get-tuple-element.33.tables_ref, bf16[160,256]{1,0:T(8,128)(2,1)S(1)} %collective-permute-done.2.even_ref, ...), custom_call_target="tpu_custom_call" | custom-call | tf_op jit(solution)/shard_map/prolong/pallas_call | solution.py:719
  42.6 0.2 collective-permute-start.4
  42.7 0.3 collective-permute-start.5
  43.1 0.0 copy-done
  43.1 1.9 %weigh.1.weight_ref = f32[7,20,40,256]{3,2,1,0:T(8,128)S(1)} custom-call(f32[3,3,8,128]{3,2,1,0:T(8,128)S(1)} %get-tuple-element.32.scalar_ref, f32[8,8,256]{2,1,0:T(8,128)S(1)} %get-tuple-element.48.packed_ref, f32[32,16,256]{2,1,0:T(8,128)S(1)} %copy-done, bf16[160,256]{1,0:T(8,128)(2,1)S(1)} %collective-permute-done.2.even_ref, ...), custom_call_target="tpu_custom_call" | custom-call | tf_op jit(solution)/shard_map/weigh/pallas_call | solution.py:728
  45.0 0.0 collective-permute-done.4.top_ref
  45.0 1.4 %collective-permute-done.5.bottom_ref = f32[20,2,256]{2,1,0:T(2,128)S(1)} collective-permute-done((f32[20,2,256]{2,1,0:T(2,128)S(1)}, f32[20,2,256]{2,1,0:T(2,128)S(1)}, u32[]{:S(2)}, u32[]{:S(2)}) %collective-permute-start.5) | collective-permute-done | bytes 40992 | tf_op jit(solution)/shard_map/ppermute | solution.py:738
  46.4 1.8 %smooth.1 = f32[32,16,256]{2,1,0:T(8,128)} custom-call(f32[20,32,256]{2,1,0:T(8,128)S(1)} %get-tuple-element.45.cor_ref, f32[20,2,256]{2,1,0:T(2,128)S(1)} %collective-permute-done.4.top_ref, f32[20,2,256]{2,1,0:T(2,128)S(1)} %collective-permute-done.5.bottom_ref, f32[7,20,40,256]{3,2,1,0:T(8,128)S(1)} %weigh.1.weight_ref), custom_call_target="tpu_custom_call" | custom-call | tf_op jit(solution)/shard_map/smooth/pallas_call | solution.py:739
Async XLA Ops:
  0.6 42.5 %copy-start = (f32[32,16,256]{2,1,0:T(8,128)S(1)}, f32[32,16,256]{2,1,0:T(8,128)}, u32[]{:S(2)}) copy-start(f32[32,16,256]{2,1,0:T(8,128)} %src_in) | copy-start | bytes 1572868
  3.3 25.8 %all-to-all-start = ((bf16[8,8,5248]{2,1,0:T(8,128)(2,1)}), bf16[8,8,5248]{2,1,0:T(8,128)(2,1)S(1)}, u32[]{:S(2)}, u32[]{:S(2)}) async-start(bf16[8,8,5248]{2,1,0:T(8,128)(2,1)} %bitcast.4), calls=%async_computation | async-start | bytes 1343488 | tf_op jit(solution)/shard_map/all_to_all | solution.py:640
  12.3 2.5 %collective-permute-start = (f32[3,16,256]{2,1,0:T(8,128)S(1)}, f32[3,16,256]{2,1,0:T(8,128)S(1)}, u32[]{:S(2)}, u32[]{:S(2)}) collective-permute-start(f32[3,16,256]{2,1,0:T(8,128)S(1)} %get-tuple-element.30), channel_id=1, source_target_pairs={{0,3},{1,0},{2,1},{3,2},{4,7},{5,4},{6,5},{7,6},{8,11},{9,8},{10,9... | collective-permute-start | bytes 147464 | tf_op jit(solution)/shard_map/ppermute | solution.py:664
  13.0 3.5 %collective-permute-start.1 = (f32[3,16,256]{2,1,0:T(8,128)S(1)}, f32[3,16,256]{2,1,0:T(8,128)S(1)}, u32[]{:S(2)}, u32[]{:S(2)}) collective-permute-start(f32[3,16,256]{2,1,0:T(8,128)S(1)} %get-tuple-element.31), channel_id=1, source_target_pairs={{0,1},{1,2},{2,3},{3,0},{4,5},{5,6},{6,7},{7,4},{8,9},{9,10},{10,1... | collective-permute-start | bytes 147464 | tf_op jit(solution)/shard_map/ppermute | solution.py:665
  16.9 5.9 %collective-permute-start.2 = (bf16[160,256]{1,0:T(8,128)(2,1)S(1)}, bf16[160,256]{1,0:T(8,128)(2,1)S(1)}, u32[]{:S(2)}, u32[]{:S(2)}) collective-permute-start(bf16[160,256]{1,0:T(8,128)(2,1)S(1)} %get-tuple-element.36), channel_id=1, source_target_pairs={{0,4},{4,0},{8,12},{12,8},{16,20},{20,16},{24,28},{28,24},{1,5},{5... | collective-permute-start | bytes 245768 | tf_op jit(solution)/shard_map/ppermute | solution.py:675
  18.9 3.9 %collective-permute-start.3 = (bf16[160,256]{1,0:T(8,128)(2,1)S(1)}, bf16[160,256]{1,0:T(8,128)(2,1)S(1)}, u32[]{:S(2)}, u32[]{:S(2)}) collective-permute-start(bf16[160,256]{1,0:T(8,128)(2,1)S(1)} %get-tuple-element.37), channel_id=1, source_target_pairs={{0,0},{4,8},{8,4},{12,16},{16,12},{20,24},{24,20},{28,28},{1,1},{5... | collective-permute-start | bytes 245768 | tf_op jit(solution)/shard_map/ppermute | solution.py:676
  42.6 2.4 %collective-permute-start.4 = (f32[20,2,256]{2,1,0:T(2,128)S(1)}, f32[20,2,256]{2,1,0:T(2,128)S(1)}, u32[]{:S(2)}, u32[]{:S(2)}) collective-permute-start(f32[20,2,256]{2,1,0:T(2,128)S(1)} %get-tuple-element.46), channel_id=1, source_target_pairs={{0,3},{1,0},{2,1},{3,2},{4,7},{5,4},{6,5},{7,6},{8,11},{9,8},{10,9... | collective-permute-start | bytes 122888 | tf_op jit(solution)/shard_map/ppermute | solution.py:737
  42.7 3.6 %collective-permute-start.5 = (f32[20,2,256]{2,1,0:T(2,128)S(1)}, f32[20,2,256]{2,1,0:T(2,128)S(1)}, u32[]{:S(2)}, u32[]{:S(2)}) collective-permute-start(f32[20,2,256]{2,1,0:T(2,128)S(1)} %get-tuple-element.47), channel_id=1, source_target_pairs={{0,1},{1,2},{2,3},{3,0},{4,5},{5,6},{6,7},{7,4},{8,9},{9,10},{10,1... | collective-permute-start | bytes 122888 | tf_op jit(solution)/shard_map/ppermute | solution.py:738

commit v5 on v4

--- a/solution.py
+++ b/solution.py
@@ -15,9 +15,13 @@
 SMEM = pl.BlockSpec(memory_space=pltpu.SMEM)
 HBM = pl.BlockSpec(memory_space=pltpu.HBM)
 MIB = 1024 * 1024
-COLS_LANE = 32
-HALF = 64
-DIAG_LANE = 60
+HALF, SECOND, COLS, DIAG, PLACE, SUMS = 64, 16, 32, 46, 47, 48
+BASE = 4096
+
+
+def place_of(index, count):
+    row = index % 8
+    return row // 4 * (count // 2) + index // 8 * 4 + row % 4
 
 
 def params(mib=16):
@@ -46,7 +50,7 @@
     return copies
 
 
-def sort_kernel(slot_hbm, len_hbm, ids_hbm, basis_hbm, *refs, capacity):
+def sort_kernel(slot_hbm, len_hbm, ids_hbm, basis_hbm, *refs, capacity, count):
     slot_ref, len_ref, ids_ref, basis_ref, sems = refs[-5:]
     outs = refs[:-5]
     entries, voxels = basis_ref.shape
@@ -55,9 +59,9 @@
     support = entries // cells
     wide = outs[0].shape[1]
     border = (wide - 128 - voxels) // 2
-    chunk = voxels // 4
+    chunk = voxels // 2
     pieces = [
-        (basis_hbm.at[:, pl.ds(k * chunk, chunk)], basis_ref.at[:, pl.ds(k * chunk, chunk)]) for k in range(4)
+        (basis_hbm.at[:, pl.ds(k * chunk, chunk)], basis_ref.at[:, pl.ds(k * chunk, chunk)]) for k in range(2)
     ]
     small = [(slot_hbm, slot_ref), (len_hbm, len_ref), (ids_hbm, ids_ref)]
     copies = fetch(small + pieces, sems)
@@ -70,6 +74,7 @@
         here = lane // support == cell
         length = jnp.where(here, len_ref[cell], length)
         ident = jnp.where(here, ids_ref[cell], ident)
+    ident = place_of(ident, count)
     live = lane % support < length
     slot = jnp.where(live, slot_ref[...], -1)
     row = lax.broadcasted_iota(jnp.int32, (entries, entries), 0)
@@ -95,8 +100,9 @@
         low = jnp.sum(jnp.where(hit, ident % 256, 0).astype(jnp.float32), axis=1, keepdims=True)
         high = jnp.sum(jnp.where(hit, ident // 256, 0).astype(jnp.float32), axis=1, keepdims=True)
         tail = jnp.where(extra == 2 * k, low, jnp.where(extra == 2 * k + 1, high, tail))
-    put(tail, voxels + 2 * border)
-    for k in range(4):
+    cell = jnp.sum(jnp.where(hits[0], lane // support, 0).astype(jnp.float32), axis=1, keepdims=True)
+    put(jnp.where(extra == 2 * len(hits), cell, tail), voxels + 2 * border)
+    for k in range(2):
         copies[3 + k].wait()
         for start in range(k * chunk, (k + 1) * chunk, 512):
             move(picks[0], start, 512, start)
@@ -271,7 +277,7 @@
     return slab == lax.axis_size("slab") - 1, slab == 0
 
 
-def residual_kernel(*refs, direct):
+def residual_kernel(*refs, direct, count):
     operands, outputs, scratch = refs[:12], refs[12:20], refs[20:]
     conduct_ref, uptake_ref, sol_ref = scratch[:3]
     local, sems = scratch[3:15], scratch[15]
@@ -291,13 +297,20 @@
     mine = jnp.zeros(record_ref.shape, jnp.int32)
     for cell in range(cells):
         mine = jnp.where(line == cell, ids_ref[cell], mine)
-    scalar_ref[2, 0] = mine.astype(jnp.float32)
-    record = jnp.zeros(record_ref.shape, jnp.float32)
+    mine = place_of(mine, count).astype(jnp.float32)
+    scalar_ref[2, 0] = mine
+    lane = lax.broadcasted_iota(jnp.int32, record_ref.shape, 1)
+    record = jnp.where(lane == PLACE, mine, 0.0)
     for cell in range(cells):
-        record = jnp.where(line == cell, diag_ref[cell], record)
+        record = jnp.where((line == cell) & (lane == DIAG), diag_ref[cell], record)
     record_ref[...] = record
-    record_ref[:, :nnz] = off_ref[...]
-    record_ref[:, COLS_LANE : COLS_LANE + nnz] = cols_ref[...].astype(jnp.float32)
+    group = nnz // 2
+    cols = place_of(cols_ref[...], count).astype(jnp.float32)
+    record_ref[:, :group] = off_ref[:, :group]
+    record_ref[:, SECOND : SECOND + group] = off_ref[:, group:]
+    record_ref[:, COLS : COLS + group] = cols[:, :group] + float(BASE) * cols[:, group:]
+    record = record_ref[...]
+    record_ref[:4] = jnp.concatenate([record[:4, :HALF], record[4:, :HALF]], axis=1)
     slots, capacity = table_ref.shape
     entries = slots * capacity
     table = flat(table_ref[...]).astype(jnp.float32)
@@ -409,14 +422,15 @@
 
 def owners_of(basis):
     tail = rows_of(basis, basis[0].shape[1] - 128, 128)
-    return [
+    cell = tail[:, 6:7].astype(jnp.int32)
+    return cell, [
         (tail[:, 2 * k : 2 * k + 1] + 256.0 * tail[:, 2 * k + 1 : 2 * k + 2]).astype(jnp.int32)
         for k in range(3)
     ]
 
 
-def restrict_kernel(scalar_ref, column_ref, record_ref, even_ref, odd_ref, face_ref, res_ref, *refs):
-    basis, out_ref = refs[-2::-1], refs[-1]
+def restrict_kernel(scalar_ref, column_ref, record_ref, even_ref, odd_ref, face_ref, res_ref, *refs, capacity):
+    basis, out_ref = refs[:-1], refs[-1]
     depth, own, width = res_ref.shape
     entries = column_ref.shape[0]
     pick = column_ref[:, 0:1] == lax.broadcasted_iota(jnp.int32, (entries, own), 1)
@@ -440,65 +454,90 @@
         piece = jnp.dot(pick, plane, preferred_element_type=jnp.float32)
         total = total + piece * rows_of(basis, z * width, width)
     product = jnp.sum(total, axis=1, keepdims=True)
-    ident = owners_of(basis)[0]
+    cell, unused = owners_of(basis)
     copies, lines, lanes = out_ref.shape
+    peer = lax.broadcasted_iota(jnp.int32, (entries, 1), 0) // capacity
+    target = (peer // 8 * 4 + peer % 4) * lanes + peer % 8 // 4 * HALF + SUMS + cell
     lane = lax.broadcasted_iota(jnp.int32, (entries, lanes), 1)
+    rows = []
+    for line in range(lines):
+        share = jnp.sum(jnp.where(target == line * lanes + lane, product, 0.0), axis=0, keepdims=True)
+        rows.append(share + record_ref[line : line + 1] if line < 4 else share)
+    block = jnp.concatenate(rows, axis=0)
+
+    def put(copy, carry):
+        out_ref[copy] = block
+        return carry
+
+    lax.fori_loop(0, copies, put, 0, unroll=8)
+
+
+def solve(got, tiles):
+    extent, lanes = got[0].shape
+    turned = jnp.transpose(got[0][...])
+    chunks = range(0, extent, lanes)
+    owners = 4 * tiles
     line = lax.broadcasted_iota(jnp.int32, (8, lanes), 0)
-    for base in range(0, lines, 8):
-        block = record_ref[...] if base == 0 else jnp.zeros((8, lanes), jnp.float32)
-        for row in range(8):
-            share = jnp.where(ident == (base + row) * HALF + lane - HALF, product, 0.0)
-            share = jnp.sum(jnp.where(lane >= HALF, share, 0.0), axis=0, keepdims=True)
-            block = jnp.where((line == row) & (lane[:8] >= HALF), share, block)
-
-        def put(copy, carry):
-            out_ref[copy, base : base + 8, :] = block
-            return carry
-
-        lax.fori_loop(0, copies, put, 0, unroll=8)
-
-
-def solve(got_ref, count, nnz):
-    devices, lines, lanes = got_ref.shape
-    summed = got_ref[0]
-    if devices <= 64:
-        for device in range(1, devices):
-            summed = summed + got_ref[device]
-    else:
-        summed = lax.fori_loop(1, devices, lambda d, total: total + got_ref[d], summed)
-    rhs = jnp.concatenate([summed[at : at + 1, HALF:] for at in range(count // HALF)], axis=1)
-    record = jnp.transpose(got_ref[:, 0:8, :].reshape(count, lanes))
-    line = lax.broadcasted_iota(jnp.int32, (COLS_LANE, lanes), 0)
-    inverse = 1.0 / record[DIAG_LANE : DIAG_LANE + 1]
-    chunks = range(0, count, lanes)
-    values = [jnp.where(line < nnz, record[:COLS_LANE, at : at + lanes], 0.0) for at in chunks]
-    places = [
-        jnp.where(line < nnz, record[COLS_LANE : 2 * COLS_LANE, at : at + lanes], 0.0).astype(jnp.int32)
-        for at in chunks
-    ]
-    state = rhs * inverse
+    lane = lax.broadcasted_iota(jnp.int32, (8, lanes), 1)
+
+    def left(block, by):
+        return pltpu.roll(block, lanes - by, 1) if by else block
+
+    rhs = [jnp.zeros((8, lanes), jnp.float32) for at in range(2 * len(chunks))]
+    place = [lane + at * lanes for at in range(2 * len(chunks))]
+    for t, ref in enumerate(got):
+        total = ref[:owners]
+        for at in range(owners, extent, owners):
+            total = total + ref[at : at + owners]
+        block = jnp.transpose(jnp.concatenate([total] * (lanes // owners), axis=0))
+        value = jnp.zeros((8, lanes), jnp.float32)
+        ident = jnp.zeros((8, lanes), jnp.float32)
+        for half in range(2):
+            total = block[half * HALF + SUMS : half * HALF + SUMS + 8]
+            row = half * HALF + PLACE
+            places = jnp.broadcast_to(turned[row : row + 1, t * lanes : (t + 1) * lanes], (8, lanes))
+            for i in range(4):
+                value = jnp.where(lane // owners == 4 * half + i, left(total, i), value)
+                ident = jnp.where(line == 4 * half + i, left(places, i), ident)
+        ident = ident.astype(jnp.int32)
+        for at in range(0, lanes, 4):
+            here, amount = ident[:, at : at + 1], value[:, at : at + 1]
+            rhs = [total + jnp.where(here == spot, amount, 0.0) for total, spot in zip(rhs, place)]
+    rhs = [jnp.sum(total, axis=0, keepdims=True) for total in rhs]
+
+    values, places, inverse = [], [], []
+    for half in range(2):
+        for at in chunks:
+            block = turned[half * HALF : (half + 1) * HALF, at : at + lanes]
+            values.append(block[:COLS])
+            packed = block[COLS : COLS + SECOND]
+            second = jnp.floor(packed * (1.0 / BASE))
+            first = packed - float(BASE) * second
+            places.append(jnp.concatenate([first, second], axis=0).astype(jnp.int32) % (2 * extent))
+            inverse.append(1.0 / block[DIAG : DIAG + 1])
+    state = [total * factor for total, factor in zip(rhs, inverse)]
     for repeat in range(COARSE_SWEEPS - 1):
-        sources = [jnp.broadcast_to(state[:, at : at + lanes], (COLS_LANE, lanes)) for at in chunks]
-        pulled = []
-        for value, place in zip(values, places):
-            found = jnp.zeros((COLS_LANE, lanes), jnp.float32)
+        sources = [jnp.broadcast_to(part, (COLS, lanes)) for part in state]
+        new = []
+        for total, factor, value, spot in zip(rhs, inverse, values, places):
+            found = jnp.zeros((COLS, lanes), jnp.float32)
             for k, source in enumerate(sources):
-                taken = jnp.take_along_axis(source, place % lanes, axis=1, mode="promise_in_bounds")
-                found = jnp.where(place // lanes == k, taken, found)
-            pulled.append(jnp.sum(value * found, axis=0, keepdims=True))
-        state = (rhs - jnp.concatenate(pulled, axis=1)) * inverse
-    return state
-
-
-def prolong_kernel(scalar_ref, tables_ref, even_ref, odd_ref, got_ref, plain_ref, *refs, nnz):
-    basis = refs[-5::-1]
+                taken = jnp.take_along_axis(source, spot % lanes, axis=1, mode="promise_in_bounds")
+                found = jnp.where(spot // lanes == k, taken, found)
+            new.append((total - jnp.sum(value * found, axis=0, keepdims=True)) * factor)
+        state = new
+    return jnp.concatenate(state, axis=1)
+
+
+def prolong_kernel(scalar_ref, tables_ref, even_ref, odd_ref, plain_ref, *refs, groups):
+    got, basis = refs[:groups], refs[groups:-4]
     cor_ref, top_ref, bottom_ref, correction_ref = refs[-4:]
     planes, own, width = cor_ref.shape
     depth = plain_ref.shape[0]
     entries = tables_ref.shape[1]
     cells = correction_ref.shape[1]
-    count = cells * got_ref.shape[0]
-    state = solve(got_ref, count, nnz)
+    count = 2 * got[0].shape[0]
+    state = solve(got, lax.axis_size("tile"))
     line = lax.broadcasted_iota(jnp.int32, (cells, 1), 0)
     mine = scalar_ref[2, 0, :, 0:1].astype(jnp.int32)
 
@@ -516,7 +555,7 @@
     table_high, table_low = high[line : line + 1, :entries], low[line : line + 1, :entries]
     tables = (tables_ref[0:1], table_high.astype(jnp.int32), table_low.astype(jnp.int32))
     base = depth * width
-    owners = owners_of(basis)
+    unused, owners = owners_of(basis)
     for group, owner in enumerate(owners):
         pick = tables[group] == lax.broadcasted_iota(jnp.int32, (own, entries), 0)
         pick = jnp.where(pick, 1.0, 0.0).astype(jnp.bfloat16)
@@ -611,7 +650,7 @@
     direct = False
     parts = slabs if direct else 1
     outgoing = pl.pallas_call(
-        functools.partial(sort_kernel, capacity=capacity),
+        functools.partial(sort_kernel, capacity=capacity, count=count),
         out_shape=(shape((entries // parts, wide), bf16),) * parts,
         in_specs=[HBM] * 4,
         out_specs=(VMEM,) * parts,
@@ -683,7 +722,7 @@
     ]
     phases = phase_diffusivity.shape[0]
     residual, face, plain, packed, tables, column, record, scalars = pl.pallas_call(
-        functools.partial(residual_kernel, direct=direct),
+        functools.partial(residual_kernel, direct=direct, count=count),
         out_shape=(
             shape((depth, rows, width), bf16),
             shape((6, rows, width), f32),
@@ -704,9 +743,10 @@
         name="residual",
     )(*pinned(*operands[:10]), *operands[10:])
 
-    lines = max(8, count // HALF)
+    groups = max(1, slabs // 8)
+    lines = 4 * groups
     payload = pl.pallas_call(
-        restrict_kernel,
+        functools.partial(restrict_kernel, capacity=capacity),
         out_shape=shape((devices, lines, 128), f32),
         in_specs=[VMEM] * (7 + parts),
         out_specs=VMEM,
@@ -714,16 +754,17 @@
         name="restrict",
     )(scalars, column, record, even, odd, face, residual, *basis)
     got = lax.all_to_all(payload, ("slab", "tile"), split_axis=0, concat_axis=0, tiled=True)
+    got = [got[:, 4 * t : 4 * t + 4].reshape(4 * devices, 128) for t in range(groups)]
 
     edge = shape((planes, 2, width), f32)
     corrected, top, bottom, coarse_correction = pl.pallas_call(
-        functools.partial(prolong_kernel, nnz=nnz),
+        functools.partial(prolong_kernel, groups=groups),
         out_shape=(shape((planes, rows, width), f32), edge, edge, shape((1, cells), f32)),
-        in_specs=[VMEM] * (6 + parts),
+        in_specs=[VMEM] * (5 + groups + parts),
         out_specs=(VMEM, VMEM, VMEM, VMEM),
-        compiler_params=params(12 + count * count // (8 * MIB)),
+        compiler_params=params(12 + count // 128),
         name="prolong",
-    )(scalars, tables, even, odd, got, plain, *basis)
+    )(scalars, tables, even, odd, plain, *got, *basis)
     corrected, packed = lax.optimization_barrier((corrected, packed))
     weights = pl.pallas_call(
         weigh_kernel,

time: 48.5 us -> 47.7 us (0.984)
  blocking collectives: 11.7 us -> 10.9 us
    all_to_all x1, blocking collectives: 11.7 us -> 10.9 us  [shards(): lax.all_to_all(payload, ('slab', 'tile'), split_axis=0, concat_axis=0, ti...]
where the time goes in v5:
time: 47.7 us; the launch traced here: 47.4 us
  Pallas kernels  13.4 us (28%)
  starting transfers between devices  11.2 us (23%)
  waiting for transfers between devices  11.2 us (23%)
  blocking collectives  10.9 us (23%)
  between operations  0.72 us (2%)
    all_to_all x1, blocking collectives, shards(): lax.all_to_all(payload, ('slab', 'tile'), split_axis=0, concat_axis=0, ti...  10.9 us
    all_to_all x1, starting transfers between devices, shards(): lax.all_to_all(outgoing[0].reshape(slabs, capacity, wide), 'slab', split_...  7.26 us
    all_to_all x1, waiting for transfers between devices, shards(): lax.all_to_all(outgoing[0].reshape(slabs, capacity, wide), 'slab', split_...  6.26 us
    pallas_call x1, Pallas kernels, shards(): pl.pallas_call(functools.partial(residual_kernel, direct=direct, count=co...  3.21 us
    ppermute x2, waiting for transfers between devices, shards(): bottom = lax.ppermute(bottom, 'tile', wheel(tiles, 1))  3.14 us
    pallas_call x1, Pallas kernels, shards(): pl.pallas_call(functools.partial(sort_kernel, capacity=capacity, count=co...  2.39 us
    ppermute x1, starting transfers between devices, shards(): even = lax.ppermute(even, 'slab', pairs(slabs, False))  2.01 us
    pallas_call x1, Pallas kernels, shards(): pl.pallas_call(weigh_kernel, out_shape=shape((7, planes, tall, width), f3...  1.92 us
  transfers between devices with their start and end apart: 7, of which 4 were waited for; matrix products, arithmetic and copies ran while one was open for 0% of the time, Pallas kernels for 15%

profile of v5, /device:TPU:0, one launch (start us, length us, event | category | flops | bytes accessed | tf_op | source)
XLA Modules:
  0.0 47.4 jit_solution(2394859228502380303)
XLA Ops:
  0.6 0.0 copy-start
  0.6 2.4 %sort_basis.1 = bf16[64,5248]{1,0:T(8,128)(2,1)} custom-call(s32[1,64]{1,0:T(1,128)} %bitcast.14, s32[8]{0:T(128)} %bitcast.15, s32[8]{0:T(128)} %refs_3_.1, bf16[64,4096]{1,0:T(8,128)(2,1)} %bitcast.11), custom_call_target="tpu_custom_call" | custom-call | tf_op jit(solution)/shard_map/sort_basis/pallas_call | solution.py:652
  3.0 7.3 %all-to-all-start = ((bf16[8,8,5248]{2,1,0:T(8,128)(2,1)}), bf16[8,8,5248]{2,1,0:T(8,128)(2,1)S(1)}, u32[]{:S(2)}, u32[]{:S(2)}) async-start(bf16[8,8,5248]{2,1,0:T(8,128)(2,1)} %bitcast.4), calls=%async_computation | async-start | bytes 1343488 | tf_op jit(solution)/shard_map/all_to_all | solution.py:679
  10.3 1.7 %border.1 = (bf16[160,256]{1,0:T(8,128)(2,1)S(1)}, bf16[160,256]{1,0:T(8,128)(2,1)S(1)}, f32[3,16,256]{2,1,0:T(8,128)S(1)}, f32[3,16,256]{2,1,0:T(8,128)S(1)}) custom-call(f32[32,16,256]{2,1,0:T(8,128)} %refs_7_, s32[32,16,256]{2,1,0:T(8,128)} %refs_8_, f32[32,16,256]{2,1,0:T(8,128)} %src_in, s32[8,8]{1,0:T(8,128)} %bitcast.12), custom_call_target="tpu_custom_call" | custom-call | tf_op jit(solution)/shard_map/border/pallas_call | solution.py:688
  12.0 0.7 %collective-permute-start = (f32[3,16,256]{2,1,0:T(8,128)S(1)}, f32[3,16,256]{2,1,0:T(8,128)S(1)}, u32[]{:S(2)}, u32[]{:S(2)}) collective-permute-start(f32[3,16,256]{2,1,0:T(8,128)S(1)} %get-tuple-element.30), channel_id=1, source_target_pairs={{0,3},{1,0},{2,1},{3,2},{4,7},{5,4},{6,5},{7,6},{8,11},{9,8},{10,9... | collective-permute-start | bytes 147464 | tf_op jit(solution)/shard_map/ppermute | solution.py:703
  12.8 0.0 collective-permute-start.1
  12.8 1.8 %collective-permute-done.refs_10_.top_in.top_ref = f32[3,16,256]{2,1,0:T(8,128)S(1)} collective-permute-done((f32[3,16,256]{2,1,0:T(8,128)S(1)}, f32[3,16,256]{2,1,0:T(8,128)S(1)}, u32[]{:S(2)}, u32[]{:S(2)}) %collective-permute-start) | collective-permute-done | bytes 49184 | tf_op jit(solution)/shard_map/ppermute | solution.py:703
  14.6 1.7 %collective-permute-done.1.refs_11_.bottom_in.bottom_ref = f32[3,16,256]{2,1,0:T(8,128)S(1)} collective-permute-done((f32[3,16,256]{2,1,0:T(8,128)S(1)}, f32[3,16,256]{2,1,0:T(8,128)S(1)}, u32[]{:S(2)}, u32[]{:S(2)}) %collective-permute-start.1) | collective-permute-done | bytes 49184 | tf_op jit(solution)/shard_map/ppermute | solution.py:704
  16.3 0.4 corner.1
  16.7 2.0 %collective-permute-start.2 = (bf16[160,256]{1,0:T(8,128)(2,1)S(1)}, bf16[160,256]{1,0:T(8,128)(2,1)S(1)}, u32[]{:S(2)}, u32[]{:S(2)}) collective-permute-start(bf16[160,256]{1,0:T(8,128)(2,1)S(1)} %get-tuple-element.36), channel_id=1, source_target_pairs={{0,4},{4,0},{8,12},{12,8},{16,20},{20,16},{24,28},{28,24},{1,5},{5... | collective-permute-start | bytes 245768 | tf_op jit(solution)/shard_map/ppermute | solution.py:714
  18.7 0.7 %collective-permute-start.3 = (bf16[160,256]{1,0:T(8,128)(2,1)S(1)}, bf16[160,256]{1,0:T(8,128)(2,1)S(1)}, u32[]{:S(2)}, u32[]{:S(2)}) collective-permute-start(bf16[160,256]{1,0:T(8,128)(2,1)S(1)} %get-tuple-element.37), channel_id=1, source_target_pairs={{0,0},{4,8},{8,4},{12,16},{16,12},{20,24},{24,20},{28,28},{1,1},{5... | collective-permute-start | bytes 245768 | tf_op jit(solution)/shard_map/ppermute | solution.py:715
  19.3 3.2 %residual.1 = (bf16[16,32,256]{2,1,0:T(8,128)(2,1)S(1)}, f32[6,32,256]{2,1,0:T(8,128)S(1)}, f32[16,32,256]{2,1,0:T(8,128)S(1)}, f32[8,8,256]{2,1,0:T(8,128)S(1)}...) custom-call(f32[3]{0:T(128)} %refs_0_.1, f32[3]{0:T(128)} %refs_1_.1, ...), custom_call_target="tpu_custom_call" | custom-call | tf_op jit(solution)/shard_map/residual/pallas_call | solution.py:724
  22.6 0.0 collective-permute-done.2.even_ref
  22.6 0.0 collective-permute-done.3.odd_ref
  22.6 6.3 %all-to-all-done = bf16[8,8,5248]{2,1,0:T(8,128)(2,1)S(1)} async-done(((bf16[8,8,5248]{2,1,0:T(8,128)(2,1)}), bf16[8,8,5248]{2,1,0:T(8,128)(2,1)S(1)}, u32[]{:S(2)}, u32[]{:S(2)}) %all-to-all-start) | async-done | bytes 671776 | tf_op jit(solution)/shard_map/all_to_all | solution.py:679
  28.8 0.5 restrict.1
  29.3 10.9 %all_to_all.10 = f32[32,4,128]{2,1,0:T(4,128)S(1)} all-to-all(f32[32,4,128]{2,1,0:T(4,128)S(1)} %restrict.1), channel_id=1, replica_groups=mesh['slab'=8,'tile'=4] {'slab','tile'}, dimensions={0} | all-to-all | bytes 131072 | tf_op jit(solution)/shard_map/all_to_all | solution.py:756
  40.2 1.5 %prolong.1 = (f32[20,32,256]{2,1,0:T(8,128)S(1)}, f32[20,2,256]{2,1,0:T(2,128)S(1)}, f32[20,2,256]{2,1,0:T(2,128)S(1)}, f32[1,8]{1,0:T(1,128)}) custom-call(f32[3,3,8,128]{3,2,1,0:T(8,128)S(1)} %get-tuple-element.32.scalar_ref, s32[8,64]{1,0:T(8,128)S(1)} %get-tuple-element.33.tables_ref, bf16[160,256]{1,0:T(8,128)(2,1)S(1)} %collective-permute-done.2.even_ref, ...), custom_call_target="tpu_custom_call" | custom-call | tf_op jit(solution)/shard_map/prolong/pallas_call | solution.py:760
  41.7 0.2 collective-permute-start.4
  41.9 0.4 collective-permute-start.5
  42.3 0.0 copy-done
  42.3 1.9 %weigh.1.weight_ref = f32[7,20,40,256]{3,2,1,0:T(8,128)S(1)} custom-call(f32[3,3,8,128]{3,2,1,0:T(8,128)S(1)} %get-tuple-element.32.scalar_ref, f32[8,8,256]{2,1,0:T(8,128)S(1)} %get-tuple-element.48.packed_ref, f32[32,16,256]{2,1,0:T(8,128)S(1)} %copy-done, bf16[160,256]{1,0:T(8,128)(2,1)S(1)} %collective-permute-done.2.even_ref, ...), custom_call_target="tpu_custom_call" | custom-call | tf_op jit(solution)/shard_map/weigh/pallas_call | solution.py:769
  44.2 0.0 collective-permute-done.4.top_ref
  44.2 1.4 %collective-permute-done.5.bottom_ref = f32[20,2,256]{2,1,0:T(2,128)S(1)} collective-permute-done((f32[20,2,256]{2,1,0:T(2,128)S(1)}, f32[20,2,256]{2,1,0:T(2,128)S(1)}, u32[]{:S(2)}, u32[]{:S(2)}) %collective-permute-start.5) | collective-permute-done | bytes 40992 | tf_op jit(solution)/shard_map/ppermute | solution.py:779
  45.6 1.8 %smooth.1 = f32[32,16,256]{2,1,0:T(8,128)} custom-call(f32[20,32,256]{2,1,0:T(8,128)S(1)} %get-tuple-element.45.cor_ref, f32[20,2,256]{2,1,0:T(2,128)S(1)} %collective-permute-done.4.top_ref, f32[20,2,256]{2,1,0:T(2,128)S(1)} %collective-permute-done.5.bottom_ref, f32[7,20,40,256]{3,2,1,0:T(8,128)S(1)} %weigh.1.weight_ref), custom_call_target="tpu_custom_call" | custom-call | tf_op jit(solution)/shard_map/smooth/pallas_call | solution.py:780
Async XLA Ops:
  0.6 41.6 %copy-start = (f32[32,16,256]{2,1,0:T(8,128)S(1)}, f32[32,16,256]{2,1,0:T(8,128)}, u32[]{:S(2)}) copy-start(f32[32,16,256]{2,1,0:T(8,128)} %src_in) | copy-start | bytes 1572868
  3.0 25.8 %all-to-all-start = ((bf16[8,8,5248]{2,1,0:T(8,128)(2,1)}), bf16[8,8,5248]{2,1,0:T(8,128)(2,1)S(1)}, u32[]{:S(2)}, u32[]{:S(2)}) async-start(bf16[8,8,5248]{2,1,0:T(8,128)(2,1)} %bitcast.4), calls=%async_computation | async-start | bytes 1343488 | tf_op jit(solution)/shard_map/all_to_all | solution.py:679
  12.0 2.5 %collective-permute-start = (f32[3,16,256]{2,1,0:T(8,128)S(1)}, f32[3,16,256]{2,1,0:T(8,128)S(1)}, u32[]{:S(2)}, u32[]{:S(2)}) collective-permute-start(f32[3,16,256]{2,1,0:T(8,128)S(1)} %get-tuple-element.30), channel_id=1, source_target_pairs={{0,3},{1,0},{2,1},{3,2},{4,7},{5,4},{6,5},{7,6},{8,11},{9,8},{10,9... | collective-permute-start | bytes 147464 | tf_op jit(solution)/shard_map/ppermute | solution.py:703
  12.8 3.5 %collective-permute-start.1 = (f32[3,16,256]{2,1,0:T(8,128)S(1)}, f32[3,16,256]{2,1,0:T(8,128)S(1)}, u32[]{:S(2)}, u32[]{:S(2)}) collective-permute-start(f32[3,16,256]{2,1,0:T(8,128)S(1)} %get-tuple-element.31), channel_id=1, source_target_pairs={{0,1},{1,2},{2,3},{3,0},{4,5},{5,6},{6,7},{7,4},{8,9},{9,10},{10,1... | collective-permute-start | bytes 147464 | tf_op jit(solution)/shard_map/ppermute | solution.py:704
  16.7 5.9 %collective-permute-start.2 = (bf16[160,256]{1,0:T(8,128)(2,1)S(1)}, bf16[160,256]{1,0:T(8,128)(2,1)S(1)}, u32[]{:S(2)}, u32[]{:S(2)}) collective-permute-start(bf16[160,256]{1,0:T(8,128)(2,1)S(1)} %get-tuple-element.36), channel_id=1, source_target_pairs={{0,4},{4,0},{8,12},{12,8},{16,20},{20,16},{24,28},{28,24},{1,5},{5... | collective-permute-start | bytes 245768 | tf_op jit(solution)/shard_map/ppermute | solution.py:714
  18.7 3.9 %collective-permute-start.3 = (bf16[160,256]{1,0:T(8,128)(2,1)S(1)}, bf16[160,256]{1,0:T(8,128)(2,1)S(1)}, u32[]{:S(2)}, u32[]{:S(2)}) collective-permute-start(bf16[160,256]{1,0:T(8,128)(2,1)S(1)} %get-tuple-element.37), channel_id=1, source_target_pairs={{0,0},{4,8},{8,4},{12,16},{16,12},{20,24},{24,20},{28,28},{1,1},{5... | collective-permute-start | bytes 245768 | tf_op jit(solution)/shard_map/ppermute | solution.py:715
  41.7 2.4 %collective-permute-start.4 = (f32[20,2,256]{2,1,0:T(2,128)S(1)}, f32[20,2,256]{2,1,0:T(2,128)S(1)}, u32[]{:S(2)}, u32[]{:S(2)}) collective-permute-start(f32[20,2,256]{2,1,0:T(2,128)S(1)} %get-tuple-element.46), channel_id=1, source_target_pairs={{0,3},{1,0},{2,1},{3,2},{4,7},{5,4},{6,5},{7,6},{8,11},{9,8},{10,9... | collective-permute-start | bytes 122888 | tf_op jit(solution)/shard_map/ppermute | solution.py:778
  41.9 3.7 %collective-permute-start.5 = (f32[20,2,256]{2,1,0:T(2,128)S(1)}, f32[20,2,256]{2,1,0:T(2,128)S(1)}, u32[]{:S(2)}, u32[]{:S(2)}) collective-permute-start(f32[20,2,256]{2,1,0:T(2,128)S(1)} %get-tuple-element.47), channel_id=1, source_target_pairs={{0,1},{1,2},{2,3},{3,0},{4,5},{5,6},{6,7},{7,4},{8,9},{9,10},{10,1... | collective-permute-start | bytes 122888 | tf_op jit(solution)/shard_map/ppermute | solution.py:779

commit v6 on v5

--- a/solution.py
+++ b/solution.py
@@ -28,16 +28,43 @@
     return pltpu.CompilerParams(vmem_limit_bytes=mib * MIB)
 
 
-def wheel(count, step):
-    return [(i, (i + step) % count) for i in range(count)]
-
-
 def pairs(count, odd):
-    start = 1 if odd else 0
-    table = list(range(count))
-    for i in range(start, count - 1, 2):
-        table[i], table[i + 1] = i + 1, i
-    return list(enumerate(table))
+    shift = 1 if odd else 0
+    return [(i, ((i - shift) ^ 1) + shift) if i - shift >= 0 else (i, count - 1) for i in range(count)]
+
+
+def closed(table, count):
+    return [(source, target % count) for source, target in table]
+
+
+def along_tile(message, odd):
+    tiles = lax.axis_size("tile")
+    return lax.ppermute(message, "tile", closed(pairs(tiles, odd), tiles))
+
+
+def along_slab(message, odd):
+    slabs, tiles = lax.axis_size("slab"), lax.axis_size("tile")
+    table = []
+    for source, target in closed(pairs(slabs, odd), slabs):
+        inside = abs(source - target) == 1
+        for tile in range(tiles):
+            to = target * tiles + tile if inside else source * tiles + (tile ^ 1)
+            table.append((source * tiles + tile, to))
+    return lax.ppermute(message, ("slab", "tile"), table)
+
+
+class Either:
+    def __init__(self, flag, yes, no):
+        self.flag, self.yes, self.no = flag, yes, no
+        self.shape = yes.shape
+
+    def __getitem__(self, at):
+        return jnp.where(self.flag, self.yes[at], self.no[at])
+
+
+def from_tile(even_ref, odd_ref):
+    odd = lax.axis_index("tile") % 2 == 1
+    return Either(odd, odd_ref, even_ref), Either(odd, even_ref, odd_ref)
 
 
 def fetch(pairs_of_refs, sems):
@@ -51,13 +78,11 @@
 
 
 def sort_kernel(slot_hbm, len_hbm, ids_hbm, basis_hbm, *refs, capacity, count):
-    slot_ref, len_ref, ids_ref, basis_ref, sems = refs[-5:]
-    outs = refs[:-5]
+    out_hbm, slot_ref, len_ref, ids_ref, basis_ref, out_ref, sems = refs
     entries, voxels = basis_ref.shape
-    lines = entries // len(outs)
     cells = len_ref.shape[0]
     support = entries // cells
-    wide = outs[0].shape[1]
+    wide = out_ref.shape[1]
     border = (wide - 128 - voxels) // 2
     chunk = voxels // 2
     pieces = [
@@ -78,17 +103,19 @@
     live = lane % support < length
     slot = jnp.where(live, slot_ref[...], -1)
     row = lax.broadcasted_iota(jnp.int32, (entries, entries), 0)
-    if len(outs) > 1:
-        row = row ^ (lax.axis_index("slab") * capacity)
     above = jnp.where(row >= entries - capacity, row + capacity - entries, row + capacity)
     below = jnp.where(row < capacity, row - capacity + entries, row - capacity)
     hits = [slot == row, slot == above, slot == below]
     picks = [jnp.where(hit, 1.0, 0.0).astype(jnp.bfloat16) for hit in hits]
 
     def put(block, start):
-        for k, out in enumerate(outs):
-            part = block[k * lines : (k + 1) * lines]
-            out[:, start : start + block.shape[1]] = part.astype(jnp.bfloat16)
+        out_ref[:, start : start + block.shape[1]] = block.astype(jnp.bfloat16)
+
+    def send(k, start, size):
+        part = pl.ds(start, size)
+        copy = pltpu.make_async_copy(out_ref.at[:, part], out_hbm.at[:, part], sems.at[len(copies) + k])
+        copy.start()
+        return copy
 
     def move(pick, start, size, target):
         block = basis_ref[:, start : start + size]
@@ -107,20 +134,11 @@
         for start in range(k * chunk, (k + 1) * chunk, 512):
             move(picks[0], start, 512, start)
         if k == 0:
+            sent = send(0, 0, chunk)
             move(picks[1], 0, border, voxels)
     move(picks[2], voxels - border, border, voxels + border)
-
-
-def shuffle(table, slab, slots, capacity):
-    lane = lax.broadcasted_iota(jnp.int32, table.shape, 1)
-    size = table.shape[1]
-    bit = 1
-    while bit < slots:
-        shift = bit * capacity
-        other = jnp.where((lane // shift) % 2 == 1, pltpu.roll(table, shift, 1), pltpu.roll(table, size - shift, 1))
-        table = jnp.where((slab // bit) % 2 == 1, other, table)
-        bit *= 2
-    return table
+    send(1, chunk, wide - chunk).wait()
+    sent.wait()
 
 
 LOW, FAR, SOURCE, LABELS, CORNERS, TABLE = 32, 64, 96, 128, 144, 148
@@ -128,8 +146,8 @@
 
 
 def border_kernel(
-    sol_hbm, label_hbm, src_hbm, table_hbm, even_ref, odd_ref, top_ref, bottom_ref,
-    sol_ref, label_ref, src_ref, table_ref, sems, *, direct,
+    sol_hbm, label_hbm, src_hbm, table_hbm, even_ref, odd_ref, row_even_ref, row_odd_ref,
+    sol_ref, label_ref, src_ref, table_ref, sems,
 ):
     rows, depth, width = sol_ref.shape
     blocks = ((sol_hbm, sol_ref), (label_hbm, label_ref), (src_hbm, src_ref), (table_hbm, table_ref))
@@ -149,15 +167,10 @@
     slots, capacity = table_ref.shape
     table = flat(table_ref[...]).astype(jnp.float32)
     table = jnp.concatenate([table, jnp.zeros((1, width - table.shape[1]), jnp.float32)], axis=1)
-    tables = [table, table]
-    if direct:
-        slab, slabs = lax.axis_index("slab"), lax.axis_size("slab")
-        tables = [shuffle(table, (slab + step) % slabs, slots, capacity) for step in (1, slabs - 1)]
     line = lax.broadcasted_iota(jnp.int32, (16, width), 0) + CORNERS
-    up = up + (jnp.where(line == TABLE, tables[0], 0.0),)
-    down = down + (jnp.where(line == TABLE, tables[1], 0.0),)
+    table = jnp.where(line == TABLE, table, 0.0)
     for first, second, ref in ((up, down, even_ref), (down, up, odd_ref)):
-        near, far, origin, labels, table = [jnp.where(odd, b, a) for a, b in zip(first, second)]
+        near, far, origin, labels = [jnp.where(odd, b, a) for a, b in zip(first, second)]
         high = near.astype(jnp.bfloat16)
         ref[:LOW] = high
         ref[LOW:FAR] = (near - high.astype(jnp.float32)).astype(jnp.bfloat16)
@@ -165,10 +178,14 @@
         ref[SOURCE:LABELS] = origin.astype(jnp.bfloat16)
         ref[LABELS:CORNERS] = labels.astype(jnp.bfloat16)
         ref[CORNERS:] = table.astype(jnp.bfloat16)
-    for ref, near, far in ((top_ref, 0, 1), (bottom_ref, rows - 1, rows - 2)):
-        ref[0] = sol_ref[near]
-        ref[1] = (label_ref[near] + 3 * label_ref[far]).astype(jnp.float32)
-        ref[2] = src_ref[near]
+    first, last = [
+        (sol_ref[near], (label_ref[near] + 3 * label_ref[far]).astype(jnp.float32), src_ref[near])
+        for near, far in ((0, 1), (rows - 1, rows - 2))
+    ]
+    odd = lax.axis_index("tile") % 2 == 1
+    for k in range(3):
+        row_even_ref[k] = jnp.where(odd, first[k], last[k])
+        row_odd_ref[k] = jnp.where(odd, last[k], first[k])
 
 
 def flat(table):
@@ -208,9 +225,11 @@
     return upper[0] + lower[0], upper[1] + lower[1]
 
 
-def corner_kernel(even_in, odd_in, top_in, bottom_in, even_ref, odd_ref, top_ref, bottom_ref, sems):
-    for copy in fetch([(even_in, even_ref), (odd_in, odd_ref), (top_in, top_ref), (bottom_in, bottom_ref)], sems):
+def corner_kernel(even_in, odd_in, row_even, row_odd, even_ref, odd_ref, row_even_ref, row_odd_ref, sems):
+    moves = [(even_in, even_ref), (odd_in, odd_ref), (row_even, row_even_ref), (row_odd, row_odd_ref)]
+    for copy in fetch(moves, sems):
         copy.wait()
+    top_ref, bottom_ref = from_tile(row_even_ref, row_odd_ref)
     depth, width = top_ref.shape[1:]
     odd = lax.axis_index("slab") % 2 == 1
     line = lax.broadcasted_iota(jnp.int32, (16, width), 0)
@@ -277,12 +296,13 @@
     return slab == lax.axis_size("slab") - 1, slab == 0
 
 
-def residual_kernel(*refs, direct, count):
+def residual_kernel(*refs, count):
     operands, outputs, scratch = refs[:12], refs[12:20], refs[20:]
     conduct_ref, uptake_ref, sol_ref = scratch[:3]
     local, sems = scratch[3:15], scratch[15]
     diff_ref, upt_ref, diag_ref, ids_ref = local[:4]
-    off_ref, cols_ref, table_ref, sol_in, label_in, src_in, top_ref, bottom_ref = local[4:]
+    off_ref, cols_ref, table_ref, sol_in, label_in, src_in = local[4:10]
+    top_ref, bottom_ref = from_tile(*local[10:])
     res_ref, face_ref, plain_ref, packed_ref, tables_ref, column_ref, record_ref, scalar_ref = outputs
     for copy in fetch(list(zip(operands, local)), sems):
         copy.wait()
@@ -315,8 +335,6 @@
     entries = slots * capacity
     table = flat(table_ref[...]).astype(jnp.float32)
     table = jnp.concatenate([table, jnp.zeros((1, 128 - entries), jnp.float32)], axis=1)
-    if direct:
-        table = shuffle(table, lax.axis_index("slab"), slots, capacity)
     table = jnp.broadcast_to(table, (8, 128))
     tables_ref[...] = table[:, :entries].astype(jnp.int32)
     column_ref[...] = jnp.transpose(table)[:entries].astype(jnp.int32)
@@ -374,11 +392,12 @@
 
 
 def weigh_kernel(
-    scalar_ref, packed_ref, src_in, even_ref, odd_ref, top_ref, bottom_ref, weight_ref,
+    scalar_ref, packed_ref, src_in, even_ref, odd_ref, row_even_ref, row_odd_ref, weight_ref,
     conduct_ref, uptake_ref,
 ):
     own, depth, width = src_in.shape
     planes, rows = conduct_ref.shape[0:2]
+    top_ref, bottom_ref = from_tile(row_even_ref, row_odd_ref)
     labels = []
     for k in range(depth // 2):
         labels = labels + list(unpack_labels(packed_ref[k], own))
@@ -416,12 +435,11 @@
 
 
 def rows_of(basis, start, size):
-    parts = [ref[:, start : start + size].astype(jnp.float32) for ref in basis]
-    return parts[0] if len(parts) == 1 else jnp.concatenate(parts, axis=0)
+    return basis[:, start : start + size].astype(jnp.float32)
 
 
 def owners_of(basis):
-    tail = rows_of(basis, basis[0].shape[1] - 128, 128)
+    tail = rows_of(basis, basis.shape[1] - 128, 128)
     cell = tail[:, 6:7].astype(jnp.int32)
     return cell, [
         (tail[:, 2 * k : 2 * k + 1] + 256.0 * tail[:, 2 * k + 1 : 2 * k + 2]).astype(jnp.int32)
@@ -430,7 +448,7 @@
 
 
 def restrict_kernel(scalar_ref, column_ref, record_ref, even_ref, odd_ref, face_ref, res_ref, *refs, capacity):
-    basis, out_ref = refs[:-1], refs[-1]
+    basis, out_ref = refs
     depth, own, width = res_ref.shape
     entries = column_ref.shape[0]
     pick = column_ref[:, 0:1] == lax.broadcasted_iota(jnp.int32, (entries, own), 1)
@@ -530,8 +548,9 @@
 
 
 def prolong_kernel(scalar_ref, tables_ref, even_ref, odd_ref, plain_ref, *refs, groups):
-    got, basis = refs[:groups], refs[groups:-4]
-    cor_ref, top_ref, bottom_ref, correction_ref = refs[-4:]
+    got, basis = refs[:groups], refs[groups]
+    cor_ref, row_even_ref, row_odd_ref, correction_ref = refs[-4:]
+    odd = lax.axis_index("tile") % 2 == 1
     planes, own, width = cor_ref.shape
     depth = plain_ref.shape[0]
     entries = tables_ref.shape[1]
@@ -570,29 +589,32 @@
             added = jnp.dot(pick, part, preferred_element_type=jnp.float32)
             value = (plain_ref[z] if z < depth else wide[z]) + added
             cor_ref[z] = value
-            top_ref[z] = value[:2]
-            bottom_ref[z] = value[own - 2 :]
-
-
-def smooth_kernel(cor_ref, top_ref, bottom_ref, weight_ref, out_hbm, ext_ref, mid_ref, out_ref, sems):
-    planes, rows, width = ext_ref.shape
+            first, last = value[:2], value[own - 2 :]
+            row_even_ref[z] = jnp.where(odd, first, last)
+            row_odd_ref[z] = jnp.where(odd, last, first)
+
+
+def smooth_kernel(cor_ref, row_even_ref, row_odd_ref, weight_ref, out_hbm, new_ref, mid_ref, out_ref, sems):
+    planes, rows, width = mid_ref.shape
     own, depth, unused = out_ref.shape
-    blank = jnp.zeros((8, width), jnp.float32)
-    for z in range(planes):
-        ext_ref[z, :own] = cor_ref[z]
-        ext_ref[z, own:] = blank
-        ext_ref[z, own : own + 2] = top_ref[z]
-        ext_ref[z, rows - 2 :] = bottom_ref[z]
-
-    def sweep(ref, z, upto):
-        value = ref[z]
+    top_ref, bottom_ref = from_tile(row_even_ref, row_odd_ref)
+    gap = jnp.zeros((rows - own - 4, width), jnp.float32)
+
+    def corrected(z):
+        return jnp.concatenate([cor_ref[z], top_ref[z], gap, bottom_ref[z]], axis=0)
+
+    def middle(z):
+        return mid_ref[z]
+
+    def sweep(plane, z, upto):
+        value = plane(z)
         near = (
             pltpu.roll(value, 1, 1)[:upto],
             pltpu.roll(value, width - 1, 1)[:upto],
             pltpu.roll(value, 1, 0)[:upto],
             pltpu.roll(value, rows - 1, 0)[:upto],
-            ref[(z - 1) % planes, :upto],
-            ref[(z + 1) % planes, :upto],
+            plane((z - 1) % planes)[:upto],
+            plane((z + 1) % planes)[:upto],
         )
         total = (1.0 - OMEGA) * value[:upto] + weight_ref[6, z, :upto]
         for k in range(6):
@@ -600,12 +622,12 @@
         return total
 
     for z in [planes - 1] + list(range(depth + 1)):
-        mid_ref[z] = sweep(ext_ref, z, rows)
+        mid_ref[z] = sweep(corrected, z, rows)
     copies = []
     for start in range(0, depth, 8):
         for z in range(start, start + 8):
-            ext_ref[z, :own] = sweep(mid_ref, z, own)
-        out_ref[:, start : start + 8, :] = jnp.transpose(ext_ref[start : start + 8, :own], (1, 0, 2))
+            new_ref[z] = sweep(middle, z, own)
+        out_ref[:, start : start + 8, :] = jnp.transpose(new_ref[start : start + 8], (1, 0, 2))
         part = pl.ds(start, 8)
         copies.append(pltpu.make_async_copy(out_ref.at[:, part], out_hbm.at[:, part], sems.at[start // 8]))
         copies[-1].start()
@@ -647,21 +669,20 @@
     def pinned(*arrays):
         return [pltpu.with_memory_space_constraint(array, pltpu.HBM) for array in arrays]
 
-    direct = False
-    parts = slabs if direct else 1
     outgoing = pl.pallas_call(
         functools.partial(sort_kernel, capacity=capacity, count=count),
-        out_shape=(shape((entries // parts, wide), bf16),) * parts,
+        out_shape=shape((entries, wide), bf16),
         in_specs=[HBM] * 4,
-        out_specs=(VMEM,) * parts,
+        out_specs=HBM,
         scratch_shapes=[
             pltpu.VMEM((1, entries), i32),
             pltpu.SMEM((cells,), i32),
             pltpu.SMEM((cells,), i32),
             pltpu.VMEM((entries, voxels), bf16),
+            pltpu.VMEM((entries, wide), bf16),
             pltpu.SemaphoreType.DMA((7,)),
         ],
-        compiler_params=params(12),
+        compiler_params=params(60),
         name="sort_basis",
     )(
         *pinned(
@@ -671,22 +692,16 @@
             basis_values.reshape(entries, voxels),
         )
     )
-    if direct:
-        basis = [
-            lax.ppermute(outgoing[s], "slab", [(i, i ^ s) for i in range(slabs)]) for s in range(slabs - 1, 0, -1)
-        ] + [outgoing[0]]
-    else:
-        basis = lax.all_to_all(
-            outgoing[0].reshape(slabs, capacity, wide), "slab", split_axis=0, concat_axis=0, tiled=True
-        )
-        basis = [basis.reshape(entries, wide)]
+    basis = lax.all_to_all(
+        outgoing.reshape(slabs, capacity, wide), "slab", split_axis=0, concat_axis=0, tiled=True
+    ).reshape(entries, wide)
     outgoing, solution, phase_label, source, table = lax.optimization_barrier(
         (outgoing, solution, phase_label, source, table)
     )
     message = shape((MESSAGE, width), bf16)
     edge = shape((3, depth, width), f32)
-    even, odd, top, bottom = pl.pallas_call(
-        functools.partial(border_kernel, direct=direct),
+    even, odd, row_even, row_odd = pl.pallas_call(
+        border_kernel,
         out_shape=(message, message, edge, edge),
         in_specs=[HBM] * 4,
         out_specs=(VMEM,) * 4,
@@ -700,8 +715,8 @@
         compiler_params=params(8),
         name="border",
     )(*pinned(solution, phase_label, source, table))
-    top = lax.ppermute(top, "tile", wheel(tiles, -1))
-    bottom = lax.ppermute(bottom, "tile", wheel(tiles, 1))
+    row_even = along_tile(row_even, False)
+    row_odd = along_tile(row_odd, True)
     even, odd = pl.pallas_call(
         corner_kernel,
         out_shape=(message, message),
@@ -710,19 +725,19 @@
         scratch_shapes=[pltpu.VMEM(edge.shape, f32)] * 2 + [pltpu.SemaphoreType.DMA((4,))],
         compiler_params=params(8),
         name="corner",
-    )(even, odd, top, bottom)
-    even = lax.ppermute(even, "slab", pairs(slabs, False))
-    odd = lax.ppermute(odd, "slab", pairs(slabs, True))
-    row_top, row_bottom = top, bottom
+    )(even, odd, row_even, row_odd)
+    even = along_slab(even, False)
+    odd = along_slab(odd, True)
+    first_even, first_odd = row_even, row_odd
 
     wide_block = pltpu.VMEM((planes, tall, width), f32)
     operands = [
         phase_diffusivity, phase_uptake, coarse_diag, coarse_ids, coarse_off, coarse_cols, table,
-        solution, phase_label, source, top, bottom,
+        solution, phase_label, source, row_even, row_odd,
     ]
     phases = phase_diffusivity.shape[0]
     residual, face, plain, packed, tables, column, record, scalars = pl.pallas_call(
-        functools.partial(residual_kernel, direct=direct, count=count),
+        functools.partial(residual_kernel, count=count),
         out_shape=(
             shape((depth, rows, width), bf16),
             shape((6, rows, width), f32),
@@ -748,23 +763,23 @@
     payload = pl.pallas_call(
         functools.partial(restrict_kernel, capacity=capacity),
         out_shape=shape((devices, lines, 128), f32),
-        in_specs=[VMEM] * (7 + parts),
+        in_specs=[VMEM] * 8,
         out_specs=VMEM,
         compiler_params=params(8),
         name="restrict",
-    )(scalars, column, record, even, odd, face, residual, *basis)
+    )(scalars, column, record, even, odd, face, residual, basis)
     got = lax.all_to_all(payload, ("slab", "tile"), split_axis=0, concat_axis=0, tiled=True)
     got = [got[:, 4 * t : 4 * t + 4].reshape(4 * devices, 128) for t in range(groups)]
 
     edge = shape((planes, 2, width), f32)
-    corrected, top, bottom, coarse_correction = pl.pallas_call(
+    corrected, row_even, row_odd, coarse_correction = pl.pallas_call(
         functools.partial(prolong_kernel, groups=groups),
         out_shape=(shape((planes, rows, width), f32), edge, edge, shape((1, cells), f32)),
-        in_specs=[VMEM] * (5 + groups + parts),
+        in_specs=[VMEM] * (6 + groups),
         out_specs=(VMEM, VMEM, VMEM, VMEM),
         compiler_params=params(12 + count // 128),
         name="prolong",
-    )(scalars, tables, even, odd, plain, *got, *basis)
+    )(scalars, tables, even, odd, plain, *got, basis)
     corrected, packed = lax.optimization_barrier((corrected, packed))
     weights = pl.pallas_call(
         weigh_kernel,
@@ -774,18 +789,19 @@
         scratch_shapes=[wide_block] * 2,
         compiler_params=params(12),
         name="weigh",
-    )(scalars, packed, source, even, odd, row_top, row_bottom)
-    top = lax.ppermute(top, "tile", wheel(tiles, -1))
-    bottom = lax.ppermute(bottom, "tile", wheel(tiles, 1))
+    )(scalars, packed, source, even, odd, first_even, first_odd)
+    row_even = along_tile(row_even, False)
+    row_odd = along_tile(row_odd, True)
     smooth = pl.pallas_call(
         smooth_kernel,
         out_shape=shape((rows, depth, width), f32),
         in_specs=[VMEM] * 4,
         out_specs=HBM,
-        scratch_shapes=[wide_block] * 2 + [pltpu.VMEM(block, f32), pltpu.SemaphoreType.DMA((depth // 8,))],
+        scratch_shapes=[pltpu.VMEM((depth, rows, width), f32), wide_block, pltpu.VMEM(block, f32)]
+        + [pltpu.SemaphoreType.DMA((depth // 8,))],
         compiler_params=params(16),
         name="smooth",
-    )(corrected, top, bottom, weights)
+    )(corrected, row_even, row_odd, weights)
     return smooth, coarse_correction.reshape(cells)
 
 

time: 47.7 us -> 47.3 us (level)
  waiting for transfers between devices: 11.2 us -> 10.2 us
  starting transfers between devices: 11.2 us -> 11.9 us
    ppermute x6, waiting for transfers between devices: 4.95 us -> 3.4 us  [the longest x4 3.03 us: along_tile(): return lax.ppermute(message, 'tile', closed(pairs(tiles, odd), tiles))]
    ppermute x6, starting transfers between devices: 3.91 us -> 4.61 us  [the longest x2 2.36 us: along_slab(): return lax.ppermute(message, ('slab', 'tile'), table)]
    all_to_all x1, waiting for transfers between devices: 6.26 us -> 6.76 us  [shards(): lax.all_to_all(outgoing.reshape(slabs, capacity, wide), 'slab', split_axi...]
where the time goes in v6:
time: 47.3 us; the launch traced here: 47.1 us
  Pallas kernels  13.4 us (28%)
  starting transfers between devices  11.9 us (25%)
  blocking collectives  10.9 us (23%)
  waiting for transfers between devices  10.2 us (22%)
  between operations  0.71 us (2%)
    all_to_all x1, blocking collectives, shards(): lax.all_to_all(payload, ('slab', 'tile'), split_axis=0, concat_axis=0, ti...  10.9 us
    all_to_all x1, starting transfers between devices, shards(): lax.all_to_all(outgoing.reshape(slabs, capacity, wide), 'slab', split_axi...  7.26 us
    all_to_all x1, waiting for transfers between devices, shards(): lax.all_to_all(outgoing.reshape(slabs, capacity, wide), 'slab', split_axi...  6.76 us
    pallas_call x1, Pallas kernels, shards(): pl.pallas_call(functools.partial(residual_kernel, count=count), out_shape...  3.26 us
    ppermute x4, waiting for transfers between devices, along_tile(): return lax.ppermute(message, 'tile', closed(pairs(tiles, odd), tiles))  3.03 us
    ppermute x2, starting transfers between devices, along_slab(): return lax.ppermute(message, ('slab', 'tile'), table)  2.36 us
    pallas_call x1, Pallas kernels, shards(): pl.pallas_call(functools.partial(sort_kernel, capacity=capacity, count=co...  2.33 us
    ppermute x4, starting transfers between devices, along_tile(): return lax.ppermute(message, 'tile', closed(pairs(tiles, odd), tiles))  2.25 us
  transfers between devices with their start and end apart: 7, of which 4 were waited for; matrix products, arithmetic and copies ran while one was open for 0% of the time, Pallas kernels for 15%

profile of v6, /device:TPU:0, one launch (start us, length us, event | category | flops | bytes accessed | tf_op | source)
XLA Modules:
  0.0 47.1 jit_solution(7253063568451848040)
XLA Ops:
  0.6 0.0 copy-start
  0.6 2.3 %sort_basis.1 = bf16[64,5248]{1,0:T(8,128)(2,1)} custom-call(s32[1,64]{1,0:T(1,128)} %bitcast.15, s32[8]{0:T(128)} %bitcast.16, s32[8]{0:T(128)} %refs_3_.1, bf16[64,4096]{1,0:T(8,128)(2,1)} %bitcast.12), custom_call_target="tpu_custom_call" | custom-call | tf_op jit(solution)/shard_map/sort_basis/pallas_call | solution.py:672
  3.0 7.3 %all-to-all-start = ((bf16[8,8,5248]{2,1,0:T(8,128)(2,1)}), bf16[8,8,5248]{2,1,0:T(8,128)(2,1)S(1)}, u32[]{:S(2)}, u32[]{:S(2)}) async-start(bf16[8,8,5248]{2,1,0:T(8,128)(2,1)} %bitcast.11), calls=%async_computation | async-start | bytes 1343488 | tf_op jit(solution)/shard_map/all_to_all | solution.py:695
  10.2 1.7 %border.1 = (bf16[160,256]{1,0:T(8,128)(2,1)S(1)}, bf16[160,256]{1,0:T(8,128)(2,1)S(1)}, f32[3,16,256]{2,1,0:T(8,128)S(1)}, f32[3,16,256]{2,1,0:T(8,128)S(1)}) custom-call(f32[32,16,256]{2,1,0:T(8,128)} %refs_7_, s32[32,16,256]{2,1,0:T(8,128)} %refs_8_, f32[32,16,256]{2,1,0:T(8,128)} %src_in, s32[8,8]{1,0:T(8,128)} %bitcast.13), custom_call_target="tpu_custom_call" | custom-call | tf_op jit(solution)/shard_map/border/pallas_call | solution.py:703
  12.0 0.1 collective-permute-start
  12.1 1.6 %collective-permute-start.1 = (f32[3,16,256]{2,1,0:T(8,128)S(1)}, f32[3,16,256]{2,1,0:T(8,128)S(1)}, u32[]{:S(2)}, u32[]{:S(2)}) collective-permute-start(f32[3,16,256]{2,1,0:T(8,128)S(1)} %get-tuple-element.31), channel_id=1, source_target_pairs={{0,3},{1,2},{2,1},{3,0},{4,7},{5,6},{6,5},{7,4},{8,11},{9,10},{10,... | collective-permute-start | bytes 147464 | tf_op jit(solution)/shard_map/ppermute | solution.py:42
  13.7 0.0 collective-permute-done.refs_10_.row_even.row_even_ref
  13.7 1.9 %collective-permute-done.1.refs_11_.row_odd.row_odd_ref = f32[3,16,256]{2,1,0:T(8,128)S(1)} collective-permute-done((f32[3,16,256]{2,1,0:T(8,128)S(1)}, f32[3,16,256]{2,1,0:T(8,128)S(1)}, u32[]{:S(2)}, u32[]{:S(2)}) %collective-permute-start.1) | collective-permute-done | bytes 49184 | tf_op jit(solution)/shard_map/ppermute | solution.py:42
  15.6 0.4 corner.1
  16.0 2.1 %collective-permute-start.2 = (bf16[160,256]{1,0:T(8,128)(2,1)S(1)}, bf16[160,256]{1,0:T(8,128)(2,1)S(1)}, u32[]{:S(2)}, u32[]{:S(2)}) collective-permute-start(bf16[160,256]{1,0:T(8,128)(2,1)S(1)} %get-tuple-element.36), channel_id=1, source_target_pairs={{0,4},{1,5},{2,6},{3,7},{4,0},{5,1},{6,2},{7,3},{8,12},{9,13},{10,... | collective-permute-start | bytes 245768 | tf_op jit(solution)/shard_map/ppermute | solution.py:53
  18.1 0.3 collective-permute-start.3
  18.4 3.3 %residual.1 = (bf16[16,32,256]{2,1,0:T(8,128)(2,1)S(1)}, f32[6,32,256]{2,1,0:T(8,128)S(1)}, f32[16,32,256]{2,1,0:T(8,128)S(1)}, f32[8,8,256]{2,1,0:T(8,128)S(1)}...) custom-call(f32[3]{0:T(128)} %refs_0_.1, f32[3]{0:T(128)} %refs_1_.1, ...), custom_call_target="tpu_custom_call" | custom-call | tf_op jit(solution)/shard_map/residual/pallas_call | solution.py:739
  21.6 0.4 collective-permute-done.2.even_ref
  22.0 0.0 collective-permute-done.3.odd_ref
  22.0 6.8 %all-to-all-done = bf16[8,8,5248]{2,1,0:T(8,128)(2,1)S(1)} async-done(((bf16[8,8,5248]{2,1,0:T(8,128)(2,1)}), bf16[8,8,5248]{2,1,0:T(8,128)(2,1)S(1)}, u32[]{:S(2)}, u32[]{:S(2)}) %all-to-all-start) | async-done | bytes 671776 | tf_op jit(solution)/shard_map/all_to_all | solution.py:695
  28.8 0.4 restrict.1
  29.2 10.9 %all_to_all.10 = f32[32,4,128]{2,1,0:T(4,128)S(1)} all-to-all(f32[32,4,128]{2,1,0:T(4,128)S(1)} %restrict.1), channel_id=1, replica_groups=mesh['slab'=8,'tile'=4] {'slab','tile'}, dimensions={0} | all-to-all | bytes 131072 | tf_op jit(solution)/shard_map/all_to_all | solution.py:771
  40.1 1.5 %prolong.1 = (f32[20,32,256]{2,1,0:T(8,128)S(1)}, f32[20,2,256]{2,1,0:T(2,128)S(1)}, f32[20,2,256]{2,1,0:T(2,128)S(1)}, f32[1,8]{1,0:T(1,128)}) custom-call(f32[3,3,8,128]{3,2,1,0:T(8,128)S(1)} %get-tuple-element.32.scalar_ref, s32[8,64]{1,0:T(8,128)S(1)} %get-tuple-element.33.tables_ref, bf16[160,256]{1,0:T(8,128)(2,1)S(1)} %collective-permute-done.2.even_ref, ...), custom_call_target="tpu_custom_call" | custom-call | tf_op jit(solution)/shard_map/prolong/pallas_call | solution.py:775
  41.7 0.1 collective-permute-start.4
  41.8 0.4 collective-permute-start.5
  42.2 0.0 copy-done
  42.2 1.9 %weigh.1.weight_ref = f32[7,20,40,256]{3,2,1,0:T(8,128)S(1)} custom-call(f32[3,3,8,128]{3,2,1,0:T(8,128)S(1)} %get-tuple-element.32.scalar_ref, f32[8,8,256]{2,1,0:T(8,128)S(1)} %get-tuple-element.48.packed_ref, f32[32,16,256]{2,1,0:T(8,128)S(1)} %copy-done, bf16[160,256]{1,0:T(8,128)(2,1)S(1)} %collective-permute-done.2.even_ref, ...), custom_call_target="tpu_custom_call" | custom-call | tf_op jit(solution)/shard_map/weigh/pallas_call | solution.py:784
  44.1 0.0 collective-permute-done.4.row_even_ref
  44.1 1.1 %collective-permute-done.5.row_odd_ref = f32[20,2,256]{2,1,0:T(2,128)S(1)} collective-permute-done((f32[20,2,256]{2,1,0:T(2,128)S(1)}, f32[20,2,256]{2,1,0:T(2,128)S(1)}, u32[]{:S(2)}, u32[]{:S(2)}) %collective-permute-start.5) | collective-permute-done | bytes 40992 | tf_op jit(solution)/shard_map/ppermute | solution.py:42
  45.2 1.8 %smooth.1 = f32[32,16,256]{2,1,0:T(8,128)} custom-call(f32[20,32,256]{2,1,0:T(8,128)S(1)} %get-tuple-element.45.cor_ref, f32[20,2,256]{2,1,0:T(2,128)S(1)} %collective-permute-done.4.row_even_ref, f32[20,2,256]{2,1,0:T(2,128)S(1)} %collective-permute-done.5.row_odd_ref, f32[7,20,40,256]{3,2,1,0:T(8,128)S(1)} %weigh.1.weight_ref), custom_call_target="tpu_custom_call" | custom-call | tf_op jit(solution)/shard_map/smooth/pallas_call | solution.py:795
Async XLA Ops:
  0.6 41.6 %copy-start = (f32[32,16,256]{2,1,0:T(8,128)S(1)}, f32[32,16,256]{2,1,0:T(8,128)}, u32[]{:S(2)}) copy-start(f32[32,16,256]{2,1,0:T(8,128)} %src_in) | copy-start | bytes 1572868
  3.0 25.8 %all-to-all-start = ((bf16[8,8,5248]{2,1,0:T(8,128)(2,1)}), bf16[8,8,5248]{2,1,0:T(8,128)(2,1)S(1)}, u32[]{:S(2)}, u32[]{:S(2)}) async-start(bf16[8,8,5248]{2,1,0:T(8,128)(2,1)} %bitcast.11), calls=%async_computation | async-start | bytes 1343488 | tf_op jit(solution)/shard_map/all_to_all | solution.py:695
  12.0 1.7 %collective-permute-start = (f32[3,16,256]{2,1,0:T(8,128)S(1)}, f32[3,16,256]{2,1,0:T(8,128)S(1)}, u32[]{:S(2)}, u32[]{:S(2)}) collective-permute-start(f32[3,16,256]{2,1,0:T(8,128)S(1)} %get-tuple-element.30), channel_id=1, source_target_pairs={{0,1},{1,0},{2,3},{3,2},{4,5},{5,4},{6,7},{7,6},{8,9},{9,8},{10,11... | collective-permute-start | bytes 147464 | tf_op jit(solution)/shard_map/ppermute | solution.py:42
  12.1 3.6 %collective-permute-start.1 = (f32[3,16,256]{2,1,0:T(8,128)S(1)}, f32[3,16,256]{2,1,0:T(8,128)S(1)}, u32[]{:S(2)}, u32[]{:S(2)}) collective-permute-start(f32[3,16,256]{2,1,0:T(8,128)S(1)} %get-tuple-element.31), channel_id=1, source_target_pairs={{0,3},{1,2},{2,1},{3,0},{4,7},{5,6},{6,5},{7,4},{8,11},{9,10},{10,... | collective-permute-start | bytes 147464 | tf_op jit(solution)/shard_map/ppermute | solution.py:42
  16.0 6.0 %collective-permute-start.2 = (bf16[160,256]{1,0:T(8,128)(2,1)S(1)}, bf16[160,256]{1,0:T(8,128)(2,1)S(1)}, u32[]{:S(2)}, u32[]{:S(2)}) collective-permute-start(bf16[160,256]{1,0:T(8,128)(2,1)S(1)} %get-tuple-element.36), channel_id=1, source_target_pairs={{0,4},{1,5},{2,6},{3,7},{4,0},{5,1},{6,2},{7,3},{8,12},{9,13},{10,... | collective-permute-start | bytes 245768 | tf_op jit(solution)/shard_map/ppermute | solution.py:53
  18.1 3.9 %collective-permute-start.3 = (bf16[160,256]{1,0:T(8,128)(2,1)S(1)}, bf16[160,256]{1,0:T(8,128)(2,1)S(1)}, u32[]{:S(2)}, u32[]{:S(2)}) collective-permute-start(bf16[160,256]{1,0:T(8,128)(2,1)S(1)} %get-tuple-element.37), channel_id=1, source_target_pairs={{0,1},{1,0},{2,3},{3,2},{4,8},{5,9},{6,10},{7,11},{8,4},{9,5},{10,... | collective-permute-start | bytes 245768 | tf_op jit(solution)/shard_map/ppermute | solution.py:53
  41.7 2.5 %collective-permute-start.4 = (f32[20,2,256]{2,1,0:T(2,128)S(1)}, f32[20,2,256]{2,1,0:T(2,128)S(1)}, u32[]{:S(2)}, u32[]{:S(2)}) collective-permute-start(f32[20,2,256]{2,1,0:T(2,128)S(1)} %get-tuple-element.46), channel_id=1, source_target_pairs={{0,1},{1,0},{2,3},{3,2},{4,5},{5,4},{6,7},{7,6},{8,9},{9,8},{10,11... | collective-permute-start | bytes 122888 | tf_op jit(solution)/shard_map/ppermute | solution.py:42
  41.8 3.5 %collective-permute-start.5 = (f32[20,2,256]{2,1,0:T(2,128)S(1)}, f32[20,2,256]{2,1,0:T(2,128)S(1)}, u32[]{:S(2)}, u32[]{:S(2)}) collective-permute-start(f32[20,2,256]{2,1,0:T(2,128)S(1)} %get-tuple-element.47), channel_id=1, source_target_pairs={{0,3},{1,2},{2,1},{3,0},{4,7},{5,6},{6,5},{7,4},{8,11},{9,10},{10,... | collective-permute-start | bytes 122888 | tf_op jit(solution)/shard_map/ppermute | solution.py:42

commit v7 on v6

--- a/solution.py
+++ b/solution.py
@@ -392,7 +392,7 @@
 
 
 def weigh_kernel(
-    scalar_ref, packed_ref, src_in, even_ref, odd_ref, row_even_ref, row_odd_ref, weight_ref,
+    scalar_ref, packed_ref, src_in, even_ref, odd_ref, row_even_ref, row_odd_ref, cor_ref, weight_ref, inner_ref,
     conduct_ref, uptake_ref,
 ):
     own, depth, width = src_in.shape
@@ -432,6 +432,19 @@
             if z < depth:
                 weight_ref[6, z, own : own + 1] = scale[own : own + 1] * top_ref[2, z : z + 1]
                 weight_ref[6, z, rows - 1 :] = scale[rows - 1 :] * bottom_ref[2, z : z + 1]
+            value, inner = cor_ref[z], slice(8, own - 8)
+            beside_all = (
+                pltpu.roll(value, 1, 1)[inner],
+                pltpu.roll(value, width - 1, 1)[inner],
+                pltpu.roll(value, 1, 0)[inner],
+                pltpu.roll(value, own - 1, 0)[inner],
+                cor_ref[(z - 1) % planes, inner],
+                cor_ref[(z + 1) % planes, inner],
+            )
+            total = (1.0 - OMEGA) * value[inner] + weight_ref[6, z, inner]
+            for k, other in enumerate(beside_all):
+                total = total + weight_ref[k, z, inner] * other
+            inner_ref[z] = total
 
 
 def rows_of(basis, start, size):
@@ -594,7 +607,7 @@
             row_odd_ref[z] = jnp.where(odd, last, first)
 
 
-def smooth_kernel(cor_ref, row_even_ref, row_odd_ref, weight_ref, out_hbm, new_ref, mid_ref, out_ref, sems):
+def smooth_kernel(cor_ref, row_even_ref, row_odd_ref, weight_ref, inner_ref, out_hbm, new_ref, mid_ref, out_ref, sems):
     planes, rows, width = mid_ref.shape
     own, depth, unused = out_ref.shape
     top_ref, bottom_ref = from_tile(row_even_ref, row_odd_ref)
@@ -604,29 +617,30 @@
         return jnp.concatenate([cor_ref[z], top_ref[z], gap, bottom_ref[z]], axis=0)
 
     def middle(z):
-        return mid_ref[z]
-
-    def sweep(plane, z, upto):
+        return jnp.concatenate([mid_ref[z, :8], inner_ref[z], mid_ref[z, own - 8 :]], axis=0)
+
+    def sweep(plane, z, part):
         value = plane(z)
         near = (
-            pltpu.roll(value, 1, 1)[:upto],
-            pltpu.roll(value, width - 1, 1)[:upto],
-            pltpu.roll(value, 1, 0)[:upto],
-            pltpu.roll(value, rows - 1, 0)[:upto],
-            plane((z - 1) % planes)[:upto],
-            plane((z + 1) % planes)[:upto],
+            pltpu.roll(value, 1, 1)[part],
+            pltpu.roll(value, width - 1, 1)[part],
+            pltpu.roll(value, 1, 0)[part],
+            pltpu.roll(value, rows - 1, 0)[part],
+            plane((z - 1) % planes)[part],
+            plane((z + 1) % planes)[part],
         )
-        total = (1.0 - OMEGA) * value[:upto] + weight_ref[6, z, :upto]
+        total = (1.0 - OMEGA) * value[part] + weight_ref[6, z, part]
         for k in range(6):
-            total = total + weight_ref[k, z, :upto] * near[k]
+            total = total + weight_ref[k, z, part] * near[k]
         return total
 
     for z in [planes - 1] + list(range(depth + 1)):
-        mid_ref[z] = sweep(corrected, z, rows)
+        for part in (slice(0, 8), slice(own - 8, rows)):
+            mid_ref[z, part] = sweep(corrected, z, part)
     copies = []
     for start in range(0, depth, 8):
         for z in range(start, start + 8):
-            new_ref[z] = sweep(middle, z, own)
+            new_ref[z] = sweep(middle, z, slice(0, own))
         out_ref[:, start : start + 8, :] = jnp.transpose(new_ref[start : start + 8], (1, 0, 2))
         part = pl.ds(start, 8)
         copies.append(pltpu.make_async_copy(out_ref.at[:, part], out_hbm.at[:, part], sems.at[start // 8]))
@@ -781,27 +795,27 @@
         name="prolong",
     )(scalars, tables, even, odd, plain, *got, basis)
     corrected, packed = lax.optimization_barrier((corrected, packed))
-    weights = pl.pallas_call(
+    weights, inner = pl.pallas_call(
         weigh_kernel,
-        out_shape=shape((7, planes, tall, width), f32),
-        in_specs=[VMEM] * 7,
-        out_specs=VMEM,
+        out_shape=(shape((7, planes, tall, width), f32), shape((planes, rows - 16, width), f32)),
+        in_specs=[VMEM] * 8,
+        out_specs=(VMEM, VMEM),
         scratch_shapes=[wide_block] * 2,
         compiler_params=params(12),
         name="weigh",
-    )(scalars, packed, source, even, odd, first_even, first_odd)
+    )(scalars, packed, source, even, odd, first_even, first_odd, corrected)
     row_even = along_tile(row_even, False)
     row_odd = along_tile(row_odd, True)
     smooth = pl.pallas_call(
         smooth_kernel,
         out_shape=shape((rows, depth, width), f32),
-        in_specs=[VMEM] * 4,
+        in_specs=[VMEM] * 5,
         out_specs=HBM,
         scratch_shapes=[pltpu.VMEM((depth, rows, width), f32), wide_block, pltpu.VMEM(block, f32)]
         + [pltpu.SemaphoreType.DMA((depth // 8,))],
         compiler_params=params(16),
         name="smooth",
-    )(corrected, row_even, row_odd, weights)
+    )(corrected, row_even, row_odd, weights, inner)
     return smooth, coarse_correction.reshape(cells)
 
 

time: 47.3 us -> 47.1 us (level)
  transfers between devices with their start and end apart: 7 -> 7, of which waited for: 4 -> 4; matrix products, arithmetic and copies ran while one was open for 0% -> 0% of each run, Pallas kernels for 15% -> 16%
where the time goes in v7:
time: 47.1 us; the launch traced here: 46.8 us
  Pallas kernels  13.5 us (29%)
  starting transfers between devices  11.9 us (25%)
  blocking collectives  10.9 us (23%)
  waiting for transfers between devices  9.88 us (21%)
  between operations  0.71 us (2%)
    all_to_all x1, blocking collectives, shards(): lax.all_to_all(payload, ('slab', 'tile'), split_axis=0, concat_axis=0, ti...  10.9 us
    all_to_all x1, starting transfers between devices, shards(): lax.all_to_all(outgoing.reshape(slabs, capacity, wide), 'slab', split_axi...  7.26 us
    all_to_all x1, waiting for transfers between devices, shards(): lax.all_to_all(outgoing.reshape(slabs, capacity, wide), 'slab', split_axi...  6.76 us
    pallas_call x1, Pallas kernels, shards(): pl.pallas_call(functools.partial(residual_kernel, count=count), out_shape...  3.26 us
    ppermute x4, waiting for transfers between devices, along_tile(): return lax.ppermute(message, 'tile', closed(pairs(tiles, odd), tiles))  2.75 us
    ppermute x2, starting transfers between devices, along_slab(): return lax.ppermute(message, ('slab', 'tile'), table)  2.36 us
    pallas_call x1, Pallas kernels, shards(): pl.pallas_call(functools.partial(sort_kernel, capacity=capacity, count=co...  2.31 us
    ppermute x4, starting transfers between devices, along_tile(): return lax.ppermute(message, 'tile', closed(pairs(tiles, odd), tiles))  2.25 us
  transfers between devices with their start and end apart: 7, of which 4 were waited for; matrix products, arithmetic and copies ran while one was open for 0% of the time, Pallas kernels for 16%

profile of v7, /device:TPU:0, one launch (start us, length us, event | category | flops | bytes accessed | tf_op | source)
XLA Modules:
  0.0 46.8 jit_solution(3434541693800100212)
XLA Ops:
  0.6 0.0 copy-start
  0.6 2.3 %sort_basis.1 = bf16[64,5248]{1,0:T(8,128)(2,1)} custom-call(s32[1,64]{1,0:T(1,128)} %bitcast.15, s32[8]{0:T(128)} %bitcast.16, s32[8]{0:T(128)} %refs_3_.1, bf16[64,4096]{1,0:T(8,128)(2,1)} %bitcast.12), custom_call_target="tpu_custom_call" | custom-call | tf_op jit(solution)/shard_map/sort_basis/pallas_call | solution.py:686
  3.0 7.3 %all-to-all-start = ((bf16[8,8,5248]{2,1,0:T(8,128)(2,1)}), bf16[8,8,5248]{2,1,0:T(8,128)(2,1)S(1)}, u32[]{:S(2)}, u32[]{:S(2)}) async-start(bf16[8,8,5248]{2,1,0:T(8,128)(2,1)} %bitcast.11), calls=%async_computation | async-start | bytes 1343488 | tf_op jit(solution)/shard_map/all_to_all | solution.py:709
  10.2 1.7 %border.1 = (bf16[160,256]{1,0:T(8,128)(2,1)S(1)}, bf16[160,256]{1,0:T(8,128)(2,1)S(1)}, f32[3,16,256]{2,1,0:T(8,128)S(1)}, f32[3,16,256]{2,1,0:T(8,128)S(1)}) custom-call(f32[32,16,256]{2,1,0:T(8,128)} %refs_7_, s32[32,16,256]{2,1,0:T(8,128)} %refs_8_, f32[32,16,256]{2,1,0:T(8,128)} %src_in, s32[8,8]{1,0:T(8,128)} %bitcast.13), custom_call_target="tpu_custom_call" | custom-call | tf_op jit(solution)/shard_map/border/pallas_call | solution.py:717
  12.0 0.1 collective-permute-start
  12.0 1.6 %collective-permute-start.1 = (f32[3,16,256]{2,1,0:T(8,128)S(1)}, f32[3,16,256]{2,1,0:T(8,128)S(1)}, u32[]{:S(2)}, u32[]{:S(2)}) collective-permute-start(f32[3,16,256]{2,1,0:T(8,128)S(1)} %get-tuple-element.33), channel_id=1, source_target_pairs={{0,3},{1,2},{2,1},{3,0},{4,7},{5,6},{6,5},{7,4},{8,11},{9,10},{10,... | collective-permute-start | bytes 147464 | tf_op jit(solution)/shard_map/ppermute | solution.py:42
  13.7 0.0 collective-permute-done.refs_10_.row_even.row_even_ref
  13.7 1.9 %collective-permute-done.1.refs_11_.row_odd.row_odd_ref = f32[3,16,256]{2,1,0:T(8,128)S(1)} collective-permute-done((f32[3,16,256]{2,1,0:T(8,128)S(1)}, f32[3,16,256]{2,1,0:T(8,128)S(1)}, u32[]{:S(2)}, u32[]{:S(2)}) %collective-permute-start.1) | collective-permute-done | bytes 49184 | tf_op jit(solution)/shard_map/ppermute | solution.py:42
  15.6 0.4 corner.1
  16.0 2.1 %collective-permute-start.2 = (bf16[160,256]{1,0:T(8,128)(2,1)S(1)}, bf16[160,256]{1,0:T(8,128)(2,1)S(1)}, u32[]{:S(2)}, u32[]{:S(2)}) collective-permute-start(bf16[160,256]{1,0:T(8,128)(2,1)S(1)} %get-tuple-element.38), channel_id=1, source_target_pairs={{0,4},{1,5},{2,6},{3,7},{4,0},{5,1},{6,2},{7,3},{8,12},{9,13},{10,... | collective-permute-start | bytes 245768 | tf_op jit(solution)/shard_map/ppermute | solution.py:53
  18.1 0.3 collective-permute-start.3
  18.4 3.3 %residual.1 = (bf16[16,32,256]{2,1,0:T(8,128)(2,1)S(1)}, f32[6,32,256]{2,1,0:T(8,128)S(1)}, f32[16,32,256]{2,1,0:T(8,128)S(1)}, f32[8,8,256]{2,1,0:T(8,128)S(1)}...) custom-call(f32[3]{0:T(128)} %refs_0_.1, f32[3]{0:T(128)} %refs_1_.1, ...), custom_call_target="tpu_custom_call" | custom-call | tf_op jit(solution)/shard_map/residual/pallas_call | solution.py:753
  21.6 0.4 collective-permute-done.2.even_ref
  22.0 0.0 collective-permute-done.3.odd_ref
  22.0 6.8 %all-to-all-done = bf16[8,8,5248]{2,1,0:T(8,128)(2,1)S(1)} async-done(((bf16[8,8,5248]{2,1,0:T(8,128)(2,1)}), bf16[8,8,5248]{2,1,0:T(8,128)(2,1)S(1)}, u32[]{:S(2)}, u32[]{:S(2)}) %all-to-all-start) | async-done | bytes 671776 | tf_op jit(solution)/shard_map/all_to_all | solution.py:709
  28.8 0.5 restrict.1
  29.2 10.9 %all_to_all.10 = f32[32,4,128]{2,1,0:T(4,128)S(1)} all-to-all(f32[32,4,128]{2,1,0:T(4,128)S(1)} %restrict.1), channel_id=1, replica_groups=mesh['slab'=8,'tile'=4] {'slab','tile'}, dimensions={0} | all-to-all | bytes 131072 | tf_op jit(solution)/shard_map/all_to_all | solution.py:785
  40.1 1.5 %prolong.1 = (f32[20,32,256]{2,1,0:T(8,128)S(1)}, f32[20,2,256]{2,1,0:T(2,128)S(1)}, f32[20,2,256]{2,1,0:T(2,128)S(1)}, f32[1,8]{1,0:T(1,128)}) custom-call(f32[3,3,8,128]{3,2,1,0:T(8,128)S(1)} %get-tuple-element.34.scalar_ref, s32[8,64]{1,0:T(8,128)S(1)} %get-tuple-element.35.tables_ref, bf16[160,256]{1,0:T(8,128)(2,1)S(1)} %collective-permute-done.2.even_ref, ...), custom_call_target="tpu_custom_call" | custom-call | tf_op jit(solution)/shard_map/prolong/pallas_call | solution.py:789
  41.6 0.1 collective-permute-start.4
  41.7 0.4 collective-permute-start.5
  42.2 0.0 copy-done
  42.2 2.2 %weigh.1 = (f32[7,20,40,256]{3,2,1,0:T(8,128)S(1)}, f32[20,16,256]{2,1,0:T(8,128)S(1)}) custom-call(f32[3,3,8,128]{3,2,1,0:T(8,128)S(1)} %get-tuple-element.34.scalar_ref, f32[8,8,256]{2,1,0:T(8,128)S(1)} %get-tuple-element.50.packed_ref, f32[32,16,256]{2,1,0:T(8,128)S(1)} %copy-done, bf16[160,256]{1,0:T(8,128)(2,1)S(1)} %collective-permute-done.2.even_ref, ...), custom_call_target="tpu_custom_call" | custom-call | tf_op jit(solution)/shard_map/weigh/pallas_call | solution.py:798
  44.4 0.0 collective-permute-done.4.row_even_ref
  44.4 0.8 %collective-permute-done.5.row_odd_ref = f32[20,2,256]{2,1,0:T(2,128)S(1)} collective-permute-done((f32[20,2,256]{2,1,0:T(2,128)S(1)}, f32[20,2,256]{2,1,0:T(2,128)S(1)}, u32[]{:S(2)}, u32[]{:S(2)}) %collective-permute-start.5) | collective-permute-done | bytes 40992 | tf_op jit(solution)/shard_map/ppermute | solution.py:42
  45.2 1.6 %smooth.1 = f32[32,16,256]{2,1,0:T(8,128)} custom-call(f32[20,32,256]{2,1,0:T(8,128)S(1)} %get-tuple-element.47.cor_ref, f32[20,2,256]{2,1,0:T(2,128)S(1)} %collective-permute-done.4.row_even_ref, f32[20,2,256]{2,1,0:T(2,128)S(1)} %collective-permute-done.5.row_odd_ref, f32[7,20,40,256]{3,2,1,0:T(8,128)S(1)} %get-tuple-element.51.weight_ref, ...), custom_call_target="tpu_custom_call" | custom-call | tf_op jit(solution)/shard_map/smooth/pallas_call | solution.py:809
Async XLA Ops:
  0.6 41.5 %copy-start = (f32[32,16,256]{2,1,0:T(8,128)S(1)}, f32[32,16,256]{2,1,0:T(8,128)}, u32[]{:S(2)}) copy-start(f32[32,16,256]{2,1,0:T(8,128)} %src_in) | copy-start | bytes 1572868
  3.0 25.8 %all-to-all-start = ((bf16[8,8,5248]{2,1,0:T(8,128)(2,1)}), bf16[8,8,5248]{2,1,0:T(8,128)(2,1)S(1)}, u32[]{:S(2)}, u32[]{:S(2)}) async-start(bf16[8,8,5248]{2,1,0:T(8,128)(2,1)} %bitcast.11), calls=%async_computation | async-start | bytes 1343488 | tf_op jit(solution)/shard_map/all_to_all | solution.py:709
  12.0 1.7 %collective-permute-start = (f32[3,16,256]{2,1,0:T(8,128)S(1)}, f32[3,16,256]{2,1,0:T(8,128)S(1)}, u32[]{:S(2)}, u32[]{:S(2)}) collective-permute-start(f32[3,16,256]{2,1,0:T(8,128)S(1)} %get-tuple-element.32), channel_id=1, source_target_pairs={{0,1},{1,0},{2,3},{3,2},{4,5},{5,4},{6,7},{7,6},{8,9},{9,8},{10,11... | collective-permute-start | bytes 147464 | tf_op jit(solution)/shard_map/ppermute | solution.py:42
  12.0 3.6 %collective-permute-start.1 = (f32[3,16,256]{2,1,0:T(8,128)S(1)}, f32[3,16,256]{2,1,0:T(8,128)S(1)}, u32[]{:S(2)}, u32[]{:S(2)}) collective-permute-start(f32[3,16,256]{2,1,0:T(8,128)S(1)} %get-tuple-element.33), channel_id=1, source_target_pairs={{0,3},{1,2},{2,1},{3,0},{4,7},{5,6},{6,5},{7,4},{8,11},{9,10},{10,... | collective-permute-start | bytes 147464 | tf_op jit(solution)/shard_map/ppermute | solution.py:42
  16.0 6.0 %collective-permute-start.2 = (bf16[160,256]{1,0:T(8,128)(2,1)S(1)}, bf16[160,256]{1,0:T(8,128)(2,1)S(1)}, u32[]{:S(2)}, u32[]{:S(2)}) collective-permute-start(bf16[160,256]{1,0:T(8,128)(2,1)S(1)} %get-tuple-element.38), channel_id=1, source_target_pairs={{0,4},{1,5},{2,6},{3,7},{4,0},{5,1},{6,2},{7,3},{8,12},{9,13},{10,... | collective-permute-start | bytes 245768 | tf_op jit(solution)/shard_map/ppermute | solution.py:53
  18.1 3.9 %collective-permute-start.3 = (bf16[160,256]{1,0:T(8,128)(2,1)S(1)}, bf16[160,256]{1,0:T(8,128)(2,1)S(1)}, u32[]{:S(2)}, u32[]{:S(2)}) collective-permute-start(bf16[160,256]{1,0:T(8,128)(2,1)S(1)} %get-tuple-element.39), channel_id=1, source_target_pairs={{0,1},{1,0},{2,3},{3,2},{4,8},{5,9},{6,10},{7,11},{8,4},{9,5},{10,... | collective-permute-start | bytes 245768 | tf_op jit(solution)/shard_map/ppermute | solution.py:53
  41.6 2.8 %collective-permute-start.4 = (f32[20,2,256]{2,1,0:T(2,128)S(1)}, f32[20,2,256]{2,1,0:T(2,128)S(1)}, u32[]{:S(2)}, u32[]{:S(2)}) collective-permute-start(f32[20,2,256]{2,1,0:T(2,128)S(1)} %get-tuple-element.48), channel_id=1, source_target_pairs={{0,1},{1,0},{2,3},{3,2},{4,5},{5,4},{6,7},{7,6},{8,9},{9,8},{10,11... | collective-permute-start | bytes 122888 | tf_op jit(solution)/shard_map/ppermute | solution.py:42
  41.7 3.5 %collective-permute-start.5 = (f32[20,2,256]{2,1,0:T(2,128)S(1)}, f32[20,2,256]{2,1,0:T(2,128)S(1)}, u32[]{:S(2)}, u32[]{:S(2)}) collective-permute-start(f32[20,2,256]{2,1,0:T(2,128)S(1)} %get-tuple-element.49), channel_id=1, source_target_pairs={{0,3},{1,2},{2,1},{3,0},{4,7},{5,6},{6,5},{7,4},{8,11},{9,10},{10,... | collective-permute-start | bytes 122888 | tf_op jit(solution)/shard_map/ppermute | solution.py:42

commit v8 on v7

--- a/solution.py
+++ b/solution.py
@@ -280,9 +280,8 @@
             conduct_ref[z] = conduct
             uptake_ref[z] = uptake
 
-    def in_plane(self, z):
-        rows, width = self.conduct_ref.shape[1:]
-        plane = self.conduct_ref[z]
+    def in_plane(self, plane):
+        rows, width = plane.shape
         return (
             jnp.where(self.lane == 0, 0.0, pltpu.roll(plane, 1, 1)),
             jnp.where(self.lane == width - 1, 0.0, pltpu.roll(plane, width - 1, 1)),
@@ -297,13 +296,12 @@
 
 
 def residual_kernel(*refs, count):
-    operands, outputs, scratch = refs[:12], refs[12:20], refs[20:]
-    conduct_ref, uptake_ref, sol_ref = scratch[:3]
-    local, sems = scratch[3:15], scratch[15]
+    operands, outputs, scratch = refs[:12], refs[12:21], refs[21:]
+    sol_ref, uptake_ref, local, sems = scratch[0], scratch[1], scratch[2:14], scratch[14]
     diff_ref, upt_ref, diag_ref, ids_ref = local[:4]
     off_ref, cols_ref, table_ref, sol_in, label_in, src_in = local[4:10]
     top_ref, bottom_ref = from_tile(*local[10:])
-    res_ref, face_ref, plain_ref, packed_ref, tables_ref, column_ref, record_ref, scalar_ref = outputs
+    res_ref, face_ref, plain_ref, conduct_ref, code_ref, tables_ref, column_ref, record_ref, scalar_ref = outputs
     for copy in fetch(list(zip(operands, local)), sems):
         copy.wait()
     own, depth, width = sol_in.shape
@@ -343,13 +341,16 @@
     for start in range(0, depth, 8):
         block = jnp.transpose(label_in[:, start : start + 8, :].astype(jnp.float32), (1, 0, 2))
         labels = labels + [block[at] for at in range(8)]
-    for k in range(depth // 2):
-        packed_ref[k] = pack_labels(labels[2 * k], labels[2 * k + 1], 8)
     top_pairs = [top_ref[1, z : z + 1] for z in range(depth)]
     bottom_pairs = [bottom_ref[1, z : z + 1] for z in range(depth)]
     phases = range(diff_ref.shape[0])
     diffs, uptakes = [diff_ref[phase] for phase in phases], [upt_ref[phase] for phase in phases]
     grid = Grid(diffs, uptakes, labels, top_pairs, bottom_pairs, {}, conduct_ref, uptake_ref)
+    gap = jnp.zeros((4, width), jnp.float32)
+    for z in range(depth):
+        (top, far), (bottom, farther) = part_pair(top_pairs[z]), part_pair(bottom_pairs[z])
+        rim = jnp.concatenate([top, far, gap, farther, bottom], axis=0)
+        code_ref[z] = jnp.concatenate([labels[z], rim, rim], axis=0).astype(jnp.bfloat16)
     blank = jnp.zeros((8, width), jnp.float32)
     for start in range(0, depth, 8):
         block = jnp.transpose(sol_in[:, start : start + 8, :], (1, 0, 2))
@@ -366,7 +367,7 @@
         for at in range(8):
             z = start + at
             conduct, value = conduct_ref[z], sol_ref[z]
-            near = sum(grid.in_plane(z))
+            near = sum(grid.in_plane(conduct_ref[z]))
             diagonal = uptake_ref[z] + 2.0 * conduct + 0.5 * near
             flow = conduct * beside(value, grid.lane) + beside(conduct * value, grid.lane)
             applied = (diagonal * value - 0.5 * flow)[:own]
@@ -377,10 +378,7 @@
             left = block[at] - applied
             res_ref[z] = left.astype(jnp.bfloat16)
             if z in (0, depth - 1):
-                side = 0 if z == 0 else 3
-                face_ref[side] = left
-                face_ref[side + 1] = conduct
-                face_ref[side + 2] = value
+                face_ref[0 if z == 0 else 1] = left
 
 
 def phase_rows(scalar_ref, kind, width):
@@ -392,25 +390,36 @@
 
 
 def weigh_kernel(
-    scalar_ref, packed_ref, src_in, even_ref, odd_ref, row_even_ref, row_odd_ref, cor_ref, weight_ref, inner_ref,
+    scalar_ref, own_conduct_ref, code_ref, src_in, even_ref, odd_ref, row_even_ref, row_odd_ref, cor_ref,
+    weight_ref, inner_ref, done_ref,
     conduct_ref, uptake_ref,
 ):
     own, depth, width = src_in.shape
-    planes, rows = conduct_ref.shape[0:2]
+    planes, rows = weight_ref.shape[1:3]
     top_ref, bottom_ref = from_tile(row_even_ref, row_odd_ref)
-    labels = []
-    for k in range(depth // 2):
-        labels = labels + list(unpack_labels(packed_ref[k], own))
     high, low = from_slab(even_ref, odd_ref, LABELS, CORNERS)
     (high_near, high_far), (low_near, low_far) = unpack_labels(high, own), unpack_labels(low, own)
-    labels = labels + [high_near, high_far, low_far, low_near]
+    labels = [high_near, high_far, low_far, low_near]
     high, low = from_slab(even_ref, odd_ref, CORNERS, MESSAGE)
-    top_pairs = [top_ref[1, z : z + 1] for z in range(depth)] + [high[0:1], high[1:2], low[1:2], low[0:1]]
-    bottom_pairs = [bottom_ref[1, z : z + 1] for z in range(depth)] + [high[2:3], high[3:4], low[3:4], low[2:3]]
+    top_pairs = [high[0:1], high[1:2], low[1:2], low[0:1]]
+    bottom_pairs = [high[2:3], high[3:4], low[3:4], low[2:3]]
     above, below = ends()
-    outside = {depth: above, depth + 1: above, depth + 2: below, depth + 3: below}
+    outside = {0: above, 1: above, 2: below, 3: below}
     diffs, uptakes = phase_rows(scalar_ref, 0, width), phase_rows(scalar_ref, 1, width)
     grid = Grid(diffs, uptakes, labels, top_pairs, bottom_pairs, outside, conduct_ref, uptake_ref)
+
+    def conduct_of(z):
+        return own_conduct_ref[z] if z < depth else conduct_ref[z - depth]
+
+    def uptake_of(z):
+        if z >= depth:
+            return uptake_ref[z - depth]
+        code = code_ref[z].astype(jnp.float32)[:rows]
+        found = jnp.zeros((rows, width), jnp.float32)
+        for phase, value in enumerate(uptakes):
+            found = jnp.where(code == float(phase), value, found)
+        return found
+
     blank = jnp.zeros((8, width), jnp.float32)
     outer = dict(zip((depth, planes - 1), from_slab(even_ref, odd_ref, SOURCE, LABELS)))
     for start in (0, 8, planes - 1, depth):
@@ -420,9 +429,9 @@
         else:
             sources = {start: outer[start]}
         for z, source in sources.items():
-            conduct = conduct_ref[z]
-            near = grid.in_plane(z) + (conduct_ref[(z - 1) % planes], conduct_ref[(z + 1) % planes])
-            diagonal = uptake_ref[z] + 3.0 * conduct + 0.5 * sum(near[1:], near[0])
+            conduct = conduct_of(z)
+            near = grid.in_plane(conduct) + (conduct_of((z - 1) % planes), conduct_of((z + 1) % planes))
+            diagonal = uptake_of(z) + 3.0 * conduct + 0.5 * sum(near[1:], near[0])
             inside = conduct > 0.0
             scale = jnp.where(inside, OMEGA / jnp.where(inside, diagonal, 1.0), 0.0)
             for k, other in enumerate(near):
@@ -432,19 +441,26 @@
             if z < depth:
                 weight_ref[6, z, own : own + 1] = scale[own : own + 1] * top_ref[2, z : z + 1]
                 weight_ref[6, z, rows - 1 :] = scale[rows - 1 :] * bottom_ref[2, z : z + 1]
-            value, inner = cor_ref[z], slice(8, own - 8)
-            beside_all = (
-                pltpu.roll(value, 1, 1)[inner],
-                pltpu.roll(value, width - 1, 1)[inner],
-                pltpu.roll(value, 1, 0)[inner],
-                pltpu.roll(value, own - 1, 0)[inner],
-                cor_ref[(z - 1) % planes, inner],
-                cor_ref[(z + 1) % planes, inner],
-            )
-            total = (1.0 - OMEGA) * value[inner] + weight_ref[6, z, inner]
-            for k, other in enumerate(beside_all):
-                total = total + weight_ref[k, z, inner] * other
-            inner_ref[z] = total
+            inner_ref[z] = inner_sweep(cor_ref, weight_ref, z, slice(0, own))
+    for z in range(depth):
+        done_ref[z] = inner_sweep(inner_ref, weight_ref, z, slice(8, own - 8))
+
+
+def inner_sweep(ref, weight_ref, z, part):
+    planes, own, width = ref.shape
+    value = ref[z]
+    near = (
+        pltpu.roll(value, 1, 1)[part],
+        pltpu.roll(value, width - 1, 1)[part],
+        pltpu.roll(value, 1, 0)[part],
+        pltpu.roll(value, own - 1, 0)[part],
+        ref[(z - 1) % planes, part],
+        ref[(z + 1) % planes, part],
+    )
+    total = (1.0 - OMEGA) * value[part] + weight_ref[6, z, part]
+    for k, other in enumerate(near):
+        total = total + weight_ref[k, z, part] * other
+    return total
 
 
 def rows_of(basis, start, size):
@@ -460,7 +476,7 @@
     ]
 
 
-def restrict_kernel(scalar_ref, column_ref, record_ref, even_ref, odd_ref, face_ref, res_ref, *refs, capacity):
+def restrict_kernel(scalar_ref, column_ref, record_ref, even_ref, odd_ref, face_ref, conduct_ref, plain_ref, res_ref, *refs, capacity):
     basis, out_ref = refs
     depth, own, width = res_ref.shape
     entries = column_ref.shape[0]
@@ -470,14 +486,14 @@
     packed = from_slab(even_ref, odd_ref, LABELS, CORNERS)
     diffs = phase_rows(scalar_ref, 0, width)
     faces = {}
-    for z, side, at in ((0, 0, 1), (depth - 1, 3, 0)):
+    for z, side, at in ((0, 0, 1), (depth - 1, 1, 0)):
         label = unpack_labels(packed[at], own)[0]
         beyond = jnp.zeros(label.shape, jnp.float32)
         for phase, diff in enumerate(diffs):
             beyond = jnp.where(label == float(phase), diff, beyond)
         beyond = jnp.where(ends()[at], 0.0, beyond)
         value = jnp.where(ends()[at], 0.0, values[at])
-        applied = 0.5 * (face_ref[side + 1] + beyond) * (face_ref[side + 2] - value)
+        applied = 0.5 * (conduct_ref[z, :own] + beyond) * (plain_ref[z] - value)
         faces[z] = (face_ref[side] - applied).astype(jnp.bfloat16)
     total = jnp.zeros((entries, width), jnp.float32)
     for z in range(depth):
@@ -607,7 +623,7 @@
             row_odd_ref[z] = jnp.where(odd, last, first)
 
 
-def smooth_kernel(cor_ref, row_even_ref, row_odd_ref, weight_ref, inner_ref, out_hbm, new_ref, mid_ref, out_ref, sems):
+def smooth_kernel(cor_ref, row_even_ref, row_odd_ref, weight_ref, inner_ref, done_ref, out_hbm, new_ref, mid_ref, out_ref, sems):
     planes, rows, width = mid_ref.shape
     own, depth, unused = out_ref.shape
     top_ref, bottom_ref = from_tile(row_even_ref, row_odd_ref)
@@ -617,7 +633,7 @@
         return jnp.concatenate([cor_ref[z], top_ref[z], gap, bottom_ref[z]], axis=0)
 
     def middle(z):
-        return jnp.concatenate([mid_ref[z, :8], inner_ref[z], mid_ref[z, own - 8 :]], axis=0)
+        return jnp.concatenate([mid_ref[z, :8], inner_ref[z, 8 : own - 8], mid_ref[z, own - 8 :]], axis=0)
 
     def sweep(plane, z, part):
         value = plane(z)
@@ -640,7 +656,9 @@
     copies = []
     for start in range(0, depth, 8):
         for z in range(start, start + 8):
-            new_ref[z] = sweep(middle, z, slice(0, own))
+            for part in (slice(0, 8), slice(own - 8, own)):
+                new_ref[z, part] = sweep(middle, z, part)
+            new_ref[z, 8 : own - 8] = done_ref[z]
         out_ref[:, start : start + 8, :] = jnp.transpose(new_ref[start : start + 8], (1, 0, 2))
         part = pl.ds(start, 8)
         copies.append(pltpu.make_async_copy(out_ref.at[:, part], out_hbm.at[:, part], sems.at[start // 8]))
@@ -750,21 +768,22 @@
         solution, phase_label, source, row_even, row_odd,
     ]
     phases = phase_diffusivity.shape[0]
-    residual, face, plain, packed, tables, column, record, scalars = pl.pallas_call(
+    residual, face, plain, conduct, uptake, tables, column, record, scalars = pl.pallas_call(
         functools.partial(residual_kernel, count=count),
         out_shape=(
             shape((depth, rows, width), bf16),
-            shape((6, rows, width), f32),
+            shape((2, rows, width), f32),
             shape((depth, rows, width), f32),
-            shape((depth // 2, 8, width), f32),
+            shape((depth, tall, width), f32),
+            shape((depth, tall + 8, width), bf16),
             shape((8, entries), i32),
             shape((entries, 8), i32),
             shape((cells, 128), f32),
             shape((3, phases, 8, 128), f32),
         ),
         in_specs=[HBM] * 12,
-        out_specs=(VMEM,) * 8,
-        scratch_shapes=[pltpu.VMEM((depth, tall, width), f32)] * 3
+        out_specs=(VMEM,) * 9,
+        scratch_shapes=[pltpu.VMEM((depth, tall, width), f32)] * 2
         + [pltpu.SMEM(array.shape, array.dtype) for array in operands[:4]]
         + [pltpu.VMEM(array.shape, array.dtype) for array in operands[4:]]
         + [pltpu.SemaphoreType.DMA((12,))],
@@ -777,11 +796,11 @@
     payload = pl.pallas_call(
         functools.partial(restrict_kernel, capacity=capacity),
         out_shape=shape((devices, lines, 128), f32),
-        in_specs=[VMEM] * 8,
+        in_specs=[VMEM] * 10,
         out_specs=VMEM,
         compiler_params=params(8),
         name="restrict",
-    )(scalars, column, record, even, odd, face, residual, basis)
+    )(scalars, column, record, even, odd, face, conduct, plain, residual, basis)
     got = lax.all_to_all(payload, ("slab", "tile"), split_axis=0, concat_axis=0, tiled=True)
     got = [got[:, 4 * t : 4 * t + 4].reshape(4 * devices, 128) for t in range(groups)]
 
@@ -794,28 +813,28 @@
         compiler_params=params(12 + count // 128),
         name="prolong",
     )(scalars, tables, even, odd, plain, *got, basis)
-    corrected, packed = lax.optimization_barrier((corrected, packed))
-    weights, inner = pl.pallas_call(
+    corrected, conduct = lax.optimization_barrier((corrected, conduct))
+    weights, inner, done = pl.pallas_call(
         weigh_kernel,
-        out_shape=(shape((7, planes, tall, width), f32), shape((planes, rows - 16, width), f32)),
-        in_specs=[VMEM] * 8,
-        out_specs=(VMEM, VMEM),
-        scratch_shapes=[wide_block] * 2,
+        out_shape=(shape((7, planes, tall, width), f32), shape((planes, rows, width), f32), shape((depth, rows - 16, width), f32)),
+        in_specs=[VMEM] * 9,
+        out_specs=(VMEM, VMEM, VMEM),
+        scratch_shapes=[pltpu.VMEM((4, tall, width), f32)] * 2,
         compiler_params=params(12),
         name="weigh",
-    )(scalars, packed, source, even, odd, first_even, first_odd, corrected)
+    )(scalars, conduct, uptake, source, even, odd, first_even, first_odd, corrected)
     row_even = along_tile(row_even, False)
     row_odd = along_tile(row_odd, True)
     smooth = pl.pallas_call(
         smooth_kernel,
         out_shape=shape((rows, depth, width), f32),
-        in_specs=[VMEM] * 5,
+        in_specs=[VMEM] * 6,
         out_specs=HBM,
         scratch_shapes=[pltpu.VMEM((depth, rows, width), f32), wide_block, pltpu.VMEM(block, f32)]
         + [pltpu.SemaphoreType.DMA((depth // 8,))],
         compiler_params=params(16),
         name="smooth",
-    )(corrected, row_even, row_odd, weights, inner)
+    )(corrected, row_even, row_odd, weights, inner, done)
     return smooth, coarse_correction.reshape(cells)
 
 

time: 47.1 us -> 47 us (level)
  transfers between devices with their start and end apart: 7 -> 7, of which waited for: 4 -> 4; matrix products, arithmetic and copies ran while one was open for 0% -> 0% of each run, Pallas kernels for 16% -> 17%
where the time goes in v8:
time: 47 us; the launch traced here: 46.8 us
  Pallas kernels  13.7 us (29%)
  starting transfers between devices  11.9 us (25%)
  blocking collectives  10.9 us (23%)
  waiting for transfers between devices  9.65 us (21%)
  between operations  0.71 us (2%)
    all_to_all x1, blocking collectives, shards(): lax.all_to_all(payload, ('slab', 'tile'), split_axis=0, concat_axis=0, ti...  10.9 us
    all_to_all x1, starting transfers between devices, shards(): lax.all_to_all(outgoing.reshape(slabs, capacity, wide), 'slab', split_axi...  7.26 us
    all_to_all x1, waiting for transfers between devices, shards(): lax.all_to_all(outgoing.reshape(slabs, capacity, wide), 'slab', split_axi...  6.76 us
    pallas_call x1, Pallas kernels, shards(): pl.pallas_call(functools.partial(residual_kernel, count=count), out_shape...  3.27 us
    ppermute x4, waiting for transfers between devices, along_tile(): return lax.ppermute(message, 'tile', closed(pairs(tiles, odd), tiles))  2.52 us
    pallas_call x1, Pallas kernels, shards(): pl.pallas_call(weigh_kernel, out_shape=(shape((7, planes, tall, width), f...  2.43 us
    ppermute x2, starting transfers between devices, along_slab(): return lax.ppermute(message, ('slab', 'tile'), table)  2.36 us
    pallas_call x1, Pallas kernels, shards(): pl.pallas_call(functools.partial(sort_kernel, capacity=capacity, count=co...  2.31 us
  transfers between devices with their start and end apart: 7, of which 4 were waited for; matrix products, arithmetic and copies ran while one was open for 0% of the time, Pallas kernels for 17%

profile of v8, /device:TPU:0, one launch (start us, length us, event | category | flops | bytes accessed | tf_op | source)
XLA Modules:
  0.0 46.8 jit_solution(15203936410931728908)
XLA Ops:
  0.6 0.0 copy-start
  0.6 2.3 %sort_basis.1 = bf16[64,5248]{1,0:T(8,128)(2,1)} custom-call(s32[1,64]{1,0:T(1,128)} %bitcast.15, s32[8]{0:T(128)} %bitcast.16, s32[8]{0:T(128)} %refs_3_.1, bf16[64,4096]{1,0:T(8,128)(2,1)} %bitcast.12), custom_call_target="tpu_custom_call" | custom-call | tf_op jit(solution)/shard_map/sort_basis/pallas_call | solution.py:704
  3.0 7.3 %all-to-all-start = ((bf16[8,8,5248]{2,1,0:T(8,128)(2,1)}), bf16[8,8,5248]{2,1,0:T(8,128)(2,1)S(1)}, u32[]{:S(2)}, u32[]{:S(2)}) async-start(bf16[8,8,5248]{2,1,0:T(8,128)(2,1)} %bitcast.11), calls=%async_computation | async-start | bytes 1343488 | tf_op jit(solution)/shard_map/all_to_all | solution.py:727
  10.2 1.7 %border.1 = (bf16[160,256]{1,0:T(8,128)(2,1)S(1)}, bf16[160,256]{1,0:T(8,128)(2,1)S(1)}, f32[3,16,256]{2,1,0:T(8,128)S(1)}, f32[3,16,256]{2,1,0:T(8,128)S(1)}) custom-call(f32[32,16,256]{2,1,0:T(8,128)} %refs_7_, s32[32,16,256]{2,1,0:T(8,128)} %refs_8_, f32[32,16,256]{2,1,0:T(8,128)} %src_in, s32[8,8]{1,0:T(8,128)} %bitcast.13), custom_call_target="tpu_custom_call" | custom-call | tf_op jit(solution)/shard_map/border/pallas_call | solution.py:735
  12.0 0.1 collective-permute-start
  12.0 1.6 %collective-permute-start.1 = (f32[3,16,256]{2,1,0:T(8,128)S(1)}, f32[3,16,256]{2,1,0:T(8,128)S(1)}, u32[]{:S(2)}, u32[]{:S(2)}) collective-permute-start(f32[3,16,256]{2,1,0:T(8,128)S(1)} %get-tuple-element.35), channel_id=1, source_target_pairs={{0,3},{1,2},{2,1},{3,0},{4,7},{5,6},{6,5},{7,4},{8,11},{9,10},{10,... | collective-permute-start | bytes 147464 | tf_op jit(solution)/shard_map/ppermute | solution.py:42
  13.7 0.0 collective-permute-done.refs_10_.row_even.row_even_ref
  13.7 1.9 %collective-permute-done.1.refs_11_.row_odd.row_odd_ref = f32[3,16,256]{2,1,0:T(8,128)S(1)} collective-permute-done((f32[3,16,256]{2,1,0:T(8,128)S(1)}, f32[3,16,256]{2,1,0:T(8,128)S(1)}, u32[]{:S(2)}, u32[]{:S(2)}) %collective-permute-start.1) | collective-permute-done | bytes 49184 | tf_op jit(solution)/shard_map/ppermute | solution.py:42
  15.6 0.4 corner.1
  16.0 2.1 %collective-permute-start.2 = (bf16[160,256]{1,0:T(8,128)(2,1)S(1)}, bf16[160,256]{1,0:T(8,128)(2,1)S(1)}, u32[]{:S(2)}, u32[]{:S(2)}) collective-permute-start(bf16[160,256]{1,0:T(8,128)(2,1)S(1)} %get-tuple-element.40), channel_id=1, source_target_pairs={{0,4},{1,5},{2,6},{3,7},{4,0},{5,1},{6,2},{7,3},{8,12},{9,13},{10,... | collective-permute-start | bytes 245768 | tf_op jit(solution)/shard_map/ppermute | solution.py:53
  18.1 0.3 collective-permute-start.3
  18.4 3.3 %residual.1 = (bf16[16,32,256]{2,1,0:T(8,128)(2,1)S(1)}, f32[2,32,256]{2,1,0:T(8,128)S(1)}, f32[16,32,256]{2,1,0:T(8,128)S(1)}, f32[16,40,256]{2,1,0:T(8,128)S(1...) custom-call(f32[3]{0:T(128)} %refs_0_.1, ...), custom_call_target="tpu_custom_call" | custom-call | tf_op jit(solution)/shard_map/residual/pallas_call | solution.py:771
  21.6 0.4 collective-permute-done.2.even_ref
  22.0 0.0 collective-permute-done.3.odd_ref
  22.0 6.8 %all-to-all-done = bf16[8,8,5248]{2,1,0:T(8,128)(2,1)S(1)} async-done(((bf16[8,8,5248]{2,1,0:T(8,128)(2,1)}), bf16[8,8,5248]{2,1,0:T(8,128)(2,1)S(1)}, u32[]{:S(2)}, u32[]{:S(2)}) %all-to-all-start) | async-done | bytes 671776 | tf_op jit(solution)/shard_map/all_to_all | solution.py:727
  28.8 0.5 restrict.1
  29.2 10.9 %all_to_all.10 = f32[32,4,128]{2,1,0:T(4,128)S(1)} all-to-all(f32[32,4,128]{2,1,0:T(4,128)S(1)} %restrict.1), channel_id=1, replica_groups=mesh['slab'=8,'tile'=4] {'slab','tile'}, dimensions={0} | all-to-all | bytes 131072 | tf_op jit(solution)/shard_map/all_to_all | solution.py:804
  40.1 1.5 %prolong.1 = (f32[20,32,256]{2,1,0:T(8,128)S(1)}, f32[20,2,256]{2,1,0:T(2,128)S(1)}, f32[20,2,256]{2,1,0:T(2,128)S(1)}, f32[1,8]{1,0:T(1,128)}) custom-call(f32[3,3,8,128]{3,2,1,0:T(8,128)S(1)} %get-tuple-element.36.scalar_ref, s32[8,64]{1,0:T(8,128)S(1)} %get-tuple-element.37.tables_ref, bf16[160,256]{1,0:T(8,128)(2,1)S(1)} %collective-permute-done.2.even_ref, ...), custom_call_target="tpu_custom_call" | custom-call | tf_op jit(solution)/shard_map/prolong/pallas_call | solution.py:808
  41.6 0.1 collective-permute-start.4
  41.7 0.4 collective-permute-start.5
  42.2 0.0 copy-done
  42.2 2.4 %weigh.1 = (f32[7,20,40,256]{3,2,1,0:T(8,128)S(1)}, f32[20,32,256]{2,1,0:T(8,128)S(1)}, f32[16,16,256]{2,1,0:T(8,128)S(1)}) custom-call(f32[3,3,8,128]{3,2,1,0:T(8,128)S(1)} %get-tuple-element.36.scalar_ref, f32[16,40,256]{2,1,0:T(8,128)S(1)} %get-tuple-element.52.conduct_ref.own_conduct_ref, bf16[16,48,256]{2,1,0:T(8,128)(2,1)S(1)} %get-tuple-element.53.code_ref, ...), custom_call_target="tpu_custom_call" | custom-call | tf_op jit(solution)/shard_map/weigh/pallas_call | solution.py:817
  44.6 0.0 collective-permute-done.4.row_even_ref
  44.6 0.6 %collective-permute-done.5.row_odd_ref = f32[20,2,256]{2,1,0:T(2,128)S(1)} collective-permute-done((f32[20,2,256]{2,1,0:T(2,128)S(1)}, f32[20,2,256]{2,1,0:T(2,128)S(1)}, u32[]{:S(2)}, u32[]{:S(2)}) %collective-permute-start.5) | collective-permute-done | bytes 40992 | tf_op jit(solution)/shard_map/ppermute | solution.py:42
  45.2 1.5 %smooth.1 = f32[32,16,256]{2,1,0:T(8,128)} custom-call(f32[20,32,256]{2,1,0:T(8,128)S(1)} %get-tuple-element.49.cor_ref, f32[20,2,256]{2,1,0:T(2,128)S(1)} %collective-permute-done.4.row_even_ref, f32[20,2,256]{2,1,0:T(2,128)S(1)} %collective-permute-done.5.row_odd_ref, f32[7,20,40,256]{3,2,1,0:T(8,128)S(1)} %get-tuple-element.54.weight_ref, ...), custom_call_target="tpu_custom_call" | custom-call | tf_op jit(solution)/shard_map/smooth/pallas_call | solution.py:828
Async XLA Ops:
  0.6 41.5 %copy-start = (f32[32,16,256]{2,1,0:T(8,128)S(1)}, f32[32,16,256]{2,1,0:T(8,128)}, u32[]{:S(2)}) copy-start(f32[32,16,256]{2,1,0:T(8,128)} %src_in) | copy-start | bytes 1572868
  3.0 25.8 %all-to-all-start = ((bf16[8,8,5248]{2,1,0:T(8,128)(2,1)}), bf16[8,8,5248]{2,1,0:T(8,128)(2,1)S(1)}, u32[]{:S(2)}, u32[]{:S(2)}) async-start(bf16[8,8,5248]{2,1,0:T(8,128)(2,1)} %bitcast.11), calls=%async_computation | async-start | bytes 1343488 | tf_op jit(solution)/shard_map/all_to_all | solution.py:727
  12.0 1.7 %collective-permute-start = (f32[3,16,256]{2,1,0:T(8,128)S(1)}, f32[3,16,256]{2,1,0:T(8,128)S(1)}, u32[]{:S(2)}, u32[]{:S(2)}) collective-permute-start(f32[3,16,256]{2,1,0:T(8,128)S(1)} %get-tuple-element.34), channel_id=1, source_target_pairs={{0,1},{1,0},{2,3},{3,2},{4,5},{5,4},{6,7},{7,6},{8,9},{9,8},{10,11... | collective-permute-start | bytes 147464 | tf_op jit(solution)/shard_map/ppermute | solution.py:42
  12.0 3.6 %collective-permute-start.1 = (f32[3,16,256]{2,1,0:T(8,128)S(1)}, f32[3,16,256]{2,1,0:T(8,128)S(1)}, u32[]{:S(2)}, u32[]{:S(2)}) collective-permute-start(f32[3,16,256]{2,1,0:T(8,128)S(1)} %get-tuple-element.35), channel_id=1, source_target_pairs={{0,3},{1,2},{2,1},{3,0},{4,7},{5,6},{6,5},{7,4},{8,11},{9,10},{10,... | collective-permute-start | bytes 147464 | tf_op jit(solution)/shard_map/ppermute | solution.py:42
  16.0 6.0 %collective-permute-start.2 = (bf16[160,256]{1,0:T(8,128)(2,1)S(1)}, bf16[160,256]{1,0:T(8,128)(2,1)S(1)}, u32[]{:S(2)}, u32[]{:S(2)}) collective-permute-start(bf16[160,256]{1,0:T(8,128)(2,1)S(1)} %get-tuple-element.40), channel_id=1, source_target_pairs={{0,4},{1,5},{2,6},{3,7},{4,0},{5,1},{6,2},{7,3},{8,12},{9,13},{10,... | collective-permute-start | bytes 245768 | tf_op jit(solution)/shard_map/ppermute | solution.py:53
  18.1 3.9 %collective-permute-start.3 = (bf16[160,256]{1,0:T(8,128)(2,1)S(1)}, bf16[160,256]{1,0:T(8,128)(2,1)S(1)}, u32[]{:S(2)}, u32[]{:S(2)}) collective-permute-start(bf16[160,256]{1,0:T(8,128)(2,1)S(1)} %get-tuple-element.41), channel_id=1, source_target_pairs={{0,1},{1,0},{2,3},{3,2},{4,8},{5,9},{6,10},{7,11},{8,4},{9,5},{10,... | collective-permute-start | bytes 245768 | tf_op jit(solution)/shard_map/ppermute | solution.py:53
  41.6 3.0 %collective-permute-start.4 = (f32[20,2,256]{2,1,0:T(2,128)S(1)}, f32[20,2,256]{2,1,0:T(2,128)S(1)}, u32[]{:S(2)}, u32[]{:S(2)}) collective-permute-start(f32[20,2,256]{2,1,0:T(2,128)S(1)} %get-tuple-element.50), channel_id=1, source_target_pairs={{0,1},{1,0},{2,3},{3,2},{4,5},{5,4},{6,7},{7,6},{8,9},{9,8},{10,11... | collective-permute-start | bytes 122888 | tf_op jit(solution)/shard_map/ppermute | solution.py:42
  41.7 3.5 %collective-permute-start.5 = (f32[20,2,256]{2,1,0:T(2,128)S(1)}, f32[20,2,256]{2,1,0:T(2,128)S(1)}, u32[]{:S(2)}, u32[]{:S(2)}) collective-permute-start(f32[20,2,256]{2,1,0:T(2,128)S(1)} %get-tuple-element.51), channel_id=1, source_target_pairs={{0,3},{1,2},{2,1},{3,0},{4,7},{5,6},{6,5},{7,4},{8,11},{9,10},{10,... | collective-permute-start | bytes 122888 | tf_op jit(solution)/shard_map/ppermute | solution.py:42
